TPU v7x, 32 devices: a whole 2x2x4 slice. The times are simulated.
32 devices in a mesh: dp: 8 (over y, x, core), head: 4 (over z).
Axes of the slice: x: 2, y: 2, z: 4, core: 2. Of those that a mesh axis runs over, the one named last changes fastest.
Arguments:
- text_in: bfloat16 [4096, 768], P('dp'), may hold values from -6 to 6
- visual_in: bfloat16 [4096, 768], P('dp'), may hold values from -80 to 80
- visual_count: int32 [8], P('dp'), may hold values from 256 to 512, as said below
- line_index: int32 [2, 4096], P(None, 'dp'), may hold values from 0 to 47
- box_index: int32 [2, 2, 4096], P(None, None, 'dp'), may hold values from 0 to 31
- qkv_weight: bfloat16 [768, 3, 1536], P(None, None, 'head'), may hold values from -0.21875 to 0.21875
- bias_table: float32 [24, 64], P('head'), may hold values from -5 to 5
- out_weight: bfloat16 [1536, 768], replicated, may hold values from -0.75 to 0.75
- out_bias: float32 [768], replicated, may hold values from -3 to 3
- norm1_gain: float32 [768], replicated, may hold values from 0.25 to 1.75
- norm1_shift: float32 [768], replicated, may hold values from -3 to 3
- ffn_weight_in: bfloat16 [768, 3072], replicated, may hold values from -0.21875 to 0.21875
- ffn_bias_in: float32 [3072], replicated, may hold values from -3 to 3
- ffn_weight_out: bfloat16 [3072, 768], replicated, may hold values from -0.109375 to 0.109375
- ffn_bias_out: float32 [768], replicated, may hold values from -3 to 3
- norm2_gain: float32 [768], replicated, may hold values from 0.25 to 1.75
- norm2_shift: float32 [768], replicated, may hold values from -3 to 3
- batch_gain: float32 [768], replicated, may hold values from 0.25 to 1.75
- batch_shift: float32 [768], replicated, may hold values from -3 to 3
- cotangent: bfloat16 [4096, 768], P('dp'), may hold values from -6 to 6
Outputs:
- layer_out: bfloat16 [4096, 768], P('dp')
- grad_text: float32 [4096, 768], P(('dp', 'head'))
- grad_visual: float32 [4096, 768], P(('dp', 'head'))
- grad_qkv: float32 [768, 3, 1536], P('dp', None, 'head')
- grad_bias_table: float32 [24, 64], P('head', 'dp')
- grad_out_weight: float32 [1536, 768], P('head', 'dp')
- grad_out_bias: float32 [768], P(('dp', 'head'))
- grad_norm1_gain: float32 [768], P(('dp', 'head'))
- grad_norm1_shift: float32 [768], P(('dp', 'head'))
- grad_ffn_in: float32 [768, 3072], P(('dp', 'head'))
- grad_ffn_bias_in: float32 [3072], P(('dp', 'head'))
- grad_ffn_out: float32 [3072, 768], P(('dp', 'head'))
- grad_ffn_bias_out: float32 [768], P(('dp', 'head'))
- grad_norm2_gain: float32 [768], P(('dp', 'head'))
- grad_norm2_shift: float32 [768], P(('dp', 'head'))
- batch_gain_gradient: float32 [768], replicated
- batch_shift_gradient: float32 [768], replicated
Inputs may be any that keep to these rules, and one draw needn't show every extreme that they name: `visual_count`: each page holds half of 512 or 512 visual tokens; both occur in every draw.
All inputs are finite; a program needn't handle non-finite values.
Results may differ from a plain program's by a relative error of at most 0.018.
The roundings to bfloat16 on the way count: a program that leaves them out, or rounds other values in their place, can miss the bound.
Values may be sent and summed in bfloat16 or wider, within the bound.
No kernel may reach another device: no remote copies, remote signals or barrier semaphores. Data moves between devices by JAX's collectives and lax.ppermute only.
A program may use at most 128 MiB of HBM per device.

v0:
```python
import functools

import jax
import jax.numpy as jnp
from jax import lax
from jax.experimental import pallas as pl
from jax.experimental.pallas import tpu as pltpu
from jax.sharding import PartitionSpec as P

HD = 64
NB_REL = 32
NB_BOX = 16
LINES = 48
BOXES = 32

EPSILON = 1e-05
FLOOR_SCORE = -1000000000.0
SCALE = HD ** (-0.5)
LEVELS = 128
MASK_LANE = LINES + 2 * BOXES
VMEM_LIMIT = 12 * 1024 * 1024
VEC_ROWS = 16
CHUNKS = 2

F32 = jnp.float32
BF16 = jnp.bfloat16

NN = (((1,), (0,)), ((), ()))
NT = (((1,), (1,)), ((), ()))
TN = (((0,), (0,)), ((), ()))
TT = (((0,), (1,)), ((), ()))


def dot(left, right, dims=NN):
    return lax.dot_general(left, right, dims, preferred_element_type=F32)


def iota(shape, axis):
    return lax.broadcasted_iota(jnp.int32, shape, axis)


def one_hot(condition):
    return condition.astype(F32).astype(BF16)


def thirds(value):
    high = value.astype(BF16)
    rest = value - high.astype(F32)
    middle = rest.astype(BF16)
    return high, middle, (rest - middle.astype(F32)).astype(BF16)


def picked(value, selector, dims=NN):
    return functools.reduce(jnp.add, (dot(part, selector, dims) for part in thirds(value)))


def call(kernel, name, micros, outs, args, count=None, scratch=(), final=()):
    vmem = pl.BlockSpec(memory_space=pltpu.VMEM)
    scalars = [] if count is None else [count]
    return pl.pallas_call(
        kernel,
        out_shape=tuple(
            jax.ShapeDtypeStruct(*entry) if place in final else pltpu.VMEM(*entry)
            for place, entry in enumerate(outs)
        ),
        in_specs=[pl.BlockSpec(memory_space=pltpu.SMEM)] * len(scalars) + [vmem] * len(args),
        out_specs=tuple(vmem for entry in outs),
        scratch_shapes=list(scratch),
        compiler_params=pltpu.CompilerParams(vmem_limit_bytes=VMEM_LIMIT),
        cost_estimate=pl.CostEstimate(
            flops=int(micros * 1e9), bytes_accessed=int(micros * 3e6), transcendentals=0
        ),
        name=name,
    )(*scalars, *[pltpu.with_memory_space_constraint(a, pltpu.VMEM) for a in args])


def head_groups(heads_local, body, loop=True):
    if heads_local % 2 or not loop:
        for first in range(0, heads_local, 2):
            body(first, min(2, heads_local - first))
        return

    def step(pair, carry):
        body(pair * 2, 2)
        return carry

    lax.fori_loop(0, heads_local // 2, step, 0)


def lanes(first, heads, offset=0):
    start = offset + first * HD
    if isinstance(first, int):
        return slice(start, start + heads * HD)
    return pl.ds(pl.multiple_of(start, 128), heads * HD)


def stream_is_visual():
    return lax.axis_index("head") >= lax.axis_size("head") // 2


def stats_kernel(count_ref, visual_ref, out_ref):
    tokens, width = visual_ref.shape
    number = count_ref[0].astype(F32)
    keep = (iota((tokens, 1), 0) < count_ref[0]).astype(F32)
    visual = visual_ref[...].astype(F32)
    total = jnp.sum(visual * keep, axis=0, keepdims=True)
    centred = (visual - total / number) * keep
    spread = jnp.sum(centred * centred, axis=0, keepdims=True)
    out_ref[...] = jnp.concatenate(
        [total, spread, jnp.full((1, width), number, F32), jnp.zeros((5, width), F32)], axis=0
    )


def joined_stats(blocks):
    total = functools.reduce(jnp.add, (b[0:1] for b in blocks))
    number = functools.reduce(jnp.add, (b[2:3] for b in blocks))
    mean = total / number
    spread = functools.reduce(
        jnp.add, (b[1:2] + b[2:3] * (b[0:1] / b[2:3] - mean) ** 2 for b in blocks)
    )
    return total, spread, number


def join_stats_kernel(*refs):
    total, spread, number = joined_stats([ref[...] for ref in refs[:-1]])
    refs[-1][...] = jnp.concatenate(
        [total, spread, number, jnp.zeros((5, total.shape[1]), F32)], axis=0
    )


GROUPS = (
    (0, LINES, NB_REL // 2, 0),
    (LINES, LINES + BOXES, NB_BOX // 2, NB_REL),
    (LINES + BOXES, LINES + 2 * BOXES, NB_BOX // 2, NB_REL + NB_BOX),
)


def bucket_map(level, half, offset, table_width):
    bucket = jnp.clip(level, -half, half - 1) + half + offset
    return one_hot(bucket == iota((table_width, LEVELS), 0))


def same_group(row, lane):
    inside = jnp.zeros(row.shape, jnp.bool_)
    for start, stop, unused_half, unused_offset in GROUPS:
        inside = inside | ((row >= start) & (row < stop) & (lane >= start) & (lane < stop))
    return inside


def by_level(level, line, across, down):
    wanted = jnp.where(level < LINES, line, jnp.where(level < LINES + BOXES, across, down))
    return wanted == level


def prep_kernel(count_ref, line_ref, box_ref, table_ref, bias_ref, *refs):
    oh_ref, back_ref, tab_ref, small_ref, b1_ref = refs[8:]
    width = small_ref.shape[1]
    small_ref[...] = jnp.concatenate([ref[...] for ref in refs[:8]], axis=0)
    for c in range(bias_ref.shape[1] // width):
        b1_ref[c : c + 1, :] = bias_ref[:, c * width : (c + 1) * width]
    visual = stream_is_visual()
    tokens = line_ref.shape[1]
    heads_local, table_width = table_ref.shape
    line = jnp.where(visual, line_ref[1:2, :], line_ref[0:1, :])
    across = jnp.where(visual, box_ref[1, 0:1, :], box_ref[0, 0:1, :]) + LINES
    down = jnp.where(visual, box_ref[1, 1:2, :], box_ref[0, 1:2, :]) + (LINES + BOXES)
    level = iota((LEVELS, tokens), 0)
    back_ref[...] = one_hot(by_level(LEVELS - 1 - level, line, across, down))
    closed = jnp.logical_and(visual, iota((LEVELS, tokens), 1) >= count_ref[0])
    mask = jnp.where(closed, FLOOR_SCORE, 0.0)
    flags = by_level(level, line, across, down).astype(F32)
    oh_ref[...] = jnp.transpose(jnp.where(level == MASK_LANE, mask, flags)).astype(BF16)
    row = iota((LEVELS, LEVELS), 0)
    lane = iota((LEVELS, LEVELS), 1)
    inside = same_group(row, lane)
    offsets = iota((table_width, LEVELS), 1) - LEVELS // 2
    table = table_ref[...]
    spread = [
        picked(table, bucket_map(offsets, half, offset, table_width))
        for unused_start, unused_stop, half, offset in GROUPS
    ]
    for head in range(heads_local):
        rows = [jnp.broadcast_to(s[head : head + 1, :], (LEVELS, LEVELS)) for s in spread]
        chosen = jnp.where(row < LINES, rows[0], jnp.where(row < LINES + BOXES, rows[1], rows[2]))
        turned = pltpu.roll(chosen, LEVELS // 2, 1, stride=1, stride_axis=0)
        pairs = jnp.where(inside, turned, 0.0)
        high = jnp.where((lane == MASK_LANE) & (row < LINES), 1.0, pairs)
        tab_ref[:, head * LEVELS : (head + 1) * LEVELS] = high.astype(BF16)


def attend_chunk(
    chunk, count_ref, q_ref, k_ref, vt_ref, tab_ref, oh_ref, heads_ref, prob_ref, left_ref
):
    visual = stream_is_visual()
    tokens, local_width = q_ref.shape
    heads_local = local_width // HD
    block = heads_ref.shape[1]
    span = slice(chunk * block, (chunk + 1) * block)
    place = iota((1, block), 1) + chunk * block
    allowed = jnp.logical_or(jnp.logical_not(visual), place < count_ref[0]).astype(F32)
    one = oh_ref[...]
    left_ref[...] = dot(oh_ref[span, :], tab_ref[...]).astype(BF16)
    ones = jnp.ones((16, tokens), F32).astype(BF16)

    def group(first, heads):
        span_lanes = lanes(first, heads)
        queries = q_ref[span, span_lanes] * jnp.asarray(SCALE, BF16)
        keys = k_ref[:, span_lanes]
        values = vt_ref[span_lanes, :]
        biases = left_ref[:, lanes(2 * first, 2 * heads)]

        def scores(n):
            own = slice(n * HD, (n + 1) * HD)
            right = jnp.concatenate(
                [biases[:, n * LEVELS : (n + 1) * LEVELS], queries[:, own]], axis=1
            )
            return dot(jnp.concatenate([one, keys[:, own]], axis=1), right, NT)

        results = []
        following = scores(0)
        for n in range(heads):
            own = slice(n * HD, (n + 1) * HD)
            current = following
            if n + 1 < heads:
                following = scores(n + 1)
            shifted = jnp.exp(current - jnp.max(current, axis=0, keepdims=True))
            mixed = dot(jnp.concatenate([values[own], ones], axis=0), shifted.astype(BF16))
            share = 1.0 / mixed[HD : HD + 1]
            prob_ref[first + n] = (shifted * share).astype(BF16)
            results.append((mixed[:HD] * (share * allowed)).astype(BF16))
        heads_ref[span_lanes, :] = jnp.concatenate(results, axis=0)

    head_groups(heads_local, group, loop=chunk > 0)


def attend_first_kernel(pieces, count_ref, text_ref, visual_ref, small_ref, w_ref, tab_ref, oh_ref, *refs):
    piece_refs, refs = refs[:pieces], refs[pieces:]
    stats_ref, x_ref, q_ref, k_ref, v_ref, kt_ref, vt_ref, heads_ref, prob_ref, left_ref = refs
    visual = stream_is_visual()
    tokens, width = text_ref.shape
    total, spread, number = joined_stats([ref[...] for ref in piece_refs])
    mean = total / number
    scale = lax.rsqrt(spread / number + EPSILON)
    gain, shift = small_ref[6:7, :], small_ref[7:8, :]
    stats_ref[...] = jnp.concatenate(
        [mean, scale, gain, number, jnp.zeros((4, width), F32)], axis=0
    )

    @pl.when(visual)
    def _():
        keep = (iota((tokens, 1), 0) < count_ref[0]).astype(F32)
        centred = (visual_ref[...].astype(F32) - mean) * keep
        x_ref[...] = ((centred * scale * gain + shift) * keep).astype(BF16)

    @pl.when(jnp.logical_not(visual))
    def _():
        x_ref[...] = text_ref[...]

    x = x_ref[...]
    q_ref[...] = dot(x, w_ref[0]).astype(BF16)
    k_ref[...] = dot(x, w_ref[1]).astype(BF16)
    v_ref[...] = dot(x, w_ref[2]).astype(BF16)
    kt_ref[...] = dot(w_ref[1], x, TT).astype(BF16)
    vt_ref[...] = dot(w_ref[2], x, TT).astype(BF16)
    attend_chunk(
        0, count_ref, q_ref, k_ref, vt_ref, tab_ref, oh_ref, heads_ref, prob_ref, left_ref
    )


ERF_P = 0.3275911 * 0.7071067811865476
ERF_A = (0.254829592, -0.284496736, 1.421413741, -1.453152027, 1.061405429)


def gelu_parts(pre):
    t = 1.0 / (1.0 + ERF_P * jnp.abs(pre))
    bell = jnp.exp(-0.5 * pre * pre)
    poly = 0.5 * ERF_A[4]
    for coefficient in ERF_A[3::-1]:
        poly = poly * t + 0.5 * coefficient
    tail = poly * t * bell
    cdf = jnp.where(pre >= 0.0, 1.0 - tail, tail)
    return pre * cdf, cdf + pre * (bell * 0.3989422804014327)


def normed_rows(hidden):
    average = jnp.mean(hidden, axis=-1, keepdims=True)
    centred = hidden - average
    scale = lax.rsqrt(jnp.mean(centred * centred, axis=-1, keepdims=True) + EPSILON)
    return centred * scale, scale


def normed_back(upstream, hat, scale, gain):
    scaled = upstream * gain
    return scale * (
        scaled
        - jnp.mean(scaled, axis=-1, keepdims=True)
        - hat * jnp.mean(scaled * hat, axis=-1, keepdims=True)
    )


def ffn_kernel(chunk, relative, pieces, *refs):
    (text_ref, cot_ref, wo, w1, w2, small_ref, b1_ref), refs = refs[:7], refs[7:]
    piece_refs, refs = refs[:pieces], refs[pieces:]
    out_ref, share_ref, act_ref, dpre_ref, low_ref, branch_ref, mix_ref = refs[:7]
    dheads_ref, dheadst_ref, vec_ref, slope = refs[7:]
    local_width, block = piece_refs[0].shape
    width = text_ref.shape[1]
    hidden_width = w1.shape[1]
    head_rank = lax.axis_index("head")
    out_bias, gain1, shift1, b2, gain2, shift2 = (small_ref[i : i + 1, :] for i in range(6))
    parts = hidden_width // width
    share = share_ref.shape[0]
    rows = slice(chunk * block, (chunk + 1) * block)
    own_rows = pl.ds(pl.multiple_of(head_rank * local_width, 64), local_width)

    sources = [
        (ref[...], head_rank ^ index if relative else index)
        for index, ref in enumerate(piece_refs)
    ]
    mixed = text_ref[rows, :].astype(F32) + out_bias
    for piece, source in sources:
        wo_rows = pl.ds(pl.multiple_of(source * local_width, 64), local_width)
        mixed = mixed + dot(piece, wo[wo_rows, :], TN)
    hat1, scale1 = normed_rows(mixed)
    after = hat1 * gain1 + shift1
    after_low = after.astype(BF16)
    low_ref[...] = after_low
    branch = jnp.zeros((block, width), F32)
    for c in range(parts):
        cols = slice(c * width, (c + 1) * width)
        act, slope[:, cols] = gelu_parts(dot(after_low, w1[:, cols]) + b1_ref[c : c + 1, :])
        act = act.astype(BF16)
        act_ref[:, cols] = act
        branch = branch + dot(act, w2[cols, :])
    hat2, scale2 = normed_rows(after + (branch + b2))
    out_ref[...] = (hat2 * gain2 + shift2).astype(BF16)
    upstream = cot_ref[rows, :].astype(F32)
    dh_two = normed_back(upstream, hat2, scale2, gain2)
    dbranch = dh_two.astype(BF16)
    branch_ref[...] = dbranch
    vec = [None] * 3
    dy = dh_two
    for c in range(parts):
        cols = slice(c * width, (c + 1) * width)
        dpre = (dot(dbranch, w2[cols, :], NT) * slope[:, cols]).astype(BF16)
        dpre_ref[:, cols] = dpre
        vec.append(dpre.astype(F32))
        dy = dy + dot(dpre, w1[:, cols], NT)
    dh_one = normed_back(dy, hat1, scale1, gain1)
    vec[:3] = [dh_one, dy * hat1, dy]
    vec += [dbranch.astype(F32), upstream * hat2, upstream]
    sums = [jnp.sum(v, axis=0, keepdims=True) for v in vec]
    vec_ref[...] = jnp.concatenate(
        sums + [jnp.zeros((VEC_ROWS - len(sums), width), F32)], axis=0
    )
    share_ref[...] = jnp.zeros_like(share_ref)
    per_block = block // share
    for part in range(per_block):

        @pl.when(head_rank == chunk * per_block + part)
        def _():
            share_ref[...] = dh_one[part * share : (part + 1) * share]

    dmix = dh_one.astype(BF16)
    mix_ref[...] = dmix
    dheads_ref[...] = dot(dmix, wo[own_rows, :], NT).astype(BF16)
    dheadst_ref[...] = dot(wo[own_rows, :], dmix, NT).astype(BF16)


def owner_of(half, step):
    place = lax.axis_index("dp")
    core = place & 1
    return (((place >> 1) ^ step) << 1) | (core if half == 0 else 1 - core)


def own_order():
    return [owner_of(half, step) for half in range(2) for step in range(4)]


def weight_grad_in_kernel(*refs):
    head_rank = lax.axis_index("head")
    low_refs, dpre_refs, vec_refs = (refs[i * CHUNKS : (i + 1) * CHUNKS] for i in range(3))
    mine_ref, sib_ref = refs[3 * CHUNKS :]
    width = low_refs[0].shape[1]
    parts = dpre_refs[0].shape[1] // width
    width_own = width // 8
    part_in = width_own // 4
    lane = iota((part_in, width), 1)
    row = iota((part_in, width), 0)
    pick = jnp.concatenate(
        [
            (lane == owner * width_own + head_rank * part_in + row).astype(F32)
            for owner in own_order()
        ],
        axis=0,
    ).astype(BF16)
    low_t = [dot(pick, low[...], NT).astype(BF16) for low in low_refs]
    grads = []
    for p in range(parts):
        cols = slice(p * width, (p + 1) * width)
        grads.append(
            functools.reduce(
                jnp.add, (dot(low_t[c], dpre_refs[c][:, cols]) for c in range(CHUNKS))
            )
        )
    vec = functools.reduce(jnp.add, (v[...] for v in vec_refs))
    for n in range(8):
        rows = slice(n * part_in, (n + 1) * part_in)
        block = jnp.concatenate([grad[rows] for grad in grads] + [vec], axis=0)
        target = mine_ref if n < 4 else sib_ref
        target[n % 4] = block.astype(target.dtype)


def weight_grad_out_kernel(*refs):
    head_rank = lax.axis_index("head")
    names = ("out", "act", "branch", "mix", "heads")
    groups = {name: refs[i * CHUNKS : (i + 1) * CHUNKS] for i, name in enumerate(names)}
    layer_ref, mine_ref, sib_ref, whole = refs[len(names) * CHUNKS :]
    block, width = groups["out"][0].shape
    hidden_width = groups["act"][0].shape[1]
    owners = own_order()
    width_own = width // 8
    window = hidden_width // 8
    part_out = window // 4
    half_own = width_own // 2
    for c in range(CHUNKS):
        layer_ref[c * block : (c + 1) * block, :] = groups["out"][c][...]
    whole[...] = functools.reduce(
        jnp.add, (dot(groups["mix"][c][...], groups["heads"][c][...], TT) for c in range(CHUNKS))
    )
    pick = one_hot(
        iota((part_out, window), 1) == head_rank * part_out + iota((part_out, window), 0)
    )
    grad = jnp.zeros((8 * part_out, width), F32)
    for c in range(CHUNKS):
        stacked = []
        for owner in owners:
            cols = pl.ds(pl.multiple_of(owner * window, 128), window)
            stacked.append(dot(pick, groups["act"][c][:, cols], NT).astype(BF16))
        grad = grad + dot(jnp.concatenate(stacked, axis=0), groups["branch"][c][...])
    for n, owner in enumerate(owners):
        start = pl.multiple_of(owner * width_own, 8)
        packed = jnp.concatenate(
            [whole[pl.ds(start, half_own), :], whole[pl.ds(start + half_own, half_own), :]],
            axis=1,
        )
        target = mine_ref if n < 4 else sib_ref
        target[n % 4] = jnp.concatenate(
            [grad[n * part_out : (n + 1) * part_out], packed], axis=0
        ).astype(target.dtype)


X_FIRST = ((0, 2), (1, 3))
Y_FIRST = ((0, 1), (2, 3))


def join_cores_kernel(plans, *refs):
    mine_ref, other_ref, outs = refs[0], refs[1], refs[2:]
    start = 0
    for (keep, send), keep_ref, send_ref in zip(plans, outs[::2], outs[1::2]):
        rows = slice(start, start + keep_ref.shape[1])
        start = rows.stop
        for places, out in ((keep, keep_ref), (send, send_ref)):
            for n, place in enumerate(places):
                total = mine_ref[place, rows, :] + other_ref[place, rows, :].astype(F32)
                out[n] = total.astype(out.dtype)


def join_chips_kernel(*refs):
    count = len(refs) // 4
    ins, outs = refs[: 2 * count], refs[2 * count :]
    for n in range(count):
        keep, other = ins[2 * n : 2 * n + 2]
        for m, out in enumerate(outs[2 * n : 2 * n + 2]):
            out[...] = (keep[m] + other[m].astype(F32)).astype(out.dtype)


def attend_back_heads(count_ref, refs, dqkv_ref, pair_ref):
    q_ref, k_ref, v_ref, kt_ref, oh_ref, back_ref = refs[:6]
    groups = [refs[6 + i * CHUNKS : 6 + (i + 1) * CHUNKS] for i in range(4)]
    head_refs, dhead_refs, dheadt_refs, prob_refs = groups
    visual = stream_is_visual()
    tokens = q_ref.shape[0]
    block = tokens // CHUNKS
    count = count_ref[0]
    one = oh_ref[...]
    back = back_ref[...]
    inside = same_group(LEVELS - 1 - iota((LEVELS, LEVELS), 0), iota((LEVELS, LEVELS), 1))
    extra = one_hot(iota((tokens, 16), 1) < 2)
    sublane = iota((16, block), 0)
    free = jnp.logical_not(visual)
    rows_open = []
    lanes_open = []
    for c in range(CHUNKS):
        rows_open.append(
            jnp.logical_or(free, iota((block, 1), 0) + c * block < count).astype(BF16)
        )
        lanes_open.append(
            jnp.logical_or(free, iota((1, block), 1) + c * block < count).astype(BF16)
        )

    def group(first, heads):
        span_lanes = lanes(first, heads)
        turned = [[], [], []]
        for n in range(heads):
            own = slice(n * HD, (n + 1) * HD)
            left = jnp.concatenate([v_ref[:, span_lanes][:, own], extra], axis=1)
            below = jnp.concatenate([back, kt_ref[span_lanes, :][own]], axis=0)
            dquery_t = []
            dkey = jnp.zeros((tokens, HD), F32)
            dvalue = jnp.zeros((tokens, HD), F32)
            pairs = jnp.zeros((LEVELS, LEVELS), F32)
            for c in range(CHUNKS):
                span = slice(c * block, (c + 1) * block)
                dout = dhead_refs[c][:, span_lanes][:, own] * rows_open[c]
                dout_t = dheadt_refs[c][span_lanes, :][own] * lanes_open[c]
                inner = -jnp.sum(
                    dout_t.astype(F32) * head_refs[c][span_lanes, :][own].astype(F32),
                    axis=0,
                    keepdims=True,
                )
                high = inner.astype(BF16).astype(F32)
                tail = jnp.where(sublane == 0, high, jnp.where(sublane == 1, inner - high, 0.0))
                centred = dot(left, jnp.concatenate([dout_t, tail.astype(BF16)], axis=0))
                prob = prob_refs[c][first + n]
                dscore = (prob.astype(F32) * centred).astype(BF16)
                both = dot(below, dscore)
                level = both[:LEVELS]
                level_high = level.astype(BF16)
                level_low = (level - level_high.astype(F32)).astype(BF16)
                one_part = one[span, :]
                pairs = pairs + dot(level_high, one_part) + dot(level_low, one_part)
                dquery_t.append(both[LEVELS:] * SCALE)
                dkey = dkey + dot(dscore, q_ref[span, span_lanes][:, own])
                dvalue = dvalue + dot(prob, dout)
            pair_ref[first + n] = jnp.where(inside, pairs, 0.0)
            turned[0].append(jnp.concatenate(dquery_t, axis=1))
            turned[1].append(dkey * SCALE)
            turned[2].append(dvalue)
        for m in range(3):
            joined = jnp.concatenate(turned[m], axis=0 if m == 0 else 1)
            if m == 0:
                joined = jnp.transpose(joined)
            dqkv_ref[m, :, span_lanes] = joined.astype(BF16)

    head_groups(q_ref.shape[1] // HD, group)


def back_kernel(
    relative, count_ref, w_ref, visual_ref, stats_ref, *refs
):
    steps = lax.axis_size("head")
    inner, refs = refs[: 6 + 4 * CHUNKS], refs[6 + 4 * CHUNKS :]
    dqkv_ref, pair_ref, sums_ref = refs[:3]
    attend_back_heads(count_ref, inner, dqkv_ref, pair_ref)
    visual = stream_is_visual()
    tokens = visual_ref.shape[0]
    share = tokens // steps
    mean, scale = stats_ref[0:1, :], stats_ref[1:2, :]
    shift_sum = jnp.zeros(mean.shape, F32)
    gain_sum = jnp.zeros(mean.shape, F32)
    for k in range(steps):
        if relative:
            start = pl.multiple_of((lax.axis_index("head") ^ k) * share, share)
            target = refs[3 + k % 2].at[k // 2]
        else:
            start = k * share
            target = refs[3].at[k]
        rows = pl.ds(start, share)
        part = functools.reduce(
            jnp.add, (dot(dqkv_ref[m, rows, :], w_ref[m], NT) for m in range(3))
        )
        target[...] = part.astype(target.dtype)
        keep = jnp.logical_and(visual, iota((share, 1), 0) + start < count_ref[0]).astype(F32)
        kept = part * keep
        shift_sum = shift_sum + jnp.sum(kept, axis=0, keepdims=True)
        hat = (visual_ref[rows, :].astype(F32) - mean) * scale
        gain_sum = gain_sum + jnp.sum(kept * hat, axis=0, keepdims=True)
    sums_ref[...] = jnp.concatenate(
        [shift_sum, gain_sum, jnp.zeros((6, mean.shape[1]), F32)], axis=0
    )


def join_pair_kernel(keep_ref, other_ref, own_ref, send_ref):
    own_ref[...] = keep_ref[0] + other_ref[0].astype(F32)
    send_ref[...] = (keep_ref[1] + other_ref[1].astype(F32)).astype(BF16)


def table_sums(pair_refs):
    table_width = NB_REL + 2 * NB_BOX
    sums = [[], [], []]
    for ref in pair_refs:
        for head in range(ref.shape[0]):
            turned = pltpu.roll(ref[head], LEVELS // 2 + 1, 1, stride=1, stride_axis=0)
            for n, (start, stop, unused_half, unused_offset) in enumerate(GROUPS):
                rows = turned[LEVELS - stop : LEVELS - start]
                sums[n].append(jnp.sum(rows, axis=0, keepdims=True))
    table = jnp.zeros((8, table_width), F32)
    offsets = LEVELS // 2 - iota((table_width, LEVELS), 1)
    for n, (unused_start, unused_stop, half, offset) in enumerate(GROUPS):
        missing = 8 - len(sums[n])
        stacked = jnp.concatenate(sums[n] + [jnp.zeros((missing, LEVELS), F32)], axis=0)
        table = table + picked(stacked, bucket_map(offsets, half, offset, table_width), NT)
    return table


def qkv_grad_kernel(fused, x_ref, dqkv_ref, pair_ref, *outs):
    tokens, width = x_ref.shape
    local_width = dqkv_ref.shape[2]
    table = table_sums((pair_ref,))
    x = x_ref[...]

    if not fused:
        grad_ref, table_ref = outs
        table_ref[...] = table
        for m in range(3):
            grad_ref[m] = dot(x, dqkv_ref[m], TN).astype(BF16)
        return
    mine_ref, sib_ref, whole = outs
    width_own = width // 8
    padded = jnp.concatenate(
        [
            jnp.concatenate([table, jnp.zeros((8, local_width - table.shape[1]), F32)], axis=1),
            jnp.zeros((8, local_width), F32),
        ],
        axis=0,
    )
    for m in range(3):
        whole[m] = dot(x, dqkv_ref[m], TN)
    for half, target in ((1, sib_ref), (0, mine_ref)):
        for k in range(4):
            rows = pl.ds(pl.multiple_of(owner_of(half, k) * width_own, 8), width_own)
            tall = jnp.concatenate([whole[m, rows, :] for m in range(3)] + [padded], axis=0)
            middle = tall.shape[0] // 2
            target[k] = jnp.concatenate([tall[:middle], tall[middle:]], axis=1).astype(
                target.dtype
            )


def finish_grads_kernel(hidden_width, *refs):
    block_refs, outs = refs[:8], refs[8:]
    grad_in, grad_out, grad_ow, bias_in, grad_qkv, grad_table = outs[:6]
    sums = [
        own[...] + other[...].astype(F32) for own, other in zip(block_refs[::2], block_refs[1::2])
    ]
    total = jnp.concatenate(sums, axis=0)
    width = total.shape[1]
    part_in = grad_in.shape[0]
    part_out = grad_out.shape[0]
    half_own = grad_ow.shape[1] // 2
    local_width = grad_ow.shape[0]
    parts = hidden_width // width
    place = lax.axis_index("dp") * lax.axis_size("head") + lax.axis_index("head")
    grad_in[...] = jnp.concatenate(
        [total[p * part_in : (p + 1) * part_in] for p in range(parts)], axis=1
    )
    base = parts * part_in
    vec = total[base : base + VEC_ROWS]
    base += VEC_ROWS
    grad_out[...] = total[base : base + part_out]
    base += part_out
    packed = total[base : base + half_own]
    grad_ow[...] = jnp.transpose(
        jnp.concatenate([packed[:, :local_width], packed[:, local_width:]], axis=0)
    )
    base += half_own
    lane = iota((width, 128), 0)
    column = iota((width, 128), 1)
    own = picked(vec, one_hot((lane == place * part_in + column) & (column < part_in)))
    for row, out in zip((0, 1, 2, 7, 8, 9), outs[6:]):
        out[...] = own[row : row + 1, :part_in]
    first = place * part_out
    wide = picked(
        vec, one_hot((lane == lax.rem(first, width) + column) & (column < part_out))
    )
    row = iota((VEC_ROWS, 128), 0)
    chosen = jnp.where(row == 3 + lax.div(first, width), wide, 0.0)
    bias_in[...] = jnp.sum(chosen, axis=0, keepdims=True)[:, :part_out]
    grads = jnp.concatenate([total[base:, :local_width], total[base:, local_width:]], axis=0)
    width_own = grad_qkv.shape[1]
    for m in range(3):
        grad_qkv[m] = grads[m * width_own : (m + 1) * width_own]
    table = grads[3 * width_own : 3 * width_own + 8]
    buckets = grad_table.shape[1]
    lane = iota((local_width, 128), 0)
    column = iota((local_width, 128), 1)
    start = lax.axis_index("dp") * buckets
    cut = picked(table, one_hot((lane == start + column) & (column < buckets)))
    grad_table[...] = cut[: grad_table.shape[0], :buckets]


def finish_inputs_kernel(steps, relative, sums, count_ref, visual_ref, stats_ref, *refs):
    share_refs, refs = refs[:CHUNKS], refs[CHUNKS:]
    part_refs, refs = refs[: 1 + relative], refs[1 + relative :]
    sum_refs, refs = refs[:sums], refs[sums:]
    text_ref, grad_ref, gain_ref, shift_ref = refs
    head_rank = lax.axis_index("head")
    share = text_ref.shape[0]
    half = steps // 2
    if relative:
        same, other = (ref[...].astype(F32) for ref in part_refs)
        text = jnp.where(stream_is_visual(), other, same)
        visual = jnp.where(stream_is_visual(), same, other)
    else:
        text, visual = (
            functools.reduce(
                jnp.add, (part_refs[0][k].astype(F32) for k in range(start, start + half))
            )
            for start in (0, half)
        )
    text_ref[...] = functools.reduce(jnp.add, (ref[...] for ref in share_refs)) + text
    total = functools.reduce(jnp.add, (ref[...] for ref in sum_refs))
    mean, scale, gain, number = (stats_ref[i : i + 1, :] for i in range(4))
    start = pl.multiple_of(head_rank * share, share)
    keep = (iota((share, 1), 0) + start < count_ref[0]).astype(F32)
    hat = (visual_ref[pl.ds(start, share), :].astype(F32) - mean) * keep * scale
    dnormed = visual * keep
    shift_gradient, gain_gradient = total[0:1], total[1:2]
    shift_ref[...] = shift_gradient
    gain_ref[...] = gain_gradient
    grad_ref[...] = (
        keep
        * scale
        * gain
        * (dnormed - shift_gradient / number - hat * gain_gradient / number)
    )


def swap(value, axis, mask):
    size = lax.axis_size(axis)
    return lax.ppermute(value, axis, [(i, i ^ mask) for i in range(size)])


def after(value, *earlier):
    return lax.optimization_barrier((value, *earlier))[0]


def gather_heads(chunks):
    return [[piece] + [swap(piece, "head", k) for k in (1, 2, 3)] for piece in chunks]


def across_chips(mine, other, plans, sizes, name):
    axes = {X_FIRST: (2, 4), Y_FIRST: (4, 2)}
    width = mine.shape[2]
    outs = []
    for size in sizes:
        outs += [((2, size, width), F32), ((2, size, width), BF16)]
    joined = call(functools.partial(join_cores_kernel, plans), name, 1, outs, [mine, other])
    return [
        (keep, swap(send, "dp", axes[plan][0]), axes[plan][1])
        for plan, keep, send in zip(plans, joined[::2], joined[1::2])
    ]


def second_exchange(stages, name, earlier=()):
    outs = []
    args = []
    for keep, other, mask in stages:
        outs += [(keep.shape[1:], F32), (keep.shape[1:], BF16)]
        args += [keep, other]
    args[1] = after(args[1], *earlier)
    joined = call(join_chips_kernel, name, 1, outs, args)
    blocks = []
    for n, stage in enumerate(stages):
        blocks += [joined[2 * n], swap(joined[2 * n + 1], "dp", stage[2])]
    return blocks, joined


def per_device(
    text_in,
    visual_in,
    visual_count,
    line_index,
    box_index,
    qkv_weight,
    bias_table,
    out_weight,
    out_bias,
    norm1_gain,
    norm1_shift,
    ffn_weight_in,
    ffn_bias_in,
    ffn_weight_out,
    ffn_bias_out,
    norm2_gain,
    norm2_shift,
    batch_gain,
    batch_shift,
    cotangent,
):
    tokens, width = text_in.shape
    local_width = qkv_weight.shape[2]
    heads_local = local_width // HD
    head_count = lax.axis_size("head")
    dp_count = lax.axis_size("dp")
    head_rank = lax.axis_index("head")
    dp_rank = lax.axis_index("dp")
    fused = head_count == 4 and dp_count == 8
    share = tokens // head_count
    block = tokens // CHUNKS
    hidden_width = ffn_weight_in.shape[1]
    table_width = bias_table.shape[1]
    part_in = width // (dp_count * head_count)
    part_out = hidden_width // (dp_count * head_count)
    weight = jnp.transpose(qkv_weight, (1, 0, 2))
    row_vectors = [
        value.reshape(1, width)
        for value in (
            out_bias,
            norm1_gain,
            norm1_shift,
            ffn_bias_out,
            norm2_gain,
            norm2_shift,
            batch_gain,
            batch_shift,
        )
    ]

    packed_shape = ((8, width), F32)
    (packed,) = call(
        stats_kernel, "stats", 2, [packed_shape], [visual_in], visual_count
    )
    if fused:
        (packed,) = call(
            join_stats_kernel, "join_stats", 1, [packed_shape], [packed, swap(packed, "dp", 1)]
        )
        packed = [packed] + [swap(packed, "dp", k) for k in (2, 4, 6)]
    else:
        gathered = lax.all_gather(packed, "dp")
        packed = [gathered[i] for i in range(dp_count)]
    one, back, tab, small, bias_in = call(
        prep_kernel,
        "prep",
        2,
        [
            ((tokens, LEVELS), BF16),
            ((LEVELS, tokens), BF16),
            ((LEVELS, heads_local * LEVELS), BF16),
            ((8, width), F32),
            ((8, width), F32),
        ],
        [line_index, box_index, bias_table, ffn_bias_in.reshape(1, hidden_width)] + row_vectors,
        visual_count,
    )

    rows = ((tokens, local_width), BF16)
    turned = ((local_width, tokens), BF16)
    left = [pltpu.VMEM((block, heads_local * LEVELS), BF16)]
    chunk_outs = [((local_width, block), BF16), ((heads_local, tokens, block), BF16)]
    stats, x, q, k, v, kt, vt, heads_one, prob_one = call(
        functools.partial(attend_first_kernel, len(packed)),
        "attend_first",
        6,
        [packed_shape, ((tokens, width), BF16), rows, rows, rows, turned, turned] + chunk_outs,
        [text_in, visual_in, small, weight, tab, one] + packed,
        visual_count,
        scratch=left,
        final=(1,),
    )
    heads_two, prob_two = call(
        functools.partial(attend_chunk, 1),
        "attend_second",
        3,
        chunk_outs,
        [q, k, vt, tab, one],
        visual_count,
        scratch=left,
    )
    heads = (heads_one, heads_two)
    if fused:
        pieces = gather_heads(heads)
    else:
        pieces = []
        for piece in heads:
            gathered = lax.all_gather(piece, "head")
            pieces.append([gathered[i] for i in range(head_count)])

    results = []
    for c in range(CHUNKS):
        text = after(text_in, results[-1][-1]) if results else text_in
        results.append(
            call(
                functools.partial(ffn_kernel, c, fused, len(pieces[c])),
                f"ffn_{c}",
                9,
                [
                    ((block, width), BF16),
                    ((share, width), F32),
                    ((block, hidden_width), BF16),
                    ((block, hidden_width), BF16),
                    ((block, width), BF16),
                    ((block, width), BF16),
                    ((block, width), BF16),
                    ((block, local_width), BF16),
                    ((local_width, block), BF16),
                    ((VEC_ROWS, width), F32),
                ],
                [text, cotangent, out_weight, ffn_weight_in, ffn_weight_out, small, bias_in]
                + list(pieces[c]),
                scratch=[pltpu.VMEM((block, hidden_width), F32)],
            )
        )
    out, dh_share, act, dpre, low, branch, mix, dheads, dheads_t, vec = zip(*results)
    if fused:
        in_rows = hidden_width // width * part_in + VEC_ROWS
        out_rows = part_out + width // dp_count // 2
        mine, sib = call(
            weight_grad_in_kernel,
            "weight_grad_in",
            2,
            [((4, in_rows, width), F32), ((4, in_rows, width), BF16)],
            [*low, *dpre, *vec],
        )
        other = swap(sib, "dp", 1)
        layer_out, mine_out, sib_out = call(
            weight_grad_out_kernel,
            "weight_grad_out",
            3,
            [
                ((tokens, width), BF16),
                ((4, out_rows, width), F32),
                ((4, out_rows, width), BF16),
            ],
            [after(out[0], sib), *out[1:], *act, *branch, *mix, *heads],
            scratch=[pltpu.VMEM((width, local_width), F32)],
            final=(0,),
        )
        other_out = swap(sib_out, "dp", 1)
        ffn_stages = across_chips(mine, other, [X_FIRST], [in_rows], "join_cores_in")
        ffn_stages += across_chips(mine_out, other_out, [Y_FIRST], [out_rows], "join_cores_out")
    inner = [q, k, v, kt, one, back, *heads, *dheads, *dheads_t, prob_one, prob_two]
    if fused:
        inner[0] = after(q, *(stage[0] for stage in ffn_stages))
        part_outs = [((2, share, width), F32), ((2, share, width), BF16)]
    else:
        part_outs = [((head_count, share, width), BF16)]
    dqkv, pairs, sums, *parts = call(
        functools.partial(back_kernel, fused),
        "back",
        10,
        [
            ((3, tokens, local_width), BF16),
            ((heads_local, LEVELS, LEVELS), F32),
            packed_shape,
        ]
        + part_outs,
        [weight, visual_in, stats] + inner,
        visual_count,
    )
    if fused:
        keep, send = parts
        near = swap(send, "head", 1)
        sums = sums + swap(sums, "dp", 1)
        ffn_blocks, ffn_joined = second_exchange(ffn_stages, "join_chips_ffn", [sums])
        sums = sums + swap(sums, "dp", 2)
        block_rows = 3 * (width // dp_count) + 16
        mine, sib = call(
            functools.partial(qkv_grad_kernel, True),
            "qkv_grad",
            3,
            [
                ((4, block_rows // 2, 2 * local_width), F32),
                ((4, block_rows // 2, 2 * local_width), BF16),
            ],
            [after(x, ffn_joined[0]), dqkv, pairs],
            scratch=[pltpu.VMEM((3, width, local_width), F32)],
        )
        first_rows = block_rows // 4 // 8 * 8
        stages = across_chips(
            mine,
            after(swap(sib, "dp", 1), sums),
            [X_FIRST, Y_FIRST],
            [first_rows, block_rows // 2 - first_rows],
            "join_cores_qkv",
        )
        sums = sums + swap(sums, "dp", 4)
        qkv_blocks, unused_joined = second_exchange(stages, "join_chips_qkv", ffn_blocks)
        same, send = call(
            join_pair_kernel,
            "join_pair",
            1,
            [((share, width), F32), ((share, width), BF16)],
            [keep, after(near, sums)],
        )
        received = [same, swap(send, "head", 2)]
        sums = sums + swap(sums, "head", 1)
        sums = [sums, swap(sums, "head", 2)]
        blocks = ffn_blocks + qkv_blocks
        one_row = ((1, part_in), F32)
        grad_in, grad_out, grad_ow, grad_bias_in, grad_qkv, grad_table, *own = call(
            functools.partial(finish_grads_kernel, hidden_width),
            "finish_grads",
            2,
            [
                ((part_in, hidden_width), F32),
                ((part_out, width), F32),
                ((local_width, width // dp_count), F32),
                ((1, part_out), F32),
                ((3, width // dp_count, local_width), F32),
                ((heads_local, table_width // dp_count), F32),
            ]
            + [one_row] * 6,
            blocks,
            final=range(12),
        )
        grad_bias_in = grad_bias_in.reshape(part_out)
        grad_qkv = jnp.transpose(grad_qkv, (1, 0, 2))
        own = [value.reshape(part_in) for value in own]
    else:
        layer_out = jnp.concatenate(out, axis=0)
        act, dpre, low, branch, mix = (
            jnp.concatenate(value, axis=0) for value in (act, dpre, low, branch, mix)
        )

        def scatter(value, dimension):
            return lax.psum_scatter(
                value.astype(BF16), "dp", scatter_dimension=dimension, tiled=True
            ).astype(F32)

        def own_columns(value, part):
            split = value.reshape(tokens, dp_count, head_count, part)
            return lax.dynamic_index_in_dim(split, head_rank, 2, keepdims=False).reshape(
                tokens, dp_count * part
            )

        grad_in = scatter(dot(own_columns(low, part_in), dpre, TN), 0)
        grad_out = scatter(dot(own_columns(act, part_out), branch, TN), 0)
        grad_ow = scatter(dot(jnp.concatenate(heads, axis=1), mix), 1)
        vec = lax.psum((vec[0] + vec[1]).astype(BF16), "dp").astype(F32)
        place = dp_rank * head_count + head_rank
        own = [
            lax.dynamic_slice_in_dim(vec[row], place * part_in, part_in, 0)
            for row in (0, 1, 2, 7, 8, 9)
        ]
        grad_bias_in = lax.dynamic_slice_in_dim(
            vec[3 : 3 + hidden_width // width].reshape(hidden_width), place * part_out, part_out, 0
        )
        sums = [lax.psum(sums, ("dp", "head"))]
        grad, table = call(
            functools.partial(qkv_grad_kernel, False),
            "qkv_grad",
            3,
            [((3, width, local_width), BF16), ((8, table_width), F32)],
            [x, dqkv, pairs],
        )
        received = [lax.all_to_all(parts[0], "head", 0, 0, tiled=True)]
        grad_qkv = jnp.transpose(scatter(grad, 1), (1, 0, 2))
        grad_table = scatter(table[:heads_local], 1)

    grad_text, grad_visual, gain_gradient, shift_gradient = call(
        functools.partial(finish_inputs_kernel, head_count, fused, len(sums)),
        "finish_inputs",
        2,
        [((share, width), F32)] * 2 + [((1, width), F32)] * 2,
        [visual_in, stats, *dh_share, *received, *sums],
        visual_count,
        final=range(4),
    )
    return (
        layer_out,
        grad_text,
        grad_visual,
        grad_qkv,
        grad_table,
        grad_ow,
        own[0],
        own[1],
        own[2],
        grad_in,
        grad_bias_in,
        grad_out,
        own[3],
        own[4],
        own[5],
        gain_gradient.reshape(width),
        shift_gradient.reshape(width),
    )


def solution(mesh):
    in_specs = (
        P("dp", None),
        P("dp", None),
        P("dp"),
        P(None, "dp"),
        P(None, None, "dp"),
        P(None, None, "head"),
        P("head", None),
        P(),
        P(),
        P(),
        P(),
        P(),
        P(),
        P(),
        P(),
        P(),
        P(),
        P(),
        P(),
        P("dp", None),
    )
    out_specs = (
        P("dp", None),
        P(("dp", "head"), None),
        P(("dp", "head"), None),
        P("dp", None, "head"),
        P("head", "dp"),
        P("head", "dp"),
        P(("dp", "head")),
        P(("dp", "head")),
        P(("dp", "head")),
        P(("dp", "head"), None),
        P(("dp", "head")),
        P(("dp", "head"), None),
        P(("dp", "head")),
        P(("dp", "head")),
        P(("dp", "head")),
        P(),
        P(),
    )
    return jax.shard_map(
        per_device, mesh=mesh, in_specs=in_specs, out_specs=out_specs, check_vma=False
    )
```

profile of v0, /device:TPU:0, one launch (start us, length us, event | category | flops | bytes accessed | tf_op | source)
XLA Modules:
  0.0 121.5 jit_solution(7073153573498247530)
XLA Ops:
  1.3 1.1 copy-done.4
  2.5 0.5 stats.1.refs_0_
  3.0 0.5 collective-permute-start
  3.7 0.6 collective-permute-done.refs_1_
  4.4 3.9 %collective-permute-start.3 = (f32[8,768]{1,0:T(8,128)S(1)}, f32[8,768]{1,0:T(8,128)S(1)}, u32[]{:S(2)}, u32[]{:S(2)}) collective-permute-start(f32[8,768]{1,0:T(8,128)S(1)} %join_stats.1.refs_0_), channel_id=1, source_target_pairs={{0,24},{4,28},{8,16},{12,20},{16,8},{20,12},{24,0},{28,4},{1,25},{... | collective-permute-start | bytes 73736 | tf_op jit(solution)/shard_map/ppermute | solution.py:731
  8.3 0.5 collective-permute-start.2
  9.2 0.8 collective-permute-done.3.refs_3_
  10.1 2.0 %collective-permute-done.2.refs_2_ = f32[8,768]{1,0:T(8,128)S(1)} collective-permute-done((f32[8,768]{1,0:T(8,128)S(1)}, f32[8,768]{1,0:T(8,128)S(1)}, u32[]{:S(2)}, u32[]{:S(2)}) %collective-permute-start.2) | collective-permute-done | bytes 24608 | tf_op jit(solution)/shard_map/ppermute | solution.py:731
  12.1 0.5 collective-permute-done.1.refs_1_
  12.6 4.0 %attend_first.1 = (f32[8,768]{1,0:T(8,128)S(1)}, bf16[512,768]{1,0:T(8,128)(2,1)S(1)}, bf16[512,384]{1,0:T(8,128)(2,1)S(1)}, bf16[512,384]{1,0:T(8,128)(2,1)S(1)...) custom-call(s32[1]{0:T(128)S(6)} %copy.38.count_ref, ...), custom_call_target="tpu_custom_call" | custom-call | flops 6000000000 | bytes 18000000 | tf_op jit(solution)/shard_map/attend_first/pallas_call | solution.py:60
  16.6 4.0 %collective-permute-start.6 = (bf16[384,256]{1,0:T(8,128)(2,1)S(1)}, bf16[384,256]{1,0:T(8,128)(2,1)S(1)}, u32[]{:S(2)}, u32[]{:S(2)}) collective-permute-start(bf16[384,256]{1,0:T(8,128)(2,1)S(1)} %get-tuple-element.111.refs_7_.refs_8_.refs_6_), channel_id=1, source_target_pairs={{0,3},{1,2},{2,1},{3,0},{4,7},{5,6},{6,5},{7,4},{8,11},{9,10},{10,... | collective-permute-start | bytes 589832 | tf_op jit(solution)/shard_map/ppermute | solution.py:731
  20.7 0.6 collective-permute-start.4
  21.3 2.6 %attend_second.1 = (bf16[384,256]{1,0:T(8,128)(2,1)S(1)}, bf16[6,512,256]{2,1,0:T(8,128)(2,1)S(1)}) custom-call(s32[1]{0:T(128)S(6)} %copy.38.count_ref, bf16[512,384]{1,0:T(8,128)(2,1)S(1)} %get-tuple-element.142.q_ref.refs_0_, bf16[512,384]{1,0:T(8,128)(2,1)S(1)} %get-tuple-element.117.k_ref.refs_1_, bf16[384,512]{1,0:T(8,128)(2,1)S(1)} %get-tuple-element.118.vt_ref, ...), custom_call_target="tpu_custom_call" | custom-call | flops 3000000000 | bytes 9000000 | tf_op jit(solution)/shard_map/attend_second/pallas_call | solution.py:60
  23.9 3.8 %collective-permute-start.9 = (bf16[384,256]{1,0:T(8,128)(2,1)S(1)}, bf16[384,256]{1,0:T(8,128)(2,1)S(1)}, u32[]{:S(2)}, u32[]{:S(2)}) collective-permute-start(bf16[384,256]{1,0:T(8,128)(2,1)S(1)} %get-tuple-element.119.refs_7_.refs_9_), channel_id=1, source_target_pairs={{0,3},{1,2},{2,1},{3,0},{4,7},{5,6},{6,5},{7,4},{8,11},{9,10},{10,... | collective-permute-start | bytes 589832 | tf_op jit(solution)/shard_map/ppermute | solution.py:731
  27.7 11.9 %collective-permute-start.7 = (bf16[384,256]{1,0:T(8,128)(2,1)S(1)}, bf16[384,256]{1,0:T(8,128)(2,1)S(1)}, u32[]{:S(2)}, u32[]{:S(2)}) collective-permute-start(bf16[384,256]{1,0:T(8,128)(2,1)S(1)} %get-tuple-element.119.refs_7_.refs_9_), channel_id=1, source_target_pairs={{0,1},{1,0},{2,3},{3,2},{4,5},{5,4},{6,7},{7,6},{8,9},{9,8},{10,11... | collective-permute-start | bytes 589832 | tf_op jit(solution)/shard_map/ppermute | solution.py:731
  39.6 5.8 %collective-permute-done.5.refs_9_ = bf16[384,256]{1,0:T(8,128)(2,1)S(1)} collective-permute-done((bf16[384,256]{1,0:T(8,128)(2,1)S(1)}, bf16[384,256]{1,0:T(8,128)(2,1)S(1)}, u32[]{:S(2)}, u32[]{:S(2)}) %collective-permute-start.5) | collective-permute-done | bytes 196640 | tf_op jit(solution)/shard_map/ppermute | solution.py:731
  45.5 10.3 %ffn_0.1 = (bf16[256,768]{1,0:T(8,128)(2,1)S(1)}, f32[128,768]{1,0:T(8,128)S(1)}, bf16[256,3072]{1,0:T(8,128)(2,1)S(1)}, bf16[256,3072]{1,0:T(8,128)(2,1)S(1)}, ...) custom-call(bf16[512,768]{1,0:T(8,128)(2,1)S(1)} %copy-done.2, ...), custom_call_target="tpu_custom_call" | custom-call | flops 8999999488 | bytes 27000000 | tf_op jit(solution)/shard_map/ffn_0/pallas_call | solution.py:60
  55.8 10.3 %ffn_1.1 = (bf16[256,768]{1,0:T(8,128)(2,1)S(1)}, f32[128,768]{1,0:T(8,128)S(1)}, bf16[256,3072]{1,0:T(8,128)(2,1)S(1)}, bf16[256,3072]{1,0:T(8,128)(2,1)S(1)}, ...) custom-call(bf16[512,768]{1,0:T(8,128)(2,1)S(1)} %copy-done.2, ...), custom_call_target="tpu_custom_call" | custom-call | flops 8999999488 | bytes 27000000 | tf_op jit(solution)/shard_map/ffn_1/pallas_call | solution.py:60
  66.2 1.1 weight_grad_in.1
  67.3 3.0 %weight_grad_out.1 = (bf16[512,768]{1,0:T(8,128)(2,1)}, f32[4,144,768]{2,1,0:T(8,128)S(1)}, bf16[4,144,768]{2,1,0:T(8,128)(2,1)S(1)}) custom-call(bf16[256,768]{1,0:T(8,128)(2,1)S(1)} %get-tuple-element.125.refs_0_, bf16[256,768]{1,0:T(8,128)(2,1)S(1)} %get-tuple-element.126.refs_1_, bf16[256,3072]{1,0:T(8,128)(2,1)S(1)} %get-tuple-element.127.refs_2_, ...), custom_call_target="tpu_custom_call" | custom-call | flops 3000000000 | bytes 9000000 | tf_op jit(solution)/shard_map/weight_grad_out/pallas_call | solution.py:60
  70.2 0.5 collective-permute-start.10
  70.8 2.9 %collective-permute-done.10.refs_1_ = bf16[4,112,768]{2,1,0:T(8,128)(2,1)S(1)} collective-permute-done((bf16[4,112,768]{2,1,0:T(8,128)(2,1)S(1)}, bf16[4,112,768]{2,1,0:T(8,128)(2,1)S(1)}, u32[]{:S(2)}, u32[]{:S(2)}) %collective-permute-start.10) | collective-permute-done | bytes 688160 | tf_op jit(solution)/shard_map/ppermute | solution.py:731
  73.8 0.9 collective-permute-start.19
  74.8 1.6 %collective-permute-start.20 = (bf16[2,144,768]{2,1,0:T(8,128)(2,1)S(1)}, bf16[2,144,768]{2,1,0:T(8,128)(2,1)S(1)}, u32[]{:S(2)}, u32[]{:S(2)}) collective-permute-start(bf16[2,144,768]{2,1,0:T(8,128)(2,1)S(1)} %get-tuple-element.162), channel_id=1, source_target_pairs={{0,16},{4,20},{8,24},{12,28},{16,0},{20,4},{24,8},{28,12},{1,17},{... | collective-permute-start | bytes 1327112 | tf_op jit(solution)/shard_map/ppermute | solution.py:731
  76.4 10.0 %back.1 = (bf16[3,512,384]{2,1,0:T(8,128)(2,1)S(1)}, f32[6,128,128]{2,1,0:T(8,128)S(1)}, f32[8,768]{1,0:T(8,128)S(1)}, f32[2,128,768]{2,1,0:T(8,128)S(1)}, bf16[2,128,768]{2,1,0:T(8,128)(2,1)S(1)}) custom-call(s32[1]{0:T(128)S(6)} %copy.38.count_ref, bf16[3,768,384]{2,1,0:T(8,128)(2,1)S(1)} %bitcast.15, bf16[512,768]{1,0:T(8,128)(2,1)S(1)} %copy-done.5, ...), custom_call_target="tpu_custom_call" | custom-call | flops 10000000000 | bytes 30000000 | tf_op jit(solution)/shard_map/back/pallas_call | solution.py:60
  86.5 1.2 collective-permute-done.13
  87.8 1.8 %qkv_grad.1 = (f32[4,152,768]{2,1,0:T(8,128)S(1)}, bf16[4,152,768]{2,1,0:T(8,128)(2,1)S(1)}) custom-call(bf16[512,768]{1,0:T(8,128)(2,1)S(1)} %get-tuple-element.168.x_ref, bf16[3,512,384]{2,1,0:T(8,128)(2,1)S(1)} %get-tuple-element.169.dqkv_ref, f32[6,128,128]{2,1,0:T(8,128)S(1)} %get-tuple-element.170.pair_ref), custom_call_target="tpu_custom_call" | custom-call | flops 3000000000 | bytes 9000000 | tf_op jit(solution)/shard_map/qkv_grad/pallas_call | solution.py:60
  89.8 0.7 collective-permute-start.12
  90.5 1.3 %collective-permute-start.14 = (f32[8,768]{1,0:T(8,128)S(1)}, f32[8,768]{1,0:T(8,128)S(1)}, u32[]{:S(2)}, u32[]{:S(2)}) collective-permute-start(f32[8,768]{1,0:T(8,128)S(1)} %add.12), channel_id=1, source_target_pairs={{0,8},{4,12},{8,0},{12,4},{16,24},{20,28},{24,16},{28,20},{1,9},{5... | collective-permute-start | bytes 73736 | tf_op jit(solution)/shard_map/ppermute | solution.py:731
  91.8 2.5 %collective-permute-done.14 = f32[8,768]{1,0:T(8,128)S(1)} collective-permute-done((f32[8,768]{1,0:T(8,128)S(1)}, f32[8,768]{1,0:T(8,128)S(1)}, u32[]{:S(2)}, u32[]{:S(2)}) %collective-permute-start.14) | collective-permute-done | bytes 24608 | tf_op jit(solution)/shard_map/ppermute | solution.py:731
  94.5 0.7 collective-permute-start.25
  95.2 1.3 %collective-permute-start.22 = (bf16[144,768]{1,0:T(8,128)(2,1)S(1)}, bf16[144,768]{1,0:T(8,128)(2,1)S(1)}, u32[]{:S(2)}, u32[]{:S(2)}) collective-permute-start(bf16[144,768]{1,0:T(8,128)(2,1)S(1)} %get-tuple-element.166), channel_id=1, source_target_pairs={{0,8},{4,12},{8,0},{12,4},{16,24},{20,28},{24,16},{28,20},{1,9},{5... | collective-permute-start | bytes 663560 | tf_op jit(solution)/shard_map/ppermute | solution.py:731
  96.5 0.7 collective-permute-start.24
  97.2 1.4 %collective-permute-start.15 = (f32[8,768]{1,0:T(8,128)S(1)}, f32[8,768]{1,0:T(8,128)S(1)}, u32[]{:S(2)}, u32[]{:S(2)}) collective-permute-start(f32[8,768]{1,0:T(8,128)S(1)} %add.13), channel_id=1, source_target_pairs={{0,16},{4,20},{8,24},{12,28},{16,0},{20,4},{24,8},{28,12},{1,17},{... | collective-permute-start | bytes 73736 | tf_op jit(solution)/shard_map/ppermute | solution.py:731
  98.6 3.6 %collective-permute-done.15 = f32[8,768]{1,0:T(8,128)S(1)} collective-permute-done((f32[8,768]{1,0:T(8,128)S(1)}, f32[8,768]{1,0:T(8,128)S(1)}, u32[]{:S(2)}, u32[]{:S(2)}) %collective-permute-start.15) | collective-permute-done | bytes 24608 | tf_op jit(solution)/shard_map/ppermute | solution.py:731
  102.2 1.3 %collective-permute-start.17 = (f32[8,768]{1,0:T(8,128)S(1)}, f32[8,768]{1,0:T(8,128)S(1)}, u32[]{:S(2)}, u32[]{:S(2)}) collective-permute-start(f32[8,768]{1,0:T(8,128)S(1)} %add.14), channel_id=1, source_target_pairs={{0,1},{1,0},{2,3},{3,2},{4,5},{5,4},{6,7},{7,6},{8,9},{9,8},{10,11... | collective-permute-start | bytes 73736 | tf_op jit(solution)/shard_map/ppermute | solution.py:731
  103.5 0.7 collective-permute-start.21
  104.3 1.8 %collective-permute-done.17 = f32[8,768]{1,0:T(8,128)S(1)} collective-permute-done((f32[8,768]{1,0:T(8,128)S(1)}, f32[8,768]{1,0:T(8,128)S(1)}, u32[]{:S(2)}, u32[]{:S(2)}) %collective-permute-start.17) | collective-permute-done | bytes 24608 | tf_op jit(solution)/shard_map/ppermute | solution.py:731
  106.0 3.6 %collective-permute-start.16 = (bf16[128,768]{1,0:T(8,128)(2,1)S(1)}, bf16[128,768]{1,0:T(8,128)(2,1)S(1)}, u32[]{:S(2)}, u32[]{:S(2)}) collective-permute-start(bf16[128,768]{1,0:T(8,128)(2,1)S(1)} %get-tuple-element.157), channel_id=1, source_target_pairs={{0,2},{1,3},{2,0},{3,1},{4,6},{5,7},{6,4},{7,5},{8,10},{9,11},{10,... | collective-permute-start | bytes 589832 | tf_op jit(solution)/shard_map/ppermute | solution.py:731
  109.6 1.4 %collective-permute-start.18 = (f32[8,768]{1,0:T(8,128)S(1)}, f32[8,768]{1,0:T(8,128)S(1)}, u32[]{:S(2)}, u32[]{:S(2)}) collective-permute-start(f32[8,768]{1,0:T(8,128)S(1)} %add.15.refs_4_), channel_id=1, source_target_pairs={{0,2},{1,3},{2,0},{3,1},{4,6},{5,7},{6,4},{7,5},{8,10},{9,11},{10,... | collective-permute-start | bytes 73736 | tf_op jit(solution)/shard_map/ppermute | solution.py:731
  111.2 0.8 collective-permute-start.26
  111.9 1.3 %collective-permute-start.27 = (bf16[80,768]{1,0:T(8,128)(2,1)S(1)}, bf16[80,768]{1,0:T(8,128)(2,1)S(1)}, u32[]{:S(2)}, u32[]{:S(2)}) collective-permute-start(bf16[80,768]{1,0:T(8,128)(2,1)S(1)} %get-tuple-element.182), channel_id=1, source_target_pairs={{0,8},{4,12},{8,0},{12,4},{16,24},{20,28},{24,16},{28,20},{1,9},{5... | collective-permute-start | bytes 368648 | tf_op jit(solution)/shard_map/ppermute | solution.py:731
  113.2 3.9 %collective-permute-done.18.refs_5_ = f32[8,768]{1,0:T(8,128)S(1)} collective-permute-done((f32[8,768]{1,0:T(8,128)S(1)}, f32[8,768]{1,0:T(8,128)S(1)}, u32[]{:S(2)}, u32[]{:S(2)}) %collective-permute-start.18) | collective-permute-done | bytes 24608 | tf_op jit(solution)/shard_map/ppermute | solution.py:731
  117.2 1.0 finish_inputs.1
  118.2 0.6 reduce
  118.8 0.6 reduce.1
  119.4 1.3 %finish_grads.1 = (f32[24,3072]{1,0:T(8,128)}, f32[96,768]{1,0:T(8,128)}, f32[384,96]{1,0:T(8,128)S(1)}, f32[1,96]{1,0:T(1,128)}, f32[3,96,384]{2,1,0:T(8,128)},...) custom-call(f32[112,768]{1,0:T(8,128)S(1)} %get-tuple-element.163.re, ...), custom_call_target="tpu_custom_call" | custom-call | flops 2000000000 | bytes 6000000 | tf_op jit(solution)/shard_map/finish_grads/pallas_call | solution.py:60
  120.7 0.8 copy.37
  (88 shorter events, 1.6 us)
Async XLA Ops:
  1.3 1.1 copy-start.4
  2.4 1.1 copy-start.12
  2.4 1.1 copy-start.13
  2.5 1.1 copy-start.14
  2.5 1.1 copy-start.15
  2.5 1.2 copy-start.16
  2.5 1.2 copy-start.17
  3.0 1.4 %collective-permute-start = (f32[8,768]{1,0:T(8,128)S(1)}, f32[8,768]{1,0:T(8,128)S(1)}, u32[]{:S(2)}, u32[]{:S(2)}) collective-permute-start(f32[8,768]{1,0:T(8,128)S(1)} %stats.1.refs_0_), channel_id=1, source_target_pairs={{0,4},{4,0},{8,12},{12,8},{16,20},{20,16},{24,28},{28,24},{1,5},{5... | collective-permute-start | bytes 73736 | tf_op jit(solution)/shard_map/ppermute | solution.py:731
  3.7 5.2 %copy-start.6 = (f32[3072]{0:T(1024)S(1)}, f32[3072]{0:T(1024)}, u32[]{:S(2)}) copy-start(f32[3072]{0:T(1024)} %param.32) | copy-start | bytes 36868
  3.7 5.2 %copy-start.7 = (s32[2,2,512]{2,1,0:T(2,128)S(1)}, s32[2,2,512]{2,1,0:T(2,128)}, u32[]{:S(2)}) copy-start(s32[2,2,512]{2,1,0:T(2,128)} %box_ref.1) | copy-start | bytes 24580
  3.7 5.2 %copy-start.8 = (s32[2,512]{1,0:T(2,128)S(1)}, s32[2,512]{1,0:T(2,128)}, u32[]{:S(2)}) copy-start(s32[2,512]{1,0:T(2,128)} %line_ref.1) | copy-start | bytes 12292
  3.7 5.2 %copy-start.9 = (f32[6,64]{1,0:T(8,128)S(1)}, f32[6,64]{1,0:T(8,128)}, u32[]{:S(2)}) copy-start(f32[6,64]{1,0:T(8,128)} %table_ref.1) | copy-start | bytes 4612
  4.4 8.2 %copy-start.1 = (bf16[768,3,384]{2,0,1:T(8,128)(2,1)S(1)}, bf16[768,3,384]{2,0,1:T(8,128)(2,1)}, u32[]{:S(2)}) copy-start(bf16[768,3,384]{2,0,1:T(8,128)(2,1)} %param.25) | copy-start | bytes 5308420
  4.4 8.2 %copy-start.2 = (bf16[512,768]{1,0:T(8,128)(2,1)S(1)}, bf16[512,768]{1,0:T(8,128)(2,1)}, u32[]{:S(2)}) copy-start(bf16[512,768]{1,0:T(8,128)(2,1)} %refs_0_.2) | copy-start | bytes 2359300
  4.4 8.2 %copy-start.5 = (bf16[512,768]{1,0:T(8,128)(2,1)S(1)}, bf16[512,768]{1,0:T(8,128)(2,1)}, u32[]{:S(2)}) copy-start(bf16[512,768]{1,0:T(8,128)(2,1)} %visual_ref.7) | copy-start | bytes 2359300
  4.4 5.7 %collective-permute-start.3 = (f32[8,768]{1,0:T(8,128)S(1)}, f32[8,768]{1,0:T(8,128)S(1)}, u32[]{:S(2)}, u32[]{:S(2)}) collective-permute-start(f32[8,768]{1,0:T(8,128)S(1)} %join_stats.1.refs_0_), channel_id=1, source_target_pairs={{0,24},{4,28},{8,16},{12,20},{16,8},{20,12},{24,0},{28,4},{1,25},{... | collective-permute-start | bytes 73736 | tf_op jit(solution)/shard_map/ppermute | solution.py:731
  8.3 3.8 %collective-permute-start.2 = (f32[8,768]{1,0:T(8,128)S(1)}, f32[8,768]{1,0:T(8,128)S(1)}, u32[]{:S(2)}, u32[]{:S(2)}) collective-permute-start(f32[8,768]{1,0:T(8,128)S(1)} %join_stats.1.refs_0_), channel_id=1, source_target_pairs={{0,16},{4,20},{8,24},{12,28},{16,0},{20,4},{24,8},{28,12},{1,17},{... | collective-permute-start | bytes 73736 | tf_op jit(solution)/shard_map/ppermute | solution.py:731
  8.8 3.8 %collective-permute-start.1 = (f32[8,768]{1,0:T(8,128)S(1)}, f32[8,768]{1,0:T(8,128)S(1)}, u32[]{:S(2)}, u32[]{:S(2)}) collective-permute-start(f32[8,768]{1,0:T(8,128)S(1)} %join_stats.1.refs_0_), channel_id=1, source_target_pairs={{0,8},{4,12},{8,0},{12,4},{16,24},{20,28},{24,16},{28,20},{1,9},{5... | collective-permute-start | bytes 73736 | tf_op jit(solution)/shard_map/ppermute | solution.py:731
  8.9 36.5 %slice-start = ((s8[4718592]{0:T(1024)(128)(4,1)}), s8[4194304]{0:T(1024)(128)(4,1)S(1)}, s32[]{:S(2)}) async-start(s8[4718592]{0:T(1024)(128)(4,1)} %bitcast.10), calls=%async_computation | async-start | bytes 8388608
  8.9 36.5 %slice-start.2 = ((s8[4718592]{0:T(1024)(128)(4,1)}), s8[4194304]{0:T(1024)(128)(4,1)S(1)}, s32[]{:S(2)}) async-start(s8[4718592]{0:T(1024)(128)(4,1)} %bitcast.12), calls=%async_computation.2 | async-start | bytes 8388608
  12.6 32.8 %slice-start.1 = ((s8[4718592]{0:T(1024)(128)(4,1)}), s8[524288]{0:T(1024)(128)(4,1)S(1)}, s32[]{:S(2)}) async-start(s8[4718592]{0:T(1024)(128)(4,1)} %bitcast.10), calls=%async_computation.1 | async-start | bytes 1048576
  12.6 32.8 %slice-start.3 = ((s8[4718592]{0:T(1024)(128)(4,1)}), s8[524288]{0:T(1024)(128)(4,1)S(1)}, s32[]{:S(2)}) async-start(s8[4718592]{0:T(1024)(128)(4,1)} %bitcast.12), calls=%async_computation.3 | async-start | bytes 1048576
  16.6 11.1 %collective-permute-start.6 = (bf16[384,256]{1,0:T(8,128)(2,1)S(1)}, bf16[384,256]{1,0:T(8,128)(2,1)S(1)}, u32[]{:S(2)}, u32[]{:S(2)}) collective-permute-start(bf16[384,256]{1,0:T(8,128)(2,1)S(1)} %get-tuple-element.111.refs_7_.refs_8_.refs_6_), channel_id=1, source_target_pairs={{0,3},{1,2},{2,1},{3,0},{4,7},{5,6},{6,5},{7,4},{8,11},{9,10},{10,... | collective-permute-start | bytes 589832 | tf_op jit(solution)/shard_map/ppermute | solution.py:731
  20.6 24.7 %collective-permute-start.5 = (bf16[384,256]{1,0:T(8,128)(2,1)S(1)}, bf16[384,256]{1,0:T(8,128)(2,1)S(1)}, u32[]{:S(2)}, u32[]{:S(2)}) collective-permute-start(bf16[384,256]{1,0:T(8,128)(2,1)S(1)} %get-tuple-element.111.refs_7_.refs_8_.refs_6_), channel_id=1, source_target_pairs={{0,2},{1,3},{2,0},{3,1},{4,6},{5,7},{6,4},{7,5},{8,10},{9,11},{10,... | collective-permute-start | bytes 589832 | tf_op jit(solution)/shard_map/ppermute | solution.py:731
  20.7 24.7 %collective-permute-start.4 = (bf16[384,256]{1,0:T(8,128)(2,1)S(1)}, bf16[384,256]{1,0:T(8,128)(2,1)S(1)}, u32[]{:S(2)}, u32[]{:S(2)}) collective-permute-start(bf16[384,256]{1,0:T(8,128)(2,1)S(1)} %get-tuple-element.111.refs_7_.refs_8_.refs_6_), channel_id=1, source_target_pairs={{0,1},{1,0},{2,3},{3,2},{4,5},{5,4},{6,7},{7,6},{8,9},{9,8},{10,11... | collective-permute-start | bytes 589832 | tf_op jit(solution)/shard_map/ppermute | solution.py:731
  21.3 24.1 %copy-start = (bf16[1536,768]{1,0:T(8,128)(2,1)S(1)}, bf16[1536,768]{1,0:T(8,128)(2,1)}, u32[]{:S(2)}) copy-start(bf16[1536,768]{1,0:T(8,128)(2,1)} %refs_2_.3) | copy-start | bytes 7077892
  21.3 24.1 %copy-start.3 = (bf16[512,768]{1,0:T(8,128)(2,1)S(1)}, bf16[512,768]{1,0:T(8,128)(2,1)}, u32[]{:S(2)}) copy-start(bf16[512,768]{1,0:T(8,128)(2,1)} %refs_1_.3) | copy-start | bytes 2359300
  23.9 31.9 %collective-permute-start.9 = (bf16[384,256]{1,0:T(8,128)(2,1)S(1)}, bf16[384,256]{1,0:T(8,128)(2,1)S(1)}, u32[]{:S(2)}, u32[]{:S(2)}) collective-permute-start(bf16[384,256]{1,0:T(8,128)(2,1)S(1)} %get-tuple-element.119.refs_7_.refs_9_), channel_id=1, source_target_pairs={{0,3},{1,2},{2,1},{3,0},{4,7},{5,6},{6,5},{7,4},{8,11},{9,10},{10,... | collective-permute-start | bytes 589832 | tf_op jit(solution)/shard_map/ppermute | solution.py:731
  27.7 28.1 %collective-permute-start.8 = (bf16[384,256]{1,0:T(8,128)(2,1)S(1)}, bf16[384,256]{1,0:T(8,128)(2,1)S(1)}, u32[]{:S(2)}, u32[]{:S(2)}) collective-permute-start(bf16[384,256]{1,0:T(8,128)(2,1)S(1)} %get-tuple-element.119.refs_7_.refs_9_), channel_id=1, source_target_pairs={{0,2},{1,3},{2,0},{3,1},{4,6},{5,7},{6,4},{7,5},{8,10},{9,11},{10,... | collective-permute-start | bytes 589832 | tf_op jit(solution)/shard_map/ppermute | solution.py:731
  27.7 28.1 %collective-permute-start.7 = (bf16[384,256]{1,0:T(8,128)(2,1)S(1)}, bf16[384,256]{1,0:T(8,128)(2,1)S(1)}, u32[]{:S(2)}, u32[]{:S(2)}) collective-permute-start(bf16[384,256]{1,0:T(8,128)(2,1)S(1)} %get-tuple-element.119.refs_7_.refs_9_), channel_id=1, source_target_pairs={{0,1},{1,0},{2,3},{3,2},{4,5},{5,4},{6,7},{7,6},{8,9},{9,8},{10,11... | collective-permute-start | bytes 589832 | tf_op jit(solution)/shard_map/ppermute | solution.py:731
  70.2 4.4 %collective-permute-start.11 = (bf16[4,144,768]{2,1,0:T(8,128)(2,1)S(1)}, bf16[4,144,768]{2,1,0:T(8,128)(2,1)S(1)}, u32[]{:S(2)}, u32[]{:S(2)}) collective-permute-start(bf16[4,144,768]{2,1,0:T(8,128)(2,1)S(1)} %get-tuple-element.140), channel_id=1, source_target_pairs={{0,4},{4,0},{8,12},{12,8},{16,20},{20,16},{24,28},{28,24},{1,5},{5... | collective-permute-start | bytes 2654216 | tf_op jit(solution)/shard_map/ppermute | solution.py:731
  70.2 3.4 %collective-permute-start.10 = (bf16[4,112,768]{2,1,0:T(8,128)(2,1)S(1)}, bf16[4,112,768]{2,1,0:T(8,128)(2,1)S(1)}, u32[]{:S(2)}, u32[]{:S(2)}) collective-permute-start(bf16[4,112,768]{2,1,0:T(8,128)(2,1)S(1)} %get-tuple-element.124), channel_id=1, source_target_pairs={{0,4},{4,0},{8,12},{12,8},{16,20},{20,16},{24,28},{28,24},{1,5},{5... | collective-permute-start | bytes 2064392 | tf_op jit(solution)/shard_map/ppermute | solution.py:731
  73.8 13.9 %collective-permute-start.19 = (bf16[2,112,768]{2,1,0:T(8,128)(2,1)S(1)}, bf16[2,112,768]{2,1,0:T(8,128)(2,1)S(1)}, u32[]{:S(2)}, u32[]{:S(2)}) collective-permute-start(bf16[2,112,768]{2,1,0:T(8,128)(2,1)S(1)} %get-tuple-element.160), channel_id=1, source_target_pairs={{0,8},{4,12},{8,0},{12,4},{16,24},{20,28},{24,16},{28,20},{1,9},{5... | collective-permute-start | bytes 1032200 | tf_op jit(solution)/shard_map/ppermute | solution.py:731
  74.8 12.8 %collective-permute-start.20 = (bf16[2,144,768]{2,1,0:T(8,128)(2,1)S(1)}, bf16[2,144,768]{2,1,0:T(8,128)(2,1)S(1)}, u32[]{:S(2)}, u32[]{:S(2)}) collective-permute-start(bf16[2,144,768]{2,1,0:T(8,128)(2,1)S(1)} %get-tuple-element.162), channel_id=1, source_target_pairs={{0,16},{4,20},{8,24},{12,28},{16,0},{20,4},{24,8},{28,12},{1,17},{... | collective-permute-start | bytes 1327112 | tf_op jit(solution)/shard_map/ppermute | solution.py:731
  86.4 1.3 %collective-permute-start.13 = (f32[8,768]{1,0:T(8,128)S(1)}, f32[8,768]{1,0:T(8,128)S(1)}, u32[]{:S(2)}, u32[]{:S(2)}) collective-permute-start(f32[8,768]{1,0:T(8,128)S(1)} %get-tuple-element.154), channel_id=1, source_target_pairs={{0,4},{4,0},{8,12},{12,8},{16,20},{20,16},{24,28},{28,24},{1,5},{5... | collective-permute-start | bytes 73736 | tf_op jit(solution)/shard_map/ppermute | solution.py:731
  89.6 4.8 %collective-permute-start.23 = (bf16[4,152,768]{2,1,0:T(8,128)(2,1)S(1)}, bf16[4,152,768]{2,1,0:T(8,128)(2,1)S(1)}, u32[]{:S(2)}, u32[]{:S(2)}) collective-permute-start(bf16[4,152,768]{2,1,0:T(8,128)(2,1)S(1)} %get-tuple-element.172), channel_id=1, source_target_pairs={{0,4},{4,0},{8,12},{12,8},{16,20},{20,16},{24,28},{28,24},{1,5},{5... | collective-permute-start | bytes 2801672 | tf_op jit(solution)/shard_map/ppermute | solution.py:731
  89.8 13.7 %collective-permute-start.12 = (bf16[2,128,768]{2,1,0:T(8,128)(2,1)S(1)}, bf16[2,128,768]{2,1,0:T(8,128)(2,1)S(1)}, u32[]{:S(2)}, u32[]{:S(2)}) collective-permute-start(bf16[2,128,768]{2,1,0:T(8,128)(2,1)S(1)} %get-tuple-element.153), channel_id=1, source_target_pairs={{0,1},{1,0},{2,3},{3,2},{4,5},{5,4},{6,7},{7,6},{8,9},{9,8},{10,11... | collective-permute-start | bytes 1179656 | tf_op jit(solution)/shard_map/ppermute | solution.py:731
  90.5 3.8 %collective-permute-start.14 = (f32[8,768]{1,0:T(8,128)S(1)}, f32[8,768]{1,0:T(8,128)S(1)}, u32[]{:S(2)}, u32[]{:S(2)}) collective-permute-start(f32[8,768]{1,0:T(8,128)S(1)} %add.12), channel_id=1, source_target_pairs={{0,8},{4,12},{8,0},{12,4},{16,24},{20,28},{24,16},{28,20},{1,9},{5... | collective-permute-start | bytes 73736 | tf_op jit(solution)/shard_map/ppermute | solution.py:731
  94.5 16.5 %collective-permute-start.25 = (bf16[2,80,768]{2,1,0:T(8,128)(2,1)S(1)}, bf16[2,80,768]{2,1,0:T(8,128)(2,1)S(1)}, u32[]{:S(2)}, u32[]{:S(2)}) collective-permute-start(bf16[2,80,768]{2,1,0:T(8,128)(2,1)S(1)} %get-tuple-element.178), channel_id=1, source_target_pairs={{0,16},{4,20},{8,24},{12,28},{16,0},{20,4},{24,8},{28,12},{1,17},{... | collective-permute-start | bytes 737288 | tf_op jit(solution)/shard_map/ppermute | solution.py:731
  95.2 15.9 %collective-permute-start.22 = (bf16[144,768]{1,0:T(8,128)(2,1)S(1)}, bf16[144,768]{1,0:T(8,128)(2,1)S(1)}, u32[]{:S(2)}, u32[]{:S(2)}) collective-permute-start(bf16[144,768]{1,0:T(8,128)(2,1)S(1)} %get-tuple-element.166), channel_id=1, source_target_pairs={{0,8},{4,12},{8,0},{12,4},{16,24},{20,28},{24,16},{28,20},{1,9},{5... | collective-permute-start | bytes 663560 | tf_op jit(solution)/shard_map/ppermute | solution.py:731
  96.5 14.6 %collective-permute-start.24 = (bf16[2,72,768]{2,1,0:T(8,128)(2,1)S(1)}, bf16[2,72,768]{2,1,0:T(8,128)(2,1)S(1)}, u32[]{:S(2)}, u32[]{:S(2)}) collective-permute-start(bf16[2,72,768]{2,1,0:T(8,128)(2,1)S(1)} %get-tuple-element.175), channel_id=1, source_target_pairs={{0,8},{4,12},{8,0},{12,4},{16,24},{20,28},{24,16},{28,20},{1,9},{5... | collective-permute-start | bytes 663560 | tf_op jit(solution)/shard_map/ppermute | solution.py:731
  97.2 5.0 %collective-permute-start.15 = (f32[8,768]{1,0:T(8,128)S(1)}, f32[8,768]{1,0:T(8,128)S(1)}, u32[]{:S(2)}, u32[]{:S(2)}) collective-permute-start(f32[8,768]{1,0:T(8,128)S(1)} %add.13), channel_id=1, source_target_pairs={{0,16},{4,20},{8,24},{12,28},{16,0},{20,4},{24,8},{28,12},{1,17},{... | collective-permute-start | bytes 73736 | tf_op jit(solution)/shard_map/ppermute | solution.py:731
  102.2 3.8 %collective-permute-start.17 = (f32[8,768]{1,0:T(8,128)S(1)}, f32[8,768]{1,0:T(8,128)S(1)}, u32[]{:S(2)}, u32[]{:S(2)}) collective-permute-start(f32[8,768]{1,0:T(8,128)S(1)} %add.14), channel_id=1, source_target_pairs={{0,1},{1,0},{2,3},{3,2},{4,5},{5,4},{6,7},{7,6},{8,9},{9,8},{10,11... | collective-permute-start | bytes 73736 | tf_op jit(solution)/shard_map/ppermute | solution.py:731
  103.5 6.1 %collective-permute-start.21 = (bf16[112,768]{1,0:T(8,128)(2,1)S(1)}, bf16[112,768]{1,0:T(8,128)(2,1)S(1)}, u32[]{:S(2)}, u32[]{:S(2)}) collective-permute-start(bf16[112,768]{1,0:T(8,128)(2,1)S(1)} %get-tuple-element.164), channel_id=1, source_target_pairs={{0,16},{4,20},{8,24},{12,28},{16,0},{20,4},{24,8},{28,12},{1,17},{... | collective-permute-start | bytes 516104 | tf_op jit(solution)/shard_map/ppermute | solution.py:731
  106.0 11.1 %collective-permute-start.16 = (bf16[128,768]{1,0:T(8,128)(2,1)S(1)}, bf16[128,768]{1,0:T(8,128)(2,1)S(1)}, u32[]{:S(2)}, u32[]{:S(2)}) collective-permute-start(bf16[128,768]{1,0:T(8,128)(2,1)S(1)} %get-tuple-element.157), channel_id=1, source_target_pairs={{0,2},{1,3},{2,0},{3,1},{4,6},{5,7},{6,4},{7,5},{8,10},{9,11},{10,... | collective-permute-start | bytes 589832 | tf_op jit(solution)/shard_map/ppermute | solution.py:731
  109.6 7.5 %collective-permute-start.18 = (f32[8,768]{1,0:T(8,128)S(1)}, f32[8,768]{1,0:T(8,128)S(1)}, u32[]{:S(2)}, u32[]{:S(2)}) collective-permute-start(f32[8,768]{1,0:T(8,128)S(1)} %add.15.refs_4_), channel_id=1, source_target_pairs={{0,2},{1,3},{2,0},{3,1},{4,6},{5,7},{6,4},{7,5},{8,10},{9,11},{10,... | collective-permute-start | bytes 73736 | tf_op jit(solution)/shard_map/ppermute | solution.py:731
  111.2 8.2 %collective-permute-start.26 = (bf16[72,768]{1,0:T(8,128)(2,1)S(1)}, bf16[72,768]{1,0:T(8,128)(2,1)S(1)}, u32[]{:S(2)}, u32[]{:S(2)}) collective-permute-start(bf16[72,768]{1,0:T(8,128)(2,1)S(1)} %get-tuple-element.180), channel_id=1, source_target_pairs={{0,16},{4,20},{8,24},{12,28},{16,0},{20,4},{24,8},{28,12},{1,17},{... | collective-permute-start | bytes 331784 | tf_op jit(solution)/shard_map/ppermute | solution.py:731
  111.9 7.5 %collective-permute-start.27 = (bf16[80,768]{1,0:T(8,128)(2,1)S(1)}, bf16[80,768]{1,0:T(8,128)(2,1)S(1)}, u32[]{:S(2)}, u32[]{:S(2)}) collective-permute-start(bf16[80,768]{1,0:T(8,128)(2,1)S(1)} %get-tuple-element.182), channel_id=1, source_target_pairs={{0,8},{4,12},{8,0},{12,4},{16,24},{20,28},{24,16},{28,20},{1,9},{5... | collective-permute-start | bytes 368648 | tf_op jit(solution)/shard_map/ppermute | solution.py:731
  (2 other events, 2.2 us)
where the time goes:
time: 122 us; the launch traced here: 121 us
  Pallas kernels  46.9 us (38%)
  starting transfers between devices  43.9 us (36%)
  waiting for transfers between devices  25.7 us (21%)
  local copies, waits for them, and re-layouts  2.05 us (2%)
  between operations  1.76 us (1%)
  other arithmetic  1.23 us (1%)
    pallas_call x19, Pallas kernels, call(): pl.pallas_call(kernel, out_shape=tuple((jax.ShapeDtypeStruct(*entry) if p...  46.9 us
    ppermute x28, starting transfers between devices, swap(): return lax.ppermute(value, axis, [(i, i ^ mask) for i in range(size)])  43.9 us
    ppermute x28, waiting for transfers between devices, swap(): return lax.ppermute(value, axis, [(i, i ^ mask) for i in range(size)])  25.7 us
  transfers between devices with their start and end apart: 28, of which 11 were waited for; matrix products, arithmetic and copies ran while one was open for 1% of the time, Pallas kernels for 20%

commit v1 on v0

--- a/solution.py
+++ b/solution.py
@@ -647,8 +647,8 @@
     width = total.shape[1]
     part_in = grad_in.shape[0]
     part_out = grad_out.shape[0]
-    half_own = grad_ow.shape[1] // 2
-    local_width = grad_ow.shape[0]
+    half_own = grad_ow.shape[0] // 2
+    local_width = grad_ow.shape[1]
     parts = hidden_width // width
     place = lax.axis_index("dp") * lax.axis_size("head") + lax.axis_index("head")
     grad_in[...] = jnp.concatenate(
@@ -660,9 +660,7 @@
     grad_out[...] = total[base : base + part_out]
     base += part_out
     packed = total[base : base + half_own]
-    grad_ow[...] = jnp.transpose(
-        jnp.concatenate([packed[:, :local_width], packed[:, local_width:]], axis=0)
-    )
+    grad_ow[...] = jnp.concatenate([packed[:, :local_width], packed[:, local_width:]], axis=0)
     base += half_own
     lane = iota((width, 128), 0)
     column = iota((width, 128), 1)
@@ -716,8 +714,8 @@
     hat = (visual_ref[pl.ds(start, share), :].astype(F32) - mean) * keep * scale
     dnormed = visual * keep
     shift_gradient, gain_gradient = total[0:1], total[1:2]
-    shift_ref[...] = shift_gradient
-    gain_ref[...] = gain_gradient
+    shift_ref[...] = shift_gradient.reshape(shift_ref.shape)
+    gain_ref[...] = gain_gradient.reshape(gain_ref.shape)
     grad_ref[...] = (
         keep
         * scale
@@ -736,7 +734,9 @@
 
 
 def gather_heads(chunks):
-    return [[piece] + [swap(piece, "head", k) for k in (1, 2, 3)] for piece in chunks]
+    first = [chunks[0]] + [swap(chunks[0], "head", k) for k in (1, 2, 3)]
+    second = after(chunks[1], first[2])
+    return [first, [chunks[1]] + [swap(second, "head", k) for k in (1, 2, 3)]]
 
 
 def across_chips(mine, other, plans, sizes, name):
@@ -995,7 +995,7 @@
             [
                 ((part_in, hidden_width), F32),
                 ((part_out, width), F32),
-                ((local_width, width // dp_count), F32),
+                ((width // dp_count, local_width), F32),
                 ((1, part_out), F32),
                 ((3, width // dp_count, local_width), F32),
                 ((heads_local, table_width // dp_count), F32),
@@ -1006,6 +1006,7 @@
         )
         grad_bias_in = grad_bias_in.reshape(part_out)
         grad_qkv = jnp.transpose(grad_qkv, (1, 0, 2))
+        grad_ow = jnp.transpose(grad_ow)
         own = [value.reshape(part_in) for value in own]
     else:
         layer_out = jnp.concatenate(out, axis=0)
@@ -1052,7 +1053,7 @@
         functools.partial(finish_inputs_kernel, head_count, fused, len(sums)),
         "finish_inputs",
         2,
-        [((share, width), F32)] * 2 + [((1, width), F32)] * 2,
+        [((share, width), F32)] * 2 + [((width,), F32)] * 2,
         [visual_in, stats, *dh_share, *received, *sums],
         visual_count,
         final=range(4),
@@ -1073,8 +1074,8 @@
         own[3],
         own[4],
         own[5],
-        gain_gradient.reshape(width),
-        shift_gradient.reshape(width),
+        gain_gradient,
+        shift_gradient,
     )
 
 

time: 122 us -> 117 us (0.959)
  starting transfers between devices: 43.9 us -> 29.6 us
  waiting for transfers between devices: 25.7 us -> 36.8 us
    ppermute x28, starting transfers between devices: 43.9 us -> 29.6 us  [swap(): return lax.ppermute(value, axis, [(i, i ^ mask) for i in range(size)])]
    ppermute x28, waiting for transfers between devices: 25.7 us -> 36.8 us  [swap(): return lax.ppermute(value, axis, [(i, i ^ mask) for i in range(size)])]
  transfers between devices with their start and end apart: 28 -> 28, of which waited for: 11 -> 13; matrix products, arithmetic and copies ran while one was open for 1% -> 0% of each run, Pallas kernels for 20% -> 21%
where the time goes in v1:
time: 117 us
  Pallas kernels  47 us (40%)
  waiting for transfers between devices  36.8 us (31%)
  starting transfers between devices  29.6 us (25%)
  between operations  1.85 us (2%)
  local copies, waits for them, and re-layouts  1.27 us (1%)
    pallas_call x19, Pallas kernels, call(): pl.pallas_call(kernel, out_shape=tuple((jax.ShapeDtypeStruct(*entry) if p...  47 us
    ppermute x28, waiting for transfers between devices, swap(): return lax.ppermute(value, axis, [(i, i ^ mask) for i in range(size)])  36.8 us
    ppermute x28, starting transfers between devices, swap(): return lax.ppermute(value, axis, [(i, i ^ mask) for i in range(size)])  29.6 us
  transfers between devices with their start and end apart: 28, of which 13 were waited for; matrix products, arithmetic and copies ran while one was open for 0% of the time, Pallas kernels for 21%

profile of v1, /device:TPU:0, one launch (start us, length us, event | category | flops | bytes accessed | tf_op | source)
XLA Modules:
  0.0 116.6 jit_solution(11177002573327994119)
XLA Ops:
  1.3 1.1 copy-done.4
  2.5 0.5 stats.1.refs_0_
  3.0 0.5 collective-permute-start
  3.7 0.6 collective-permute-done.refs_1_
  4.4 3.9 %collective-permute-start.3 = (f32[8,768]{1,0:T(8,128)S(1)}, f32[8,768]{1,0:T(8,128)S(1)}, u32[]{:S(2)}, u32[]{:S(2)}) collective-permute-start(f32[8,768]{1,0:T(8,128)S(1)} %join_stats.1.refs_0_), channel_id=1, source_target_pairs={{0,24},{4,28},{8,16},{12,20},{16,8},{20,12},{24,0},{28,4},{1,25},{... | collective-permute-start | bytes 73736 | tf_op jit(solution)/shard_map/ppermute | solution.py:729
  8.3 0.5 collective-permute-start.2
  8.9 0.3 prep.1
  9.2 0.8 collective-permute-done.3.refs_3_
  10.1 2.0 %collective-permute-done.2.refs_2_ = f32[8,768]{1,0:T(8,128)S(1)} collective-permute-done((f32[8,768]{1,0:T(8,128)S(1)}, f32[8,768]{1,0:T(8,128)S(1)}, u32[]{:S(2)}, u32[]{:S(2)}) %collective-permute-start.2) | collective-permute-done | bytes 24608 | tf_op jit(solution)/shard_map/ppermute | solution.py:729
  12.1 0.5 collective-permute-done.1.refs_1_
  12.6 4.0 %attend_first.1 = (f32[8,768]{1,0:T(8,128)S(1)}, bf16[512,768]{1,0:T(8,128)(2,1)S(1)}, bf16[512,384]{1,0:T(8,128)(2,1)S(1)}, bf16[512,384]{1,0:T(8,128)(2,1)S(1)...) custom-call(s32[1]{0:T(128)S(6)} %copy.37.count_ref, ...), custom_call_target="tpu_custom_call" | custom-call | flops 6000000000 | bytes 18000000 | tf_op jit(solution)/shard_map/attend_first/pallas_call | solution.py:60
  16.6 4.0 %collective-permute-start.6 = (bf16[384,256]{1,0:T(8,128)(2,1)S(1)}, bf16[384,256]{1,0:T(8,128)(2,1)S(1)}, u32[]{:S(2)}, u32[]{:S(2)}) collective-permute-start(bf16[384,256]{1,0:T(8,128)(2,1)S(1)} %get-tuple-element.112.refs_7_.refs_8_.refs_6_), channel_id=1, source_target_pairs={{0,3},{1,2},{2,1},{3,0},{4,7},{5,6},{6,5},{7,4},{8,11},{9,10},{10,... | collective-permute-start | bytes 589832 | tf_op jit(solution)/shard_map/ppermute | solution.py:729
  20.7 0.6 collective-permute-start.4
  21.3 2.6 %attend_second.1 = (bf16[384,256]{1,0:T(8,128)(2,1)S(1)}, bf16[6,512,256]{2,1,0:T(8,128)(2,1)S(1)}) custom-call(s32[1]{0:T(128)S(6)} %copy.37.count_ref, bf16[512,384]{1,0:T(8,128)(2,1)S(1)} %get-tuple-element.144.q_ref.refs_0_, bf16[512,384]{1,0:T(8,128)(2,1)S(1)} %get-tuple-element.118.k_ref.refs_1_, bf16[384,512]{1,0:T(8,128)(2,1)S(1)} %get-tuple-element.119.vt_ref, ...), custom_call_target="tpu_custom_call" | custom-call | flops 3000000000 | bytes 9000000 | tf_op jit(solution)/shard_map/attend_second/pallas_call | solution.py:60
  23.9 11.9 %collective-permute-done.5.refs_9_ = bf16[384,256]{1,0:T(8,128)(2,1)S(1)} collective-permute-done((bf16[384,256]{1,0:T(8,128)(2,1)S(1)}, bf16[384,256]{1,0:T(8,128)(2,1)S(1)}, u32[]{:S(2)}, u32[]{:S(2)}) %collective-permute-start.5) | collective-permute-done | bytes 196640 | tf_op jit(solution)/shard_map/ppermute | solution.py:729
  35.8 3.2 %collective-permute-start.9 = (bf16[384,256]{1,0:T(8,128)(2,1)S(1)}, bf16[384,256]{1,0:T(8,128)(2,1)S(1)}, u32[]{:S(2)}, u32[]{:S(2)}) collective-permute-start(bf16[384,256]{1,0:T(8,128)(2,1)S(1)} %get-tuple-element.121.refs_7_.refs_9_), channel_id=1, source_target_pairs={{0,3},{1,2},{2,1},{3,0},{4,7},{5,6},{6,5},{7,4},{8,11},{9,10},{10,... | collective-permute-start | bytes 589832 | tf_op jit(solution)/shard_map/ppermute | solution.py:729
  39.0 1.2 %collective-permute-start.7 = (bf16[384,256]{1,0:T(8,128)(2,1)S(1)}, bf16[384,256]{1,0:T(8,128)(2,1)S(1)}, u32[]{:S(2)}, u32[]{:S(2)}) collective-permute-start(bf16[384,256]{1,0:T(8,128)(2,1)S(1)} %get-tuple-element.121.refs_7_.refs_9_), channel_id=1, source_target_pairs={{0,1},{1,0},{2,3},{3,2},{4,5},{5,4},{6,7},{7,6},{8,9},{9,8},{10,11... | collective-permute-start | bytes 589832 | tf_op jit(solution)/shard_map/ppermute | solution.py:729
  40.3 10.3 %ffn_0.1 = (bf16[256,768]{1,0:T(8,128)(2,1)S(1)}, f32[128,768]{1,0:T(8,128)S(1)}, bf16[256,3072]{1,0:T(8,128)(2,1)S(1)}, bf16[256,3072]{1,0:T(8,128)(2,1)S(1)}, ...) custom-call(bf16[512,768]{1,0:T(8,128)(2,1)S(1)} %copy-done.2, ...), custom_call_target="tpu_custom_call" | custom-call | flops 8999999488 | bytes 27000000 | tf_op jit(solution)/shard_map/ffn_0/pallas_call | solution.py:60
  50.6 3.2 %collective-permute-done.8.refs_9_ = bf16[384,256]{1,0:T(8,128)(2,1)S(1)} collective-permute-done((bf16[384,256]{1,0:T(8,128)(2,1)S(1)}, bf16[384,256]{1,0:T(8,128)(2,1)S(1)}, u32[]{:S(2)}, u32[]{:S(2)}) %collective-permute-start.8) | collective-permute-done | bytes 196640 | tf_op jit(solution)/shard_map/ppermute | solution.py:729
  53.9 10.3 %ffn_1.1 = (bf16[256,768]{1,0:T(8,128)(2,1)S(1)}, f32[128,768]{1,0:T(8,128)S(1)}, bf16[256,3072]{1,0:T(8,128)(2,1)S(1)}, bf16[256,3072]{1,0:T(8,128)(2,1)S(1)}, ...) custom-call(bf16[512,768]{1,0:T(8,128)(2,1)S(1)} %copy-done.2, ...), custom_call_target="tpu_custom_call" | custom-call | flops 8999999488 | bytes 27000000 | tf_op jit(solution)/shard_map/ffn_1/pallas_call | solution.py:60
  64.2 1.1 weight_grad_in.1
  65.3 3.0 %weight_grad_out.1 = (bf16[512,768]{1,0:T(8,128)(2,1)}, f32[4,144,768]{2,1,0:T(8,128)S(1)}, bf16[4,144,768]{2,1,0:T(8,128)(2,1)S(1)}) custom-call(bf16[256,768]{1,0:T(8,128)(2,1)S(1)} %get-tuple-element.127.refs_0_, bf16[256,768]{1,0:T(8,128)(2,1)S(1)} %get-tuple-element.128.refs_1_, bf16[256,3072]{1,0:T(8,128)(2,1)S(1)} %get-tuple-element.129.refs_2_, ...), custom_call_target="tpu_custom_call" | custom-call | flops 3000000000 | bytes 9000000 | tf_op jit(solution)/shard_map/weight_grad_out/pallas_call | solution.py:60
  68.3 0.5 collective-permute-start.10
  68.8 2.9 %collective-permute-done.10.refs_1_ = bf16[4,112,768]{2,1,0:T(8,128)(2,1)S(1)} collective-permute-done((bf16[4,112,768]{2,1,0:T(8,128)(2,1)S(1)}, bf16[4,112,768]{2,1,0:T(8,128)(2,1)S(1)}, u32[]{:S(2)}, u32[]{:S(2)}) %collective-permute-start.10) | collective-permute-done | bytes 688160 | tf_op jit(solution)/shard_map/ppermute | solution.py:729
  71.8 0.9 collective-permute-start.19
  72.9 1.6 %collective-permute-start.20 = (bf16[2,144,768]{2,1,0:T(8,128)(2,1)S(1)}, bf16[2,144,768]{2,1,0:T(8,128)(2,1)S(1)}, u32[]{:S(2)}, u32[]{:S(2)}) collective-permute-start(bf16[2,144,768]{2,1,0:T(8,128)(2,1)S(1)} %get-tuple-element.164), channel_id=1, source_target_pairs={{0,16},{4,20},{8,24},{12,28},{16,0},{20,4},{24,8},{28,12},{1,17},{... | collective-permute-start | bytes 1327112 | tf_op jit(solution)/shard_map/ppermute | solution.py:729
  74.5 10.0 %back.1 = (bf16[3,512,384]{2,1,0:T(8,128)(2,1)S(1)}, f32[6,128,128]{2,1,0:T(8,128)S(1)}, f32[8,768]{1,0:T(8,128)S(1)}, f32[2,128,768]{2,1,0:T(8,128)S(1)}, bf16[2,128,768]{2,1,0:T(8,128)(2,1)S(1)}) custom-call(s32[1]{0:T(128)S(6)} %copy.37.count_ref, bf16[3,768,384]{2,1,0:T(8,128)(2,1)S(1)} %bitcast.16, bf16[512,768]{1,0:T(8,128)(2,1)S(1)} %copy-done.5, ...), custom_call_target="tpu_custom_call" | custom-call | flops 10000000000 | bytes 30000000 | tf_op jit(solution)/shard_map/back/pallas_call | solution.py:60
  84.5 1.2 %collective-permute-done.13 = f32[8,768]{1,0:T(8,128)S(1)} collective-permute-done((f32[8,768]{1,0:T(8,128)S(1)}, f32[8,768]{1,0:T(8,128)S(1)}, u32[]{:S(2)}, u32[]{:S(2)}) %collective-permute-start.13) | collective-permute-done | bytes 24608 | tf_op jit(solution)/shard_map/ppermute | solution.py:729
  85.8 1.8 %qkv_grad.1 = (f32[4,152,768]{2,1,0:T(8,128)S(1)}, bf16[4,152,768]{2,1,0:T(8,128)(2,1)S(1)}) custom-call(bf16[512,768]{1,0:T(8,128)(2,1)S(1)} %get-tuple-element.170.x_ref, bf16[3,512,384]{2,1,0:T(8,128)(2,1)S(1)} %get-tuple-element.171.dqkv_ref, f32[6,128,128]{2,1,0:T(8,128)S(1)} %get-tuple-element.172.pair_ref), custom_call_target="tpu_custom_call" | custom-call | flops 3000000000 | bytes 9000000 | tf_op jit(solution)/shard_map/qkv_grad/pallas_call | solution.py:60
  87.6 0.2 collective-permute-start.23
  87.9 1.3 %collective-permute-start.14 = (f32[8,768]{1,0:T(8,128)S(1)}, f32[8,768]{1,0:T(8,128)S(1)}, u32[]{:S(2)}, u32[]{:S(2)}) collective-permute-start(f32[8,768]{1,0:T(8,128)S(1)} %add.12), channel_id=1, source_target_pairs={{0,8},{4,12},{8,0},{12,4},{16,24},{20,28},{24,16},{28,20},{1,9},{5... | collective-permute-start | bytes 73736 | tf_op jit(solution)/shard_map/ppermute | solution.py:729
  89.2 2.5 %collective-permute-done.14 = f32[8,768]{1,0:T(8,128)S(1)} collective-permute-done((f32[8,768]{1,0:T(8,128)S(1)}, f32[8,768]{1,0:T(8,128)S(1)}, u32[]{:S(2)}, u32[]{:S(2)}) %collective-permute-start.14) | collective-permute-done | bytes 24608 | tf_op jit(solution)/shard_map/ppermute | solution.py:729
  91.7 0.2 join_cores_qkv.1
  91.9 0.7 collective-permute-start.25
  92.6 1.3 %collective-permute-start.22 = (bf16[144,768]{1,0:T(8,128)(2,1)S(1)}, bf16[144,768]{1,0:T(8,128)(2,1)S(1)}, u32[]{:S(2)}, u32[]{:S(2)}) collective-permute-start(bf16[144,768]{1,0:T(8,128)(2,1)S(1)} %get-tuple-element.168), channel_id=1, source_target_pairs={{0,8},{4,12},{8,0},{12,4},{16,24},{20,28},{24,16},{28,20},{1,9},{5... | collective-permute-start | bytes 663560 | tf_op jit(solution)/shard_map/ppermute | solution.py:729
  93.9 0.7 collective-permute-start.24
  94.6 1.4 %collective-permute-start.15 = (f32[8,768]{1,0:T(8,128)S(1)}, f32[8,768]{1,0:T(8,128)S(1)}, u32[]{:S(2)}, u32[]{:S(2)}) collective-permute-start(f32[8,768]{1,0:T(8,128)S(1)} %add.13), channel_id=1, source_target_pairs={{0,16},{4,20},{8,24},{12,28},{16,0},{20,4},{24,8},{28,12},{1,17},{... | collective-permute-start | bytes 73736 | tf_op jit(solution)/shard_map/ppermute | solution.py:729
  96.0 3.5 %collective-permute-done.15 = f32[8,768]{1,0:T(8,128)S(1)} collective-permute-done((f32[8,768]{1,0:T(8,128)S(1)}, f32[8,768]{1,0:T(8,128)S(1)}, u32[]{:S(2)}, u32[]{:S(2)}) %collective-permute-start.15) | collective-permute-done | bytes 24608 | tf_op jit(solution)/shard_map/ppermute | solution.py:729
  99.5 2.0 %collective-permute-start.17 = (f32[8,768]{1,0:T(8,128)S(1)}, f32[8,768]{1,0:T(8,128)S(1)}, u32[]{:S(2)}, u32[]{:S(2)}) collective-permute-start(f32[8,768]{1,0:T(8,128)S(1)} %add.14), channel_id=1, source_target_pairs={{0,1},{1,0},{2,3},{3,2},{4,5},{5,4},{6,7},{7,6},{8,9},{9,8},{10,11... | collective-permute-start | bytes 73736 | tf_op jit(solution)/shard_map/ppermute | solution.py:729
  101.6 0.7 collective-permute-start.21
  102.3 1.0 collective-permute-done.17
  103.4 2.0 %collective-permute-start.16 = (bf16[128,768]{1,0:T(8,128)(2,1)S(1)}, bf16[128,768]{1,0:T(8,128)(2,1)S(1)}, u32[]{:S(2)}, u32[]{:S(2)}) collective-permute-start(bf16[128,768]{1,0:T(8,128)(2,1)S(1)} %get-tuple-element.159), channel_id=1, source_target_pairs={{0,2},{1,3},{2,0},{3,1},{4,6},{5,7},{6,4},{7,5},{8,10},{9,11},{10,... | collective-permute-start | bytes 589832 | tf_op jit(solution)/shard_map/ppermute | solution.py:729
  105.4 1.6 %collective-permute-done.21.refs_1_ = bf16[112,768]{1,0:T(8,128)(2,1)S(1)} collective-permute-done((bf16[112,768]{1,0:T(8,128)(2,1)S(1)}, bf16[112,768]{1,0:T(8,128)(2,1)S(1)}, u32[]{:S(2)}, u32[]{:S(2)}) %collective-permute-start.21) | collective-permute-done | bytes 172064 | tf_op jit(solution)/shard_map/ppermute | solution.py:729
  107.1 0.8 collective-permute-start.26
  107.9 1.3 %collective-permute-start.27 = (bf16[80,768]{1,0:T(8,128)(2,1)S(1)}, bf16[80,768]{1,0:T(8,128)(2,1)S(1)}, u32[]{:S(2)}, u32[]{:S(2)}) collective-permute-start(bf16[80,768]{1,0:T(8,128)(2,1)S(1)} %get-tuple-element.184), channel_id=1, source_target_pairs={{0,8},{4,12},{8,0},{12,4},{16,24},{20,28},{24,16},{28,20},{1,9},{5... | collective-permute-start | bytes 368648 | tf_op jit(solution)/shard_map/ppermute | solution.py:729
  109.2 4.8 %collective-permute-done.18.refs_5_ = f32[8,768]{1,0:T(8,128)S(1)} collective-permute-done((f32[8,768]{1,0:T(8,128)S(1)}, f32[8,768]{1,0:T(8,128)S(1)}, u32[]{:S(2)}, u32[]{:S(2)}) %collective-permute-start.18) | collective-permute-done | bytes 24608 | tf_op jit(solution)/shard_map/ppermute | solution.py:729
  114.1 1.1 finish_inputs.1
  115.2 1.4 %finish_grads.1 = (f32[24,3072]{1,0:T(8,128)}, f32[96,768]{1,0:T(8,128)}, f32[96,384]{1,0:T(8,128)}, f32[1,96]{1,0:T(1,128)}, f32[3,96,384]{2,1,0:T(8,128)}, /*i...) custom-call(f32[112,768]{1,0:T(8,128)S(1)} %get-tuple-element.165.re, ...), custom_call_target="tpu_custom_call" | custom-call | flops 2000000000 | bytes 6000000 | tf_op jit(solution)/shard_map/finish_grads/pallas_call | solution.py:60
  (85 shorter events, 1.0 us)
Async XLA Ops:
  1.3 1.1 copy-start.4
  2.4 1.1 copy-start.12
  2.4 1.1 copy-start.13
  2.5 1.1 copy-start.14
  2.5 1.1 copy-start.15
  2.5 1.2 copy-start.16
  2.5 1.2 %copy-start.17 = (f32[768]{0:T(1024)S(1)}, f32[768]{0:T(1024)}, u32[]{:S(2)}) copy-start(f32[768]{0:T(1024)} %param.38) | copy-start | bytes 9220
  3.0 1.4 %collective-permute-start = (f32[8,768]{1,0:T(8,128)S(1)}, f32[8,768]{1,0:T(8,128)S(1)}, u32[]{:S(2)}, u32[]{:S(2)}) collective-permute-start(f32[8,768]{1,0:T(8,128)S(1)} %stats.1.refs_0_), channel_id=1, source_target_pairs={{0,4},{4,0},{8,12},{12,8},{16,20},{20,16},{24,28},{28,24},{1,5},{5... | collective-permute-start | bytes 73736 | tf_op jit(solution)/shard_map/ppermute | solution.py:729
  3.7 5.2 %copy-start.6 = (f32[3072]{0:T(1024)S(1)}, f32[3072]{0:T(1024)}, u32[]{:S(2)}) copy-start(f32[3072]{0:T(1024)} %param.32) | copy-start | bytes 36868
  3.7 5.2 %copy-start.7 = (s32[2,2,512]{2,1,0:T(2,128)S(1)}, s32[2,2,512]{2,1,0:T(2,128)}, u32[]{:S(2)}) copy-start(s32[2,2,512]{2,1,0:T(2,128)} %box_ref.1) | copy-start | bytes 24580
  3.7 5.2 %copy-start.8 = (s32[2,512]{1,0:T(2,128)S(1)}, s32[2,512]{1,0:T(2,128)}, u32[]{:S(2)}) copy-start(s32[2,512]{1,0:T(2,128)} %line_ref.1) | copy-start | bytes 12292
  3.7 5.2 %copy-start.9 = (f32[6,64]{1,0:T(8,128)S(1)}, f32[6,64]{1,0:T(8,128)}, u32[]{:S(2)}) copy-start(f32[6,64]{1,0:T(8,128)} %table_ref.1) | copy-start | bytes 4612
  4.4 8.2 %copy-start.1 = (bf16[768,3,384]{2,0,1:T(8,128)(2,1)S(1)}, bf16[768,3,384]{2,0,1:T(8,128)(2,1)}, u32[]{:S(2)}) copy-start(bf16[768,3,384]{2,0,1:T(8,128)(2,1)} %param.25) | copy-start | bytes 5308420
  4.4 8.2 %copy-start.2 = (bf16[512,768]{1,0:T(8,128)(2,1)S(1)}, bf16[512,768]{1,0:T(8,128)(2,1)}, u32[]{:S(2)}) copy-start(bf16[512,768]{1,0:T(8,128)(2,1)} %refs_0_.2) | copy-start | bytes 2359300
  4.4 8.2 %copy-start.5 = (bf16[512,768]{1,0:T(8,128)(2,1)S(1)}, bf16[512,768]{1,0:T(8,128)(2,1)}, u32[]{:S(2)}) copy-start(bf16[512,768]{1,0:T(8,128)(2,1)} %visual_ref.7) | copy-start | bytes 2359300
  4.4 5.7 %collective-permute-start.3 = (f32[8,768]{1,0:T(8,128)S(1)}, f32[8,768]{1,0:T(8,128)S(1)}, u32[]{:S(2)}, u32[]{:S(2)}) collective-permute-start(f32[8,768]{1,0:T(8,128)S(1)} %join_stats.1.refs_0_), channel_id=1, source_target_pairs={{0,24},{4,28},{8,16},{12,20},{16,8},{20,12},{24,0},{28,4},{1,25},{... | collective-permute-start | bytes 73736 | tf_op jit(solution)/shard_map/ppermute | solution.py:729
  8.3 3.8 %collective-permute-start.2 = (f32[8,768]{1,0:T(8,128)S(1)}, f32[8,768]{1,0:T(8,128)S(1)}, u32[]{:S(2)}, u32[]{:S(2)}) collective-permute-start(f32[8,768]{1,0:T(8,128)S(1)} %join_stats.1.refs_0_), channel_id=1, source_target_pairs={{0,16},{4,20},{8,24},{12,28},{16,0},{20,4},{24,8},{28,12},{1,17},{... | collective-permute-start | bytes 73736 | tf_op jit(solution)/shard_map/ppermute | solution.py:729
  8.8 3.8 %collective-permute-start.1 = (f32[8,768]{1,0:T(8,128)S(1)}, f32[8,768]{1,0:T(8,128)S(1)}, u32[]{:S(2)}, u32[]{:S(2)}) collective-permute-start(f32[8,768]{1,0:T(8,128)S(1)} %join_stats.1.refs_0_), channel_id=1, source_target_pairs={{0,8},{4,12},{8,0},{12,4},{16,24},{20,28},{24,16},{28,20},{1,9},{5... | collective-permute-start | bytes 73736 | tf_op jit(solution)/shard_map/ppermute | solution.py:729
  8.9 31.3 %slice-start = ((s8[4718592]{0:T(1024)(128)(4,1)}), s8[4194304]{0:T(1024)(128)(4,1)S(1)}, s32[]{:S(2)}) async-start(s8[4718592]{0:T(1024)(128)(4,1)} %bitcast.11), calls=%async_computation | async-start | bytes 8388608
  8.9 31.3 %slice-start.2 = ((s8[4718592]{0:T(1024)(128)(4,1)}), s8[4194304]{0:T(1024)(128)(4,1)S(1)}, s32[]{:S(2)}) async-start(s8[4718592]{0:T(1024)(128)(4,1)} %bitcast.13), calls=%async_computation.2 | async-start | bytes 8388608
  12.6 27.6 %slice-start.1 = ((s8[4718592]{0:T(1024)(128)(4,1)}), s8[524288]{0:T(1024)(128)(4,1)S(1)}, s32[]{:S(2)}) async-start(s8[4718592]{0:T(1024)(128)(4,1)} %bitcast.11), calls=%async_computation.1 | async-start | bytes 1048576
  12.6 27.6 %slice-start.3 = ((s8[4718592]{0:T(1024)(128)(4,1)}), s8[524288]{0:T(1024)(128)(4,1)S(1)}, s32[]{:S(2)}) async-start(s8[4718592]{0:T(1024)(128)(4,1)} %bitcast.13), calls=%async_computation.3 | async-start | bytes 1048576
  16.6 23.6 %collective-permute-start.6 = (bf16[384,256]{1,0:T(8,128)(2,1)S(1)}, bf16[384,256]{1,0:T(8,128)(2,1)S(1)}, u32[]{:S(2)}, u32[]{:S(2)}) collective-permute-start(bf16[384,256]{1,0:T(8,128)(2,1)S(1)} %get-tuple-element.112.refs_7_.refs_8_.refs_6_), channel_id=1, source_target_pairs={{0,3},{1,2},{2,1},{3,0},{4,7},{5,6},{6,5},{7,4},{8,11},{9,10},{10,... | collective-permute-start | bytes 589832 | tf_op jit(solution)/shard_map/ppermute | solution.py:729
  20.6 15.2 %collective-permute-start.5 = (bf16[384,256]{1,0:T(8,128)(2,1)S(1)}, bf16[384,256]{1,0:T(8,128)(2,1)S(1)}, u32[]{:S(2)}, u32[]{:S(2)}) collective-permute-start(bf16[384,256]{1,0:T(8,128)(2,1)S(1)} %get-tuple-element.112.refs_7_.refs_8_.refs_6_), channel_id=1, source_target_pairs={{0,2},{1,3},{2,0},{3,1},{4,6},{5,7},{6,4},{7,5},{8,10},{9,11},{10,... | collective-permute-start | bytes 589832 | tf_op jit(solution)/shard_map/ppermute | solution.py:729
  20.7 19.6 %collective-permute-start.4 = (bf16[384,256]{1,0:T(8,128)(2,1)S(1)}, bf16[384,256]{1,0:T(8,128)(2,1)S(1)}, u32[]{:S(2)}, u32[]{:S(2)}) collective-permute-start(bf16[384,256]{1,0:T(8,128)(2,1)S(1)} %get-tuple-element.112.refs_7_.refs_8_.refs_6_), channel_id=1, source_target_pairs={{0,1},{1,0},{2,3},{3,2},{4,5},{5,4},{6,7},{7,6},{8,9},{9,8},{10,11... | collective-permute-start | bytes 589832 | tf_op jit(solution)/shard_map/ppermute | solution.py:729
  21.3 19.0 %copy-start = (bf16[1536,768]{1,0:T(8,128)(2,1)S(1)}, bf16[1536,768]{1,0:T(8,128)(2,1)}, u32[]{:S(2)}) copy-start(bf16[1536,768]{1,0:T(8,128)(2,1)} %refs_2_.3) | copy-start | bytes 7077892
  21.3 19.0 %copy-start.3 = (bf16[512,768]{1,0:T(8,128)(2,1)S(1)}, bf16[512,768]{1,0:T(8,128)(2,1)}, u32[]{:S(2)}) copy-start(bf16[512,768]{1,0:T(8,128)(2,1)} %refs_1_.3) | copy-start | bytes 2359300
  35.8 14.8 %collective-permute-start.9 = (bf16[384,256]{1,0:T(8,128)(2,1)S(1)}, bf16[384,256]{1,0:T(8,128)(2,1)S(1)}, u32[]{:S(2)}, u32[]{:S(2)}) collective-permute-start(bf16[384,256]{1,0:T(8,128)(2,1)S(1)} %get-tuple-element.121.refs_7_.refs_9_), channel_id=1, source_target_pairs={{0,3},{1,2},{2,1},{3,0},{4,7},{5,6},{6,5},{7,4},{8,11},{9,10},{10,... | collective-permute-start | bytes 589832 | tf_op jit(solution)/shard_map/ppermute | solution.py:729
  39.0 14.8 %collective-permute-start.8 = (bf16[384,256]{1,0:T(8,128)(2,1)S(1)}, bf16[384,256]{1,0:T(8,128)(2,1)S(1)}, u32[]{:S(2)}, u32[]{:S(2)}) collective-permute-start(bf16[384,256]{1,0:T(8,128)(2,1)S(1)} %get-tuple-element.121.refs_7_.refs_9_), channel_id=1, source_target_pairs={{0,2},{1,3},{2,0},{3,1},{4,6},{5,7},{6,4},{7,5},{8,10},{9,11},{10,... | collective-permute-start | bytes 589832 | tf_op jit(solution)/shard_map/ppermute | solution.py:729
  39.0 14.8 %collective-permute-start.7 = (bf16[384,256]{1,0:T(8,128)(2,1)S(1)}, bf16[384,256]{1,0:T(8,128)(2,1)S(1)}, u32[]{:S(2)}, u32[]{:S(2)}) collective-permute-start(bf16[384,256]{1,0:T(8,128)(2,1)S(1)} %get-tuple-element.121.refs_7_.refs_9_), channel_id=1, source_target_pairs={{0,1},{1,0},{2,3},{3,2},{4,5},{5,4},{6,7},{7,6},{8,9},{9,8},{10,11... | collective-permute-start | bytes 589832 | tf_op jit(solution)/shard_map/ppermute | solution.py:729
  68.3 4.4 %collective-permute-start.11 = (bf16[4,144,768]{2,1,0:T(8,128)(2,1)S(1)}, bf16[4,144,768]{2,1,0:T(8,128)(2,1)S(1)}, u32[]{:S(2)}, u32[]{:S(2)}) collective-permute-start(bf16[4,144,768]{2,1,0:T(8,128)(2,1)S(1)} %get-tuple-element.142), channel_id=1, source_target_pairs={{0,4},{4,0},{8,12},{12,8},{16,20},{20,16},{24,28},{28,24},{1,5},{5... | collective-permute-start | bytes 2654216 | tf_op jit(solution)/shard_map/ppermute | solution.py:729
  68.3 3.4 %collective-permute-start.10 = (bf16[4,112,768]{2,1,0:T(8,128)(2,1)S(1)}, bf16[4,112,768]{2,1,0:T(8,128)(2,1)S(1)}, u32[]{:S(2)}, u32[]{:S(2)}) collective-permute-start(bf16[4,112,768]{2,1,0:T(8,128)(2,1)S(1)} %get-tuple-element.126), channel_id=1, source_target_pairs={{0,4},{4,0},{8,12},{12,8},{16,20},{20,16},{24,28},{28,24},{1,5},{5... | collective-permute-start | bytes 2064392 | tf_op jit(solution)/shard_map/ppermute | solution.py:729
  71.8 13.9 %collective-permute-start.19 = (bf16[2,112,768]{2,1,0:T(8,128)(2,1)S(1)}, bf16[2,112,768]{2,1,0:T(8,128)(2,1)S(1)}, u32[]{:S(2)}, u32[]{:S(2)}) collective-permute-start(bf16[2,112,768]{2,1,0:T(8,128)(2,1)S(1)} %get-tuple-element.162), channel_id=1, source_target_pairs={{0,8},{4,12},{8,0},{12,4},{16,24},{20,28},{24,16},{28,20},{1,9},{5... | collective-permute-start | bytes 1032200 | tf_op jit(solution)/shard_map/ppermute | solution.py:729
  72.9 12.8 %collective-permute-start.20 = (bf16[2,144,768]{2,1,0:T(8,128)(2,1)S(1)}, bf16[2,144,768]{2,1,0:T(8,128)(2,1)S(1)}, u32[]{:S(2)}, u32[]{:S(2)}) collective-permute-start(bf16[2,144,768]{2,1,0:T(8,128)(2,1)S(1)} %get-tuple-element.164), channel_id=1, source_target_pairs={{0,16},{4,20},{8,24},{12,28},{16,0},{20,4},{24,8},{28,12},{1,17},{... | collective-permute-start | bytes 1327112 | tf_op jit(solution)/shard_map/ppermute | solution.py:729
  84.4 1.3 %collective-permute-start.13 = (f32[8,768]{1,0:T(8,128)S(1)}, f32[8,768]{1,0:T(8,128)S(1)}, u32[]{:S(2)}, u32[]{:S(2)}) collective-permute-start(f32[8,768]{1,0:T(8,128)S(1)} %get-tuple-element.156), channel_id=1, source_target_pairs={{0,4},{4,0},{8,12},{12,8},{16,20},{20,16},{24,28},{28,24},{1,5},{5... | collective-permute-start | bytes 73736 | tf_op jit(solution)/shard_map/ppermute | solution.py:729
  87.6 4.1 %collective-permute-start.23 = (bf16[4,152,768]{2,1,0:T(8,128)(2,1)S(1)}, bf16[4,152,768]{2,1,0:T(8,128)(2,1)S(1)}, u32[]{:S(2)}, u32[]{:S(2)}) collective-permute-start(bf16[4,152,768]{2,1,0:T(8,128)(2,1)S(1)} %get-tuple-element.174), channel_id=1, source_target_pairs={{0,4},{4,0},{8,12},{12,8},{16,20},{20,16},{24,28},{28,24},{1,5},{5... | collective-permute-start | bytes 2801672 | tf_op jit(solution)/shard_map/ppermute | solution.py:729
  87.9 13.7 %collective-permute-start.12 = (bf16[2,128,768]{2,1,0:T(8,128)(2,1)S(1)}, bf16[2,128,768]{2,1,0:T(8,128)(2,1)S(1)}, u32[]{:S(2)}, u32[]{:S(2)}) collective-permute-start(bf16[2,128,768]{2,1,0:T(8,128)(2,1)S(1)} %get-tuple-element.155), channel_id=1, source_target_pairs={{0,1},{1,0},{2,3},{3,2},{4,5},{5,4},{6,7},{7,6},{8,9},{9,8},{10,11... | collective-permute-start | bytes 1179656 | tf_op jit(solution)/shard_map/ppermute | solution.py:729
  87.9 3.8 %collective-permute-start.14 = (f32[8,768]{1,0:T(8,128)S(1)}, f32[8,768]{1,0:T(8,128)S(1)}, u32[]{:S(2)}, u32[]{:S(2)}) collective-permute-start(f32[8,768]{1,0:T(8,128)S(1)} %add.12), channel_id=1, source_target_pairs={{0,8},{4,12},{8,0},{12,4},{16,24},{20,28},{24,16},{28,20},{1,9},{5... | collective-permute-start | bytes 73736 | tf_op jit(solution)/shard_map/ppermute | solution.py:729
  91.9 15.2 %collective-permute-start.25 = (bf16[2,80,768]{2,1,0:T(8,128)(2,1)S(1)}, bf16[2,80,768]{2,1,0:T(8,128)(2,1)S(1)}, u32[]{:S(2)}, u32[]{:S(2)}) collective-permute-start(bf16[2,80,768]{2,1,0:T(8,128)(2,1)S(1)} %get-tuple-element.180), channel_id=1, source_target_pairs={{0,16},{4,20},{8,24},{12,28},{16,0},{20,4},{24,8},{28,12},{1,17},{... | collective-permute-start | bytes 737288 | tf_op jit(solution)/shard_map/ppermute | solution.py:729
  92.6 14.4 %collective-permute-start.22 = (bf16[144,768]{1,0:T(8,128)(2,1)S(1)}, bf16[144,768]{1,0:T(8,128)(2,1)S(1)}, u32[]{:S(2)}, u32[]{:S(2)}) collective-permute-start(bf16[144,768]{1,0:T(8,128)(2,1)S(1)} %get-tuple-element.168), channel_id=1, source_target_pairs={{0,8},{4,12},{8,0},{12,4},{16,24},{20,28},{24,16},{28,20},{1,9},{5... | collective-permute-start | bytes 663560 | tf_op jit(solution)/shard_map/ppermute | solution.py:729
  93.9 13.1 %collective-permute-start.24 = (bf16[2,72,768]{2,1,0:T(8,128)(2,1)S(1)}, bf16[2,72,768]{2,1,0:T(8,128)(2,1)S(1)}, u32[]{:S(2)}, u32[]{:S(2)}) collective-permute-start(bf16[2,72,768]{2,1,0:T(8,128)(2,1)S(1)} %get-tuple-element.177), channel_id=1, source_target_pairs={{0,8},{4,12},{8,0},{12,4},{16,24},{20,28},{24,16},{28,20},{1,9},{5... | collective-permute-start | bytes 663560 | tf_op jit(solution)/shard_map/ppermute | solution.py:729
  94.6 4.9 %collective-permute-start.15 = (f32[8,768]{1,0:T(8,128)S(1)}, f32[8,768]{1,0:T(8,128)S(1)}, u32[]{:S(2)}, u32[]{:S(2)}) collective-permute-start(f32[8,768]{1,0:T(8,128)S(1)} %add.13), channel_id=1, source_target_pairs={{0,16},{4,20},{8,24},{12,28},{16,0},{20,4},{24,8},{28,12},{1,17},{... | collective-permute-start | bytes 73736 | tf_op jit(solution)/shard_map/ppermute | solution.py:729
  99.5 3.8 %collective-permute-start.17 = (f32[8,768]{1,0:T(8,128)S(1)}, f32[8,768]{1,0:T(8,128)S(1)}, u32[]{:S(2)}, u32[]{:S(2)}) collective-permute-start(f32[8,768]{1,0:T(8,128)S(1)} %add.14), channel_id=1, source_target_pairs={{0,1},{1,0},{2,3},{3,2},{4,5},{5,4},{6,7},{7,6},{8,9},{9,8},{10,11... | collective-permute-start | bytes 73736 | tf_op jit(solution)/shard_map/ppermute | solution.py:729
  101.6 5.4 %collective-permute-start.21 = (bf16[112,768]{1,0:T(8,128)(2,1)S(1)}, bf16[112,768]{1,0:T(8,128)(2,1)S(1)}, u32[]{:S(2)}, u32[]{:S(2)}) collective-permute-start(bf16[112,768]{1,0:T(8,128)(2,1)S(1)} %get-tuple-element.166), channel_id=1, source_target_pairs={{0,16},{4,20},{8,24},{12,28},{16,0},{20,4},{24,8},{28,12},{1,17},{... | collective-permute-start | bytes 516104 | tf_op jit(solution)/shard_map/ppermute | solution.py:729
  103.4 10.7 %collective-permute-start.16 = (bf16[128,768]{1,0:T(8,128)(2,1)S(1)}, bf16[128,768]{1,0:T(8,128)(2,1)S(1)}, u32[]{:S(2)}, u32[]{:S(2)}) collective-permute-start(bf16[128,768]{1,0:T(8,128)(2,1)S(1)} %get-tuple-element.159), channel_id=1, source_target_pairs={{0,2},{1,3},{2,0},{3,1},{4,6},{5,7},{6,4},{7,5},{8,10},{9,11},{10,... | collective-permute-start | bytes 589832 | tf_op jit(solution)/shard_map/ppermute | solution.py:729
  107.0 7.1 %collective-permute-start.18 = (f32[8,768]{1,0:T(8,128)S(1)}, f32[8,768]{1,0:T(8,128)S(1)}, u32[]{:S(2)}, u32[]{:S(2)}) collective-permute-start(f32[8,768]{1,0:T(8,128)S(1)} %add.15.refs_4_), channel_id=1, source_target_pairs={{0,2},{1,3},{2,0},{3,1},{4,6},{5,7},{6,4},{7,5},{8,10},{9,11},{10,... | collective-permute-start | bytes 73736 | tf_op jit(solution)/shard_map/ppermute | solution.py:729
  107.1 8.0 %collective-permute-start.26 = (bf16[72,768]{1,0:T(8,128)(2,1)S(1)}, bf16[72,768]{1,0:T(8,128)(2,1)S(1)}, u32[]{:S(2)}, u32[]{:S(2)}) collective-permute-start(bf16[72,768]{1,0:T(8,128)(2,1)S(1)} %get-tuple-element.182), channel_id=1, source_target_pairs={{0,16},{4,20},{8,24},{12,28},{16,0},{20,4},{24,8},{28,12},{1,17},{... | collective-permute-start | bytes 331784 | tf_op jit(solution)/shard_map/ppermute | solution.py:729
  107.9 7.3 %collective-permute-start.27 = (bf16[80,768]{1,0:T(8,128)(2,1)S(1)}, bf16[80,768]{1,0:T(8,128)(2,1)S(1)}, u32[]{:S(2)}, u32[]{:S(2)}) collective-permute-start(bf16[80,768]{1,0:T(8,128)(2,1)S(1)} %get-tuple-element.184), channel_id=1, source_target_pairs={{0,8},{4,12},{8,0},{12,4},{16,24},{20,28},{24,16},{28,20},{1,9},{5... | collective-permute-start | bytes 368648 | tf_op jit(solution)/shard_map/ppermute | solution.py:729
  (2 other events, 2.2 us)

commit v2 on v1

--- a/solution.py
+++ b/solution.py
@@ -546,12 +546,12 @@
     head_groups(q_ref.shape[1] // HD, group)
 
 
-def back_kernel(
-    relative, count_ref, w_ref, visual_ref, stats_ref, *refs
-):
+def back_kernel(relative, count_ref, w_ref, visual_ref, stats_ref, x_ref, *refs):
     steps = lax.axis_size("head")
     inner, refs = refs[: 6 + 4 * CHUNKS], refs[6 + 4 * CHUNKS :]
-    dqkv_ref, pair_ref, sums_ref = refs[:3]
+    sums_ref, refs = refs[0], refs[1:]
+    part_refs, refs = refs[: 1 + relative], refs[1 + relative :]
+    grad_refs, (dqkv_ref, pair_ref), whole = refs[:2], refs[2:4], refs[4:]
     attend_back_heads(count_ref, inner, dqkv_ref, pair_ref)
     visual = stream_is_visual()
     tokens = visual_ref.shape[0]
@@ -562,10 +562,10 @@
     for k in range(steps):
         if relative:
             start = pl.multiple_of((lax.axis_index("head") ^ k) * share, share)
-            target = refs[3 + k % 2].at[k // 2]
+            target = part_refs[k % 2].at[k // 2]
         else:
             start = k * share
-            target = refs[3].at[k]
+            target = part_refs[0].at[k]
         rows = pl.ds(start, share)
         part = functools.reduce(
             jnp.add, (dot(dqkv_ref[m, rows, :], w_ref[m], NT) for m in range(3))
@@ -579,6 +579,7 @@
     sums_ref[...] = jnp.concatenate(
         [shift_sum, gain_sum, jnp.zeros((6, mean.shape[1]), F32)], axis=0
     )
+    qkv_grads(relative, x_ref, dqkv_ref, pair_ref, *grad_refs, *whole)
 
 
 def join_pair_kernel(keep_ref, other_ref, own_ref, send_ref):
@@ -604,7 +605,7 @@
     return table
 
 
-def qkv_grad_kernel(fused, x_ref, dqkv_ref, pair_ref, *outs):
+def qkv_grads(fused, x_ref, dqkv_ref, pair_ref, *outs):
     tokens, width = x_ref.shape
     local_width = dqkv_ref.shape[2]
     table = table_sums((pair_ref,))
@@ -930,61 +931,60 @@
         ffn_stages = across_chips(mine, other, [X_FIRST], [in_rows], "join_cores_in")
         ffn_stages += across_chips(mine_out, other_out, [Y_FIRST], [out_rows], "join_cores_out")
     inner = [q, k, v, kt, one, back, *heads, *dheads, *dheads_t, prob_one, prob_two]
+    packed_qkv = 3 * (width // dp_count) // 2 + 8
+    scratch = [
+        pltpu.VMEM((3, tokens, local_width), BF16),
+        pltpu.VMEM((heads_local, LEVELS, LEVELS), F32),
+    ]
     if fused:
         inner[0] = after(q, *(stage[0] for stage in ffn_stages))
         part_outs = [((2, share, width), F32), ((2, share, width), BF16)]
+        grad_outs = [((4, packed_qkv, width), F32), ((4, packed_qkv, width), BF16)]
+        scratch.append(pltpu.VMEM((3, width, local_width), F32))
     else:
         part_outs = [((head_count, share, width), BF16)]
-    dqkv, pairs, sums, *parts = call(
+        grad_outs = [((3, width, local_width), BF16), ((8, table_width), F32)]
+    sums, *rest = call(
         functools.partial(back_kernel, fused),
         "back",
-        10,
-        [
-            ((3, tokens, local_width), BF16),
-            ((heads_local, LEVELS, LEVELS), F32),
-            packed_shape,
-        ]
-        + part_outs,
-        [weight, visual_in, stats] + inner,
+        12,
+        [packed_shape] + part_outs + grad_outs,
+        [weight, visual_in, stats, x] + inner,
         visual_count,
-    )
+        scratch=scratch,
+    )
+    parts, grads = rest[: len(part_outs)], rest[len(part_outs) :]
     if fused:
+        mine, sib = grads
         keep, send = parts
+        arrived = [stage[1] for stage in ffn_stages]
+        send, sib, sums, *arrived = lax.optimization_barrier((send, sib, sums, *arrived))
+        ffn_stages = [(stage[0], other, stage[2]) for stage, other in zip(ffn_stages, arrived)]
         near = swap(send, "head", 1)
         sums = sums + swap(sums, "dp", 1)
         ffn_blocks, ffn_joined = second_exchange(ffn_stages, "join_chips_ffn", [sums])
         sums = sums + swap(sums, "dp", 2)
-        block_rows = 3 * (width // dp_count) + 16
-        mine, sib = call(
-            functools.partial(qkv_grad_kernel, True),
-            "qkv_grad",
-            3,
-            [
-                ((4, block_rows // 2, 2 * local_width), F32),
-                ((4, block_rows // 2, 2 * local_width), BF16),
-            ],
-            [after(x, ffn_joined[0]), dqkv, pairs],
-            scratch=[pltpu.VMEM((3, width, local_width), F32)],
-        )
-        first_rows = block_rows // 4 // 8 * 8
+        first_rows = packed_qkv // 2 // 8 * 8
         stages = across_chips(
             mine,
-            after(swap(sib, "dp", 1), sums),
+            after(swap(sib, "dp", 1), ffn_joined[0]),
             [X_FIRST, Y_FIRST],
-            [first_rows, block_rows // 2 - first_rows],
+            [first_rows, packed_qkv - first_rows],
             "join_cores_qkv",
         )
         sums = sums + swap(sums, "dp", 4)
-        qkv_blocks, unused_joined = second_exchange(stages, "join_chips_qkv", ffn_blocks)
+        qkv_blocks, unused_joined = second_exchange(stages, "join_chips_qkv", ffn_blocks[::2])
         same, send = call(
             join_pair_kernel,
             "join_pair",
             1,
             [((share, width), F32), ((share, width), BF16)],
-            [keep, after(near, sums)],
+            [keep, near],
         )
         received = [same, swap(send, "head", 2)]
+        sums = after(sums, same)
         sums = sums + swap(sums, "head", 1)
+        sums = after(sums, *ffn_blocks)
         sums = [sums, swap(sums, "head", 2)]
         blocks = ffn_blocks + qkv_blocks
         one_row = ((1, part_in), F32)
@@ -1038,13 +1038,7 @@
             vec[3 : 3 + hidden_width // width].reshape(hidden_width), place * part_out, part_out, 0
         )
         sums = [lax.psum(sums, ("dp", "head"))]
-        grad, table = call(
-            functools.partial(qkv_grad_kernel, False),
-            "qkv_grad",
-            3,
-            [((3, width, local_width), BF16), ((8, table_width), F32)],
-            [x, dqkv, pairs],
-        )
+        grad, table = grads
         received = [lax.all_to_all(parts[0], "head", 0, 0, tiled=True)]
         grad_qkv = jnp.transpose(scatter(grad, 1), (1, 0, 2))
         grad_table = scatter(table[:heads_local], 1)

time: 117 us -> 116 us (level)
  starting transfers between devices: 29.6 us -> 27.4 us
  waiting for transfers between devices: 36.8 us -> 38.5 us
    ppermute x28, starting transfers between devices: 29.6 us -> 27.4 us  [swap(): return lax.ppermute(value, axis, [(i, i ^ mask) for i in range(size)])]
    ppermute x28, waiting for transfers between devices: 36.8 us -> 38.5 us  [swap(): return lax.ppermute(value, axis, [(i, i ^ mask) for i in range(size)])]
    pallas_call x19 -> x18, Pallas kernels: 47 us -> 46.7 us  [call(): pl.pallas_call(kernel, out_shape=tuple((jax.ShapeDtypeStruct(*entry) if p...]
  transfers between devices with their start and end apart: 28 -> 28, of which waited for: 13 -> 14; matrix products, arithmetic and copies ran while one was open for 0% -> 0% of each run, Pallas kernels for 21% -> 23%
where the time goes in v2:
time: 116 us
  Pallas kernels  46.7 us (40%)
  waiting for transfers between devices  38.5 us (33%)
  starting transfers between devices  27.4 us (24%)
  between operations  1.84 us (2%)
  local copies, waits for them, and re-layouts  1.27 us (1%)
    pallas_call x18, Pallas kernels, call(): pl.pallas_call(kernel, out_shape=tuple((jax.ShapeDtypeStruct(*entry) if p...  46.7 us
    ppermute x28, waiting for transfers between devices, swap(): return lax.ppermute(value, axis, [(i, i ^ mask) for i in range(size)])  38.5 us
    ppermute x28, starting transfers between devices, swap(): return lax.ppermute(value, axis, [(i, i ^ mask) for i in range(size)])  27.4 us
  transfers between devices with their start and end apart: 28, of which 14 were waited for; matrix products, arithmetic and copies ran while one was open for 0% of the time, Pallas kernels for 23%

profile of v2, /device:TPU:0, one launch (start us, length us, event | category | flops | bytes accessed | tf_op | source)
XLA Modules:
  0.0 115.8 jit_solution(16633702025454358091)
XLA Ops:
  1.3 1.1 copy-done.4
  2.5 0.5 stats.1.refs_0_
  3.0 0.5 collective-permute-start
  3.7 0.6 collective-permute-done.refs_1_
  4.4 3.9 %collective-permute-start.3 = (f32[8,768]{1,0:T(8,128)S(1)}, f32[8,768]{1,0:T(8,128)S(1)}, u32[]{:S(2)}, u32[]{:S(2)}) collective-permute-start(f32[8,768]{1,0:T(8,128)S(1)} %join_stats.1.refs_0_), channel_id=1, source_target_pairs={{0,24},{4,28},{8,16},{12,20},{16,8},{20,12},{24,0},{28,4},{1,25},{... | collective-permute-start | bytes 73736 | tf_op jit(solution)/shard_map/ppermute | solution.py:730
  8.3 0.5 collective-permute-start.2
  8.9 0.3 prep.1
  9.2 0.8 collective-permute-done.3.refs_3_
  10.1 2.0 %collective-permute-done.2.refs_2_ = f32[8,768]{1,0:T(8,128)S(1)} collective-permute-done((f32[8,768]{1,0:T(8,128)S(1)}, f32[8,768]{1,0:T(8,128)S(1)}, u32[]{:S(2)}, u32[]{:S(2)}) %collective-permute-start.2) | collective-permute-done | bytes 24608 | tf_op jit(solution)/shard_map/ppermute | solution.py:730
  12.1 0.5 collective-permute-done.1.refs_1_
  12.6 4.0 %attend_first.1 = (f32[8,768]{1,0:T(8,128)S(1)}, bf16[512,768]{1,0:T(8,128)(2,1)S(1)}, bf16[512,384]{1,0:T(8,128)(2,1)S(1)}, bf16[512,384]{1,0:T(8,128)(2,1)S(1)...) custom-call(s32[1]{0:T(128)S(6)} %copy.37.count_ref, ...), custom_call_target="tpu_custom_call" | custom-call | flops 6000000000 | bytes 18000000 | tf_op jit(solution)/shard_map/attend_first/pallas_call | solution.py:60
  16.6 4.0 %collective-permute-start.6 = (bf16[384,256]{1,0:T(8,128)(2,1)S(1)}, bf16[384,256]{1,0:T(8,128)(2,1)S(1)}, u32[]{:S(2)}, u32[]{:S(2)}) collective-permute-start(bf16[384,256]{1,0:T(8,128)(2,1)S(1)} %get-tuple-element.115.refs_7_.refs_8_.refs_6_), channel_id=1, source_target_pairs={{0,3},{1,2},{2,1},{3,0},{4,7},{5,6},{6,5},{7,4},{8,11},{9,10},{10,... | collective-permute-start | bytes 589832 | tf_op jit(solution)/shard_map/ppermute | solution.py:730
  20.7 0.6 collective-permute-start.4
  21.3 2.6 %attend_second.1 = (bf16[384,256]{1,0:T(8,128)(2,1)S(1)}, bf16[6,512,256]{2,1,0:T(8,128)(2,1)S(1)}) custom-call(s32[1]{0:T(128)S(6)} %copy.37.count_ref, bf16[512,384]{1,0:T(8,128)(2,1)S(1)} %get-tuple-element.148.q_ref.refs_0_, bf16[512,384]{1,0:T(8,128)(2,1)S(1)} %get-tuple-element.121.k_ref.refs_1_, bf16[384,512]{1,0:T(8,128)(2,1)S(1)} %get-tuple-element.122.vt_ref, ...), custom_call_target="tpu_custom_call" | custom-call | flops 3000000000 | bytes 9000000 | tf_op jit(solution)/shard_map/attend_second/pallas_call | solution.py:60
  23.9 11.9 %collective-permute-done.5.refs_9_ = bf16[384,256]{1,0:T(8,128)(2,1)S(1)} collective-permute-done((bf16[384,256]{1,0:T(8,128)(2,1)S(1)}, bf16[384,256]{1,0:T(8,128)(2,1)S(1)}, u32[]{:S(2)}, u32[]{:S(2)}) %collective-permute-start.5) | collective-permute-done | bytes 196640 | tf_op jit(solution)/shard_map/ppermute | solution.py:730
  35.8 3.2 %collective-permute-start.9 = (bf16[384,256]{1,0:T(8,128)(2,1)S(1)}, bf16[384,256]{1,0:T(8,128)(2,1)S(1)}, u32[]{:S(2)}, u32[]{:S(2)}) collective-permute-start(bf16[384,256]{1,0:T(8,128)(2,1)S(1)} %get-tuple-element.124.refs_7_.refs_9_), channel_id=1, source_target_pairs={{0,3},{1,2},{2,1},{3,0},{4,7},{5,6},{6,5},{7,4},{8,11},{9,10},{10,... | collective-permute-start | bytes 589832 | tf_op jit(solution)/shard_map/ppermute | solution.py:730
  39.0 1.2 %collective-permute-start.7 = (bf16[384,256]{1,0:T(8,128)(2,1)S(1)}, bf16[384,256]{1,0:T(8,128)(2,1)S(1)}, u32[]{:S(2)}, u32[]{:S(2)}) collective-permute-start(bf16[384,256]{1,0:T(8,128)(2,1)S(1)} %get-tuple-element.124.refs_7_.refs_9_), channel_id=1, source_target_pairs={{0,1},{1,0},{2,3},{3,2},{4,5},{5,4},{6,7},{7,6},{8,9},{9,8},{10,11... | collective-permute-start | bytes 589832 | tf_op jit(solution)/shard_map/ppermute | solution.py:730
  40.3 10.3 %ffn_0.1 = (bf16[256,768]{1,0:T(8,128)(2,1)S(1)}, f32[128,768]{1,0:T(8,128)S(1)}, bf16[256,3072]{1,0:T(8,128)(2,1)S(1)}, bf16[256,3072]{1,0:T(8,128)(2,1)S(1)}, ...) custom-call(bf16[512,768]{1,0:T(8,128)(2,1)S(1)} %copy-done.2, ...), custom_call_target="tpu_custom_call" | custom-call | flops 8999999488 | bytes 27000000 | tf_op jit(solution)/shard_map/ffn_0/pallas_call | solution.py:60
  50.6 3.2 %collective-permute-done.8.refs_9_ = bf16[384,256]{1,0:T(8,128)(2,1)S(1)} collective-permute-done((bf16[384,256]{1,0:T(8,128)(2,1)S(1)}, bf16[384,256]{1,0:T(8,128)(2,1)S(1)}, u32[]{:S(2)}, u32[]{:S(2)}) %collective-permute-start.8) | collective-permute-done | bytes 196640 | tf_op jit(solution)/shard_map/ppermute | solution.py:730
  53.9 10.3 %ffn_1.1 = (bf16[256,768]{1,0:T(8,128)(2,1)S(1)}, f32[128,768]{1,0:T(8,128)S(1)}, bf16[256,3072]{1,0:T(8,128)(2,1)S(1)}, bf16[256,3072]{1,0:T(8,128)(2,1)S(1)}, ...) custom-call(bf16[512,768]{1,0:T(8,128)(2,1)S(1)} %copy-done.2, ...), custom_call_target="tpu_custom_call" | custom-call | flops 8999999488 | bytes 27000000 | tf_op jit(solution)/shard_map/ffn_1/pallas_call | solution.py:60
  64.2 1.1 weight_grad_in.1
  65.3 3.0 %weight_grad_out.1 = (bf16[512,768]{1,0:T(8,128)(2,1)}, f32[4,144,768]{2,1,0:T(8,128)S(1)}, bf16[4,144,768]{2,1,0:T(8,128)(2,1)S(1)}) custom-call(bf16[256,768]{1,0:T(8,128)(2,1)S(1)} %get-tuple-element.130.refs_0_, bf16[256,768]{1,0:T(8,128)(2,1)S(1)} %get-tuple-element.131.refs_1_, bf16[256,3072]{1,0:T(8,128)(2,1)S(1)} %get-tuple-element.132.refs_2_, ...), custom_call_target="tpu_custom_call" | custom-call | flops 3000000000 | bytes 9000000 | tf_op jit(solution)/shard_map/weight_grad_out/pallas_call | solution.py:60
  68.3 0.5 collective-permute-start.10
  68.8 2.9 %collective-permute-done.10.refs_1_ = bf16[4,112,768]{2,1,0:T(8,128)(2,1)S(1)} collective-permute-done((bf16[4,112,768]{2,1,0:T(8,128)(2,1)S(1)}, bf16[4,112,768]{2,1,0:T(8,128)(2,1)S(1)}, u32[]{:S(2)}, u32[]{:S(2)}) %collective-permute-start.10) | collective-permute-done | bytes 688160 | tf_op jit(solution)/shard_map/ppermute | solution.py:730
  71.8 0.9 collective-permute-start.12
  72.9 1.6 %collective-permute-start.13 = (bf16[2,144,768]{2,1,0:T(8,128)(2,1)S(1)}, bf16[2,144,768]{2,1,0:T(8,128)(2,1)S(1)}, u32[]{:S(2)}, u32[]{:S(2)}) collective-permute-start(bf16[2,144,768]{2,1,0:T(8,128)(2,1)S(1)} %get-tuple-element.163), channel_id=1, source_target_pairs={{0,16},{4,20},{8,24},{12,28},{16,0},{20,4},{24,8},{28,12},{1,17},{... | collective-permute-start | bytes 1327112 | tf_op jit(solution)/shard_map/ppermute | solution.py:730
  74.5 11.5 %back.1 = (f32[8,768]{1,0:T(8,128)S(1)}, f32[2,128,768]{2,1,0:T(8,128)S(1)}, bf16[2,128,768]{2,1,0:T(8,128)(2,1)S(1)}, f32[4,152,768]{2,1,0:T(8,128)S(1)}, bf16[4,152,768]{2,1,0:T(8,128)(2,1)S(1)}) custom-call(s32[1]{0:T(128)S(6)} %copy.37.count_ref, bf16[3,768,384]{2,1,0:T(8,128)(2,1)S(1)} %bitcast.16, bf16[512,768]{1,0:T(8,128)(2,1)S(1)} %copy-done.5, ...), custom_call_target="tpu_custom_call" | custom-call | flops 12000000000 | bytes 36000000 | tf_op jit(solution)/shard_map/back/pallas_call | solution.py:60
  86.1 0.4 collective-permute-start.16
  86.5 2.0 %collective-permute-done.16 = f32[8,768]{1,0:T(8,128)S(1)} collective-permute-done((f32[8,768]{1,0:T(8,128)S(1)}, f32[8,768]{1,0:T(8,128)S(1)}, u32[]{:S(2)}, u32[]{:S(2)}) %collective-permute-start.16) | collective-permute-done | bytes 24608 | tf_op jit(solution)/shard_map/ppermute | solution.py:730
  88.6 1.3 %collective-permute-start.17 = (f32[8,768]{1,0:T(8,128)S(1)}, f32[8,768]{1,0:T(8,128)S(1)}, u32[]{:S(2)}, u32[]{:S(2)}) collective-permute-start(f32[8,768]{1,0:T(8,128)S(1)} %add.12), channel_id=1, source_target_pairs={{0,8},{4,12},{8,0},{12,4},{16,24},{20,28},{24,16},{28,20},{1,9},{5... | collective-permute-start | bytes 73736 | tf_op jit(solution)/shard_map/ppermute | solution.py:730
  90.0 2.4 %collective-permute-done.17 = f32[8,768]{1,0:T(8,128)S(1)} collective-permute-done((f32[8,768]{1,0:T(8,128)S(1)}, f32[8,768]{1,0:T(8,128)S(1)}, u32[]{:S(2)}, u32[]{:S(2)}) %collective-permute-start.17) | collective-permute-done | bytes 24608 | tf_op jit(solution)/shard_map/ppermute | solution.py:730
  92.4 0.5 collective-permute-start.18
  93.1 1.6 %collective-permute-start.25 = (bf16[2,80,768]{2,1,0:T(8,128)(2,1)S(1)}, bf16[2,80,768]{2,1,0:T(8,128)(2,1)S(1)}, u32[]{:S(2)}, u32[]{:S(2)}) collective-permute-start(bf16[2,80,768]{2,1,0:T(8,128)(2,1)S(1)} %get-tuple-element.186), channel_id=1, source_target_pairs={{0,16},{4,20},{8,24},{12,28},{16,0},{20,4},{24,8},{28,12},{1,17},{... | collective-permute-start | bytes 737288 | tf_op jit(solution)/shard_map/ppermute | solution.py:730
  94.6 1.3 %collective-permute-start.21 = (bf16[144,768]{1,0:T(8,128)(2,1)S(1)}, bf16[144,768]{1,0:T(8,128)(2,1)S(1)}, u32[]{:S(2)}, u32[]{:S(2)}) collective-permute-start(bf16[144,768]{1,0:T(8,128)(2,1)S(1)} %get-tuple-element.175), channel_id=1, source_target_pairs={{0,8},{4,12},{8,0},{12,4},{16,24},{20,28},{24,16},{28,20},{1,9},{5... | collective-permute-start | bytes 663560 | tf_op jit(solution)/shard_map/ppermute | solution.py:730
  96.0 0.7 collective-permute-start.24
  96.7 0.5 collective-permute-start.20
  97.2 0.4 collective-permute-done.14.other_ref
  97.6 0.5 collective-permute-start.19
  98.1 3.4 %collective-permute-done.19 = f32[8,768]{1,0:T(8,128)S(1)} collective-permute-done((f32[8,768]{1,0:T(8,128)S(1)}, f32[8,768]{1,0:T(8,128)S(1)}, u32[]{:S(2)}, u32[]{:S(2)}) %collective-permute-start.19) | collective-permute-done | bytes 24608 | tf_op jit(solution)/shard_map/ppermute | solution.py:730
  101.5 0.4 collective-permute-start.15
  101.9 2.0 %collective-permute-done.20.refs_1_ = bf16[112,768]{1,0:T(8,128)(2,1)S(1)} collective-permute-done((bf16[112,768]{1,0:T(8,128)(2,1)S(1)}, bf16[112,768]{1,0:T(8,128)(2,1)S(1)}, u32[]{:S(2)}, u32[]{:S(2)}) %collective-permute-start.20) | collective-permute-done | bytes 172064 | tf_op jit(solution)/shard_map/ppermute | solution.py:730
  103.9 0.8 collective-permute-start.22
  104.7 0.7 collective-permute-done.24.refs_1_
  105.5 0.9 collective-permute-start.26
  106.4 1.3 %collective-permute-start.27 = (bf16[80,768]{1,0:T(8,128)(2,1)S(1)}, bf16[80,768]{1,0:T(8,128)(2,1)S(1)}, u32[]{:S(2)}, u32[]{:S(2)}) collective-permute-start(bf16[80,768]{1,0:T(8,128)(2,1)S(1)} %get-tuple-element.190), channel_id=1, source_target_pairs={{0,8},{4,12},{8,0},{12,4},{16,24},{20,28},{24,16},{28,20},{1,9},{5... | collective-permute-start | bytes 368648 | tf_op jit(solution)/shard_map/ppermute | solution.py:730
  107.7 5.5 %collective-permute-done.22.refs_5_ = f32[8,768]{1,0:T(8,128)S(1)} collective-permute-done((f32[8,768]{1,0:T(8,128)S(1)}, f32[8,768]{1,0:T(8,128)S(1)}, u32[]{:S(2)}, u32[]{:S(2)}) %collective-permute-start.22) | collective-permute-done | bytes 24608 | tf_op jit(solution)/shard_map/ppermute | solution.py:730
  113.2 1.1 finish_inputs.1
  114.3 1.4 %finish_grads.1 = (f32[24,3072]{1,0:T(8,128)}, f32[96,768]{1,0:T(8,128)}, f32[96,384]{1,0:T(8,128)}, f32[1,96]{1,0:T(1,128)}, f32[3,96,384]{2,1,0:T(8,128)}, /*i...) custom-call(f32[112,768]{1,0:T(8,128)S(1)} %get-tuple-element.172.re, ...), custom_call_target="tpu_custom_call" | custom-call | flops 2000000000 | bytes 6000000 | tf_op jit(solution)/shard_map/finish_grads/pallas_call | solution.py:60
  (84 shorter events, 1.2 us)
Async XLA Ops:
  1.3 1.1 copy-start.4
  2.4 1.1 copy-start.12
  2.4 1.1 copy-start.13
  2.5 1.1 copy-start.14
  2.5 1.1 copy-start.15
  2.5 1.2 copy-start.16
  2.5 1.2 %copy-start.17 = (f32[768]{0:T(1024)S(1)}, f32[768]{0:T(1024)}, u32[]{:S(2)}) copy-start(f32[768]{0:T(1024)} %param.38) | copy-start | bytes 9220
  3.0 1.4 %collective-permute-start = (f32[8,768]{1,0:T(8,128)S(1)}, f32[8,768]{1,0:T(8,128)S(1)}, u32[]{:S(2)}, u32[]{:S(2)}) collective-permute-start(f32[8,768]{1,0:T(8,128)S(1)} %stats.1.refs_0_), channel_id=1, source_target_pairs={{0,4},{4,0},{8,12},{12,8},{16,20},{20,16},{24,28},{28,24},{1,5},{5... | collective-permute-start | bytes 73736 | tf_op jit(solution)/shard_map/ppermute | solution.py:730
  3.7 5.2 %copy-start.6 = (f32[3072]{0:T(1024)S(1)}, f32[3072]{0:T(1024)}, u32[]{:S(2)}) copy-start(f32[3072]{0:T(1024)} %param.32) | copy-start | bytes 36868
  3.7 5.2 %copy-start.7 = (s32[2,2,512]{2,1,0:T(2,128)S(1)}, s32[2,2,512]{2,1,0:T(2,128)}, u32[]{:S(2)}) copy-start(s32[2,2,512]{2,1,0:T(2,128)} %box_ref.1) | copy-start | bytes 24580
  3.7 5.2 %copy-start.8 = (s32[2,512]{1,0:T(2,128)S(1)}, s32[2,512]{1,0:T(2,128)}, u32[]{:S(2)}) copy-start(s32[2,512]{1,0:T(2,128)} %line_ref.1) | copy-start | bytes 12292
  3.7 5.2 %copy-start.9 = (f32[6,64]{1,0:T(8,128)S(1)}, f32[6,64]{1,0:T(8,128)}, u32[]{:S(2)}) copy-start(f32[6,64]{1,0:T(8,128)} %table_ref.1) | copy-start | bytes 4612
  4.4 8.2 %copy-start.1 = (bf16[768,3,384]{2,0,1:T(8,128)(2,1)S(1)}, bf16[768,3,384]{2,0,1:T(8,128)(2,1)}, u32[]{:S(2)}) copy-start(bf16[768,3,384]{2,0,1:T(8,128)(2,1)} %param.25) | copy-start | bytes 5308420
  4.4 8.2 %copy-start.2 = (bf16[512,768]{1,0:T(8,128)(2,1)S(1)}, bf16[512,768]{1,0:T(8,128)(2,1)}, u32[]{:S(2)}) copy-start(bf16[512,768]{1,0:T(8,128)(2,1)} %refs_0_.2) | copy-start | bytes 2359300
  4.4 8.2 %copy-start.5 = (bf16[512,768]{1,0:T(8,128)(2,1)S(1)}, bf16[512,768]{1,0:T(8,128)(2,1)}, u32[]{:S(2)}) copy-start(bf16[512,768]{1,0:T(8,128)(2,1)} %visual_ref.7) | copy-start | bytes 2359300
  4.4 5.7 %collective-permute-start.3 = (f32[8,768]{1,0:T(8,128)S(1)}, f32[8,768]{1,0:T(8,128)S(1)}, u32[]{:S(2)}, u32[]{:S(2)}) collective-permute-start(f32[8,768]{1,0:T(8,128)S(1)} %join_stats.1.refs_0_), channel_id=1, source_target_pairs={{0,24},{4,28},{8,16},{12,20},{16,8},{20,12},{24,0},{28,4},{1,25},{... | collective-permute-start | bytes 73736 | tf_op jit(solution)/shard_map/ppermute | solution.py:730
  8.3 3.8 %collective-permute-start.2 = (f32[8,768]{1,0:T(8,128)S(1)}, f32[8,768]{1,0:T(8,128)S(1)}, u32[]{:S(2)}, u32[]{:S(2)}) collective-permute-start(f32[8,768]{1,0:T(8,128)S(1)} %join_stats.1.refs_0_), channel_id=1, source_target_pairs={{0,16},{4,20},{8,24},{12,28},{16,0},{20,4},{24,8},{28,12},{1,17},{... | collective-permute-start | bytes 73736 | tf_op jit(solution)/shard_map/ppermute | solution.py:730
  8.8 3.8 %collective-permute-start.1 = (f32[8,768]{1,0:T(8,128)S(1)}, f32[8,768]{1,0:T(8,128)S(1)}, u32[]{:S(2)}, u32[]{:S(2)}) collective-permute-start(f32[8,768]{1,0:T(8,128)S(1)} %join_stats.1.refs_0_), channel_id=1, source_target_pairs={{0,8},{4,12},{8,0},{12,4},{16,24},{20,28},{24,16},{28,20},{1,9},{5... | collective-permute-start | bytes 73736 | tf_op jit(solution)/shard_map/ppermute | solution.py:730
  8.9 31.3 %slice-start = ((s8[4718592]{0:T(1024)(128)(4,1)}), s8[4194304]{0:T(1024)(128)(4,1)S(1)}, s32[]{:S(2)}) async-start(s8[4718592]{0:T(1024)(128)(4,1)} %bitcast.11), calls=%async_computation | async-start | bytes 8388608
  8.9 31.3 %slice-start.2 = ((s8[4718592]{0:T(1024)(128)(4,1)}), s8[4194304]{0:T(1024)(128)(4,1)S(1)}, s32[]{:S(2)}) async-start(s8[4718592]{0:T(1024)(128)(4,1)} %bitcast.13), calls=%async_computation.2 | async-start | bytes 8388608
  12.6 27.6 %slice-start.1 = ((s8[4718592]{0:T(1024)(128)(4,1)}), s8[524288]{0:T(1024)(128)(4,1)S(1)}, s32[]{:S(2)}) async-start(s8[4718592]{0:T(1024)(128)(4,1)} %bitcast.11), calls=%async_computation.1 | async-start | bytes 1048576
  12.6 27.6 %slice-start.3 = ((s8[4718592]{0:T(1024)(128)(4,1)}), s8[524288]{0:T(1024)(128)(4,1)S(1)}, s32[]{:S(2)}) async-start(s8[4718592]{0:T(1024)(128)(4,1)} %bitcast.13), calls=%async_computation.3 | async-start | bytes 1048576
  16.6 23.6 %collective-permute-start.6 = (bf16[384,256]{1,0:T(8,128)(2,1)S(1)}, bf16[384,256]{1,0:T(8,128)(2,1)S(1)}, u32[]{:S(2)}, u32[]{:S(2)}) collective-permute-start(bf16[384,256]{1,0:T(8,128)(2,1)S(1)} %get-tuple-element.115.refs_7_.refs_8_.refs_6_), channel_id=1, source_target_pairs={{0,3},{1,2},{2,1},{3,0},{4,7},{5,6},{6,5},{7,4},{8,11},{9,10},{10,... | collective-permute-start | bytes 589832 | tf_op jit(solution)/shard_map/ppermute | solution.py:730
  20.6 15.2 %collective-permute-start.5 = (bf16[384,256]{1,0:T(8,128)(2,1)S(1)}, bf16[384,256]{1,0:T(8,128)(2,1)S(1)}, u32[]{:S(2)}, u32[]{:S(2)}) collective-permute-start(bf16[384,256]{1,0:T(8,128)(2,1)S(1)} %get-tuple-element.115.refs_7_.refs_8_.refs_6_), channel_id=1, source_target_pairs={{0,2},{1,3},{2,0},{3,1},{4,6},{5,7},{6,4},{7,5},{8,10},{9,11},{10,... | collective-permute-start | bytes 589832 | tf_op jit(solution)/shard_map/ppermute | solution.py:730
  20.7 19.6 %collective-permute-start.4 = (bf16[384,256]{1,0:T(8,128)(2,1)S(1)}, bf16[384,256]{1,0:T(8,128)(2,1)S(1)}, u32[]{:S(2)}, u32[]{:S(2)}) collective-permute-start(bf16[384,256]{1,0:T(8,128)(2,1)S(1)} %get-tuple-element.115.refs_7_.refs_8_.refs_6_), channel_id=1, source_target_pairs={{0,1},{1,0},{2,3},{3,2},{4,5},{5,4},{6,7},{7,6},{8,9},{9,8},{10,11... | collective-permute-start | bytes 589832 | tf_op jit(solution)/shard_map/ppermute | solution.py:730
  21.3 19.0 %copy-start = (bf16[1536,768]{1,0:T(8,128)(2,1)S(1)}, bf16[1536,768]{1,0:T(8,128)(2,1)}, u32[]{:S(2)}) copy-start(bf16[1536,768]{1,0:T(8,128)(2,1)} %refs_2_.3) | copy-start | bytes 7077892
  21.3 19.0 %copy-start.3 = (bf16[512,768]{1,0:T(8,128)(2,1)S(1)}, bf16[512,768]{1,0:T(8,128)(2,1)}, u32[]{:S(2)}) copy-start(bf16[512,768]{1,0:T(8,128)(2,1)} %refs_1_.3) | copy-start | bytes 2359300
  35.8 14.8 %collective-permute-start.9 = (bf16[384,256]{1,0:T(8,128)(2,1)S(1)}, bf16[384,256]{1,0:T(8,128)(2,1)S(1)}, u32[]{:S(2)}, u32[]{:S(2)}) collective-permute-start(bf16[384,256]{1,0:T(8,128)(2,1)S(1)} %get-tuple-element.124.refs_7_.refs_9_), channel_id=1, source_target_pairs={{0,3},{1,2},{2,1},{3,0},{4,7},{5,6},{6,5},{7,4},{8,11},{9,10},{10,... | collective-permute-start | bytes 589832 | tf_op jit(solution)/shard_map/ppermute | solution.py:730
  39.0 14.8 %collective-permute-start.8 = (bf16[384,256]{1,0:T(8,128)(2,1)S(1)}, bf16[384,256]{1,0:T(8,128)(2,1)S(1)}, u32[]{:S(2)}, u32[]{:S(2)}) collective-permute-start(bf16[384,256]{1,0:T(8,128)(2,1)S(1)} %get-tuple-element.124.refs_7_.refs_9_), channel_id=1, source_target_pairs={{0,2},{1,3},{2,0},{3,1},{4,6},{5,7},{6,4},{7,5},{8,10},{9,11},{10,... | collective-permute-start | bytes 589832 | tf_op jit(solution)/shard_map/ppermute | solution.py:730
  39.0 14.8 %collective-permute-start.7 = (bf16[384,256]{1,0:T(8,128)(2,1)S(1)}, bf16[384,256]{1,0:T(8,128)(2,1)S(1)}, u32[]{:S(2)}, u32[]{:S(2)}) collective-permute-start(bf16[384,256]{1,0:T(8,128)(2,1)S(1)} %get-tuple-element.124.refs_7_.refs_9_), channel_id=1, source_target_pairs={{0,1},{1,0},{2,3},{3,2},{4,5},{5,4},{6,7},{7,6},{8,9},{9,8},{10,11... | collective-permute-start | bytes 589832 | tf_op jit(solution)/shard_map/ppermute | solution.py:730
  68.3 4.4 %collective-permute-start.11 = (bf16[4,144,768]{2,1,0:T(8,128)(2,1)S(1)}, bf16[4,144,768]{2,1,0:T(8,128)(2,1)S(1)}, u32[]{:S(2)}, u32[]{:S(2)}) collective-permute-start(bf16[4,144,768]{2,1,0:T(8,128)(2,1)S(1)} %get-tuple-element.146), channel_id=1, source_target_pairs={{0,4},{4,0},{8,12},{12,8},{16,20},{20,16},{24,28},{28,24},{1,5},{5... | collective-permute-start | bytes 2654216 | tf_op jit(solution)/shard_map/ppermute | solution.py:730
  68.3 3.4 %collective-permute-start.10 = (bf16[4,112,768]{2,1,0:T(8,128)(2,1)S(1)}, bf16[4,112,768]{2,1,0:T(8,128)(2,1)S(1)}, u32[]{:S(2)}, u32[]{:S(2)}) collective-permute-start(bf16[4,112,768]{2,1,0:T(8,128)(2,1)S(1)} %get-tuple-element.129), channel_id=1, source_target_pairs={{0,4},{4,0},{8,12},{12,8},{16,20},{20,16},{24,28},{28,24},{1,5},{5... | collective-permute-start | bytes 2064392 | tf_op jit(solution)/shard_map/ppermute | solution.py:730
  71.8 14.1 %collective-permute-start.12 = (bf16[2,112,768]{2,1,0:T(8,128)(2,1)S(1)}, bf16[2,112,768]{2,1,0:T(8,128)(2,1)S(1)}, u32[]{:S(2)}, u32[]{:S(2)}) collective-permute-start(bf16[2,112,768]{2,1,0:T(8,128)(2,1)S(1)} %get-tuple-element.162), channel_id=1, source_target_pairs={{0,8},{4,12},{8,0},{12,4},{16,24},{20,28},{24,16},{28,20},{1,9},{5... | collective-permute-start | bytes 1032200 | tf_op jit(solution)/shard_map/ppermute | solution.py:730
  72.9 13.1 %collective-permute-start.13 = (bf16[2,144,768]{2,1,0:T(8,128)(2,1)S(1)}, bf16[2,144,768]{2,1,0:T(8,128)(2,1)S(1)}, u32[]{:S(2)}, u32[]{:S(2)}) collective-permute-start(bf16[2,144,768]{2,1,0:T(8,128)(2,1)S(1)} %get-tuple-element.163), channel_id=1, source_target_pairs={{0,16},{4,20},{8,24},{12,28},{16,0},{20,4},{24,8},{28,12},{1,17},{... | collective-permute-start | bytes 1327112 | tf_op jit(solution)/shard_map/ppermute | solution.py:730
  86.0 6.9 %collective-permute-start.23 = (bf16[4,152,768]{2,1,0:T(8,128)(2,1)S(1)}, bf16[4,152,768]{2,1,0:T(8,128)(2,1)S(1)}, u32[]{:S(2)}, u32[]{:S(2)}) collective-permute-start(bf16[4,152,768]{2,1,0:T(8,128)(2,1)S(1)} %get-tuple-element.180), channel_id=1, source_target_pairs={{0,4},{4,0},{8,12},{12,8},{16,20},{20,16},{24,28},{28,24},{1,5},{5... | collective-permute-start | bytes 2801672 | tf_op jit(solution)/shard_map/ppermute | solution.py:730
  86.0 11.5 %collective-permute-start.14 = (bf16[2,128,768]{2,1,0:T(8,128)(2,1)S(1)}, bf16[2,128,768]{2,1,0:T(8,128)(2,1)S(1)}, u32[]{:S(2)}, u32[]{:S(2)}) collective-permute-start(bf16[2,128,768]{2,1,0:T(8,128)(2,1)S(1)} %get-tuple-element.164), channel_id=1, source_target_pairs={{0,1},{1,0},{2,3},{3,2},{4,5},{5,4},{6,7},{7,6},{8,9},{9,8},{10,11... | collective-permute-start | bytes 1179656 | tf_op jit(solution)/shard_map/ppermute | solution.py:730
  86.1 2.4 %collective-permute-start.16 = (f32[8,768]{1,0:T(8,128)S(1)}, f32[8,768]{1,0:T(8,128)S(1)}, u32[]{:S(2)}, u32[]{:S(2)}) collective-permute-start(f32[8,768]{1,0:T(8,128)S(1)} %get-tuple-element.167), channel_id=1, source_target_pairs={{0,4},{4,0},{8,12},{12,8},{16,20},{20,16},{24,28},{28,24},{1,5},{5... | collective-permute-start | bytes 73736 | tf_op jit(solution)/shard_map/ppermute | solution.py:730
  88.6 3.8 %collective-permute-start.17 = (f32[8,768]{1,0:T(8,128)S(1)}, f32[8,768]{1,0:T(8,128)S(1)}, u32[]{:S(2)}, u32[]{:S(2)}) collective-permute-start(f32[8,768]{1,0:T(8,128)S(1)} %add.12), channel_id=1, source_target_pairs={{0,8},{4,12},{8,0},{12,4},{16,24},{20,28},{24,16},{28,20},{1,9},{5... | collective-permute-start | bytes 73736 | tf_op jit(solution)/shard_map/ppermute | solution.py:730
  92.4 4.3 %collective-permute-start.18 = (f32[8,768]{1,0:T(8,128)S(1)}, f32[8,768]{1,0:T(8,128)S(1)}, u32[]{:S(2)}, u32[]{:S(2)}) collective-permute-start(f32[8,768]{1,0:T(8,128)S(1)} %add.13), channel_id=1, source_target_pairs={{0,16},{4,20},{8,24},{12,28},{16,0},{20,4},{24,8},{28,12},{1,17},{... | collective-permute-start | bytes 73736 | tf_op jit(solution)/shard_map/ppermute | solution.py:730
  93.1 12.4 %collective-permute-start.25 = (bf16[2,80,768]{2,1,0:T(8,128)(2,1)S(1)}, bf16[2,80,768]{2,1,0:T(8,128)(2,1)S(1)}, u32[]{:S(2)}, u32[]{:S(2)}) collective-permute-start(bf16[2,80,768]{2,1,0:T(8,128)(2,1)S(1)} %get-tuple-element.186), channel_id=1, source_target_pairs={{0,16},{4,20},{8,24},{12,28},{16,0},{20,4},{24,8},{28,12},{1,17},{... | collective-permute-start | bytes 737288 | tf_op jit(solution)/shard_map/ppermute | solution.py:730
  94.6 9.3 %collective-permute-start.21 = (bf16[144,768]{1,0:T(8,128)(2,1)S(1)}, bf16[144,768]{1,0:T(8,128)(2,1)S(1)}, u32[]{:S(2)}, u32[]{:S(2)}) collective-permute-start(bf16[144,768]{1,0:T(8,128)(2,1)S(1)} %get-tuple-element.175), channel_id=1, source_target_pairs={{0,8},{4,12},{8,0},{12,4},{16,24},{20,28},{24,16},{28,20},{1,9},{5... | collective-permute-start | bytes 663560 | tf_op jit(solution)/shard_map/ppermute | solution.py:730
  96.0 9.4 %collective-permute-start.24 = (bf16[2,72,768]{2,1,0:T(8,128)(2,1)S(1)}, bf16[2,72,768]{2,1,0:T(8,128)(2,1)S(1)}, u32[]{:S(2)}, u32[]{:S(2)}) collective-permute-start(bf16[2,72,768]{2,1,0:T(8,128)(2,1)S(1)} %get-tuple-element.183), channel_id=1, source_target_pairs={{0,8},{4,12},{8,0},{12,4},{16,24},{20,28},{24,16},{28,20},{1,9},{5... | collective-permute-start | bytes 663560 | tf_op jit(solution)/shard_map/ppermute | solution.py:730
  96.7 7.3 %collective-permute-start.20 = (bf16[112,768]{1,0:T(8,128)(2,1)S(1)}, bf16[112,768]{1,0:T(8,128)(2,1)S(1)}, u32[]{:S(2)}, u32[]{:S(2)}) collective-permute-start(bf16[112,768]{1,0:T(8,128)(2,1)S(1)} %get-tuple-element.173), channel_id=1, source_target_pairs={{0,16},{4,20},{8,24},{12,28},{16,0},{20,4},{24,8},{28,12},{1,17},{... | collective-permute-start | bytes 516104 | tf_op jit(solution)/shard_map/ppermute | solution.py:730
  97.6 3.9 %collective-permute-start.19 = (f32[8,768]{1,0:T(8,128)S(1)}, f32[8,768]{1,0:T(8,128)S(1)}, u32[]{:S(2)}, u32[]{:S(2)}) collective-permute-start(f32[8,768]{1,0:T(8,128)S(1)} %add.14), channel_id=1, source_target_pairs={{0,1},{1,0},{2,3},{3,2},{4,5},{5,4},{6,7},{7,6},{8,9},{9,8},{10,11... | collective-permute-start | bytes 73736 | tf_op jit(solution)/shard_map/ppermute | solution.py:730
  101.5 11.7 %collective-permute-start.15 = (bf16[128,768]{1,0:T(8,128)(2,1)S(1)}, bf16[128,768]{1,0:T(8,128)(2,1)S(1)}, u32[]{:S(2)}, u32[]{:S(2)}) collective-permute-start(bf16[128,768]{1,0:T(8,128)(2,1)S(1)} %get-tuple-element.166), channel_id=1, source_target_pairs={{0,2},{1,3},{2,0},{3,1},{4,6},{5,7},{6,4},{7,5},{8,10},{9,11},{10,... | collective-permute-start | bytes 589832 | tf_op jit(solution)/shard_map/ppermute | solution.py:730
  103.9 9.3 %collective-permute-start.22 = (f32[8,768]{1,0:T(8,128)S(1)}, f32[8,768]{1,0:T(8,128)S(1)}, u32[]{:S(2)}, u32[]{:S(2)}) collective-permute-start(f32[8,768]{1,0:T(8,128)S(1)} %add.15.refs_4_), channel_id=1, source_target_pairs={{0,2},{1,3},{2,0},{3,1},{4,6},{5,7},{6,4},{7,5},{8,10},{9,11},{10,... | collective-permute-start | bytes 73736 | tf_op jit(solution)/shard_map/ppermute | solution.py:730
  105.5 8.8 %collective-permute-start.26 = (bf16[72,768]{1,0:T(8,128)(2,1)S(1)}, bf16[72,768]{1,0:T(8,128)(2,1)S(1)}, u32[]{:S(2)}, u32[]{:S(2)}) collective-permute-start(bf16[72,768]{1,0:T(8,128)(2,1)S(1)} %get-tuple-element.188), channel_id=1, source_target_pairs={{0,16},{4,20},{8,24},{12,28},{16,0},{20,4},{24,8},{28,12},{1,17},{... | collective-permute-start | bytes 331784 | tf_op jit(solution)/shard_map/ppermute | solution.py:730
  106.4 7.9 %collective-permute-start.27 = (bf16[80,768]{1,0:T(8,128)(2,1)S(1)}, bf16[80,768]{1,0:T(8,128)(2,1)S(1)}, u32[]{:S(2)}, u32[]{:S(2)}) collective-permute-start(bf16[80,768]{1,0:T(8,128)(2,1)S(1)} %get-tuple-element.190), channel_id=1, source_target_pairs={{0,8},{4,12},{8,0},{12,4},{16,24},{20,28},{24,16},{28,20},{1,9},{5... | collective-permute-start | bytes 368648 | tf_op jit(solution)/shard_map/ppermute | solution.py:730
  (2 other events, 2.2 us)

commit v3 on v2

--- a/solution.py
+++ b/solution.py
@@ -927,7 +927,7 @@
             scratch=[pltpu.VMEM((width, local_width), F32)],
             final=(0,),
         )
-        other_out = swap(sib_out, "dp", 1)
+        other_out = swap(after(sib_out, other), "dp", 1)
         ffn_stages = across_chips(mine, other, [X_FIRST], [in_rows], "join_cores_in")
         ffn_stages += across_chips(mine_out, other_out, [Y_FIRST], [out_rows], "join_cores_out")
     inner = [q, k, v, kt, one, back, *heads, *dheads, *dheads_t, prob_one, prob_two]

time: 116 us -> 114 us (0.983)
  waiting for transfers between devices: 38.5 us -> 37.1 us
    ppermute x28, waiting for transfers between devices: 38.5 us -> 37.1 us  [swap(): return lax.ppermute(value, axis, [(i, i ^ mask) for i in range(size)])]
  transfers between devices with their start and end apart: 28 -> 28, of which waited for: 14 -> 13; matrix products, arithmetic and copies ran while one was open for 0% -> 0% of each run, Pallas kernels for 23% -> 26%
where the time goes in v3:
time: 114 us
  Pallas kernels  46.8 us (41%)
  waiting for transfers between devices  37.1 us (33%)
  starting transfers between devices  27.2 us (24%)
  between operations  1.84 us (2%)
  local copies, waits for them, and re-layouts  1.27 us (1%)
    pallas_call x18, Pallas kernels, call(): pl.pallas_call(kernel, out_shape=tuple((jax.ShapeDtypeStruct(*entry) if p...  46.8 us
    ppermute x28, waiting for transfers between devices, swap(): return lax.ppermute(value, axis, [(i, i ^ mask) for i in range(size)])  37.1 us
    ppermute x28, starting transfers between devices, swap(): return lax.ppermute(value, axis, [(i, i ^ mask) for i in range(size)])  27.2 us
  transfers between devices with their start and end apart: 28, of which 13 were waited for; matrix products, arithmetic and copies ran while one was open for 0% of the time, Pallas kernels for 26%

profile of v3, /device:TPU:0, one launch (start us, length us, event | category | flops | bytes accessed | tf_op | source)
XLA Modules:
  0.0 114.1 jit_solution(1163422839103865235)
XLA Ops:
  1.3 1.1 copy-done.4
  2.5 0.5 stats.1.refs_0_
  3.0 0.5 collective-permute-start
  3.7 0.6 collective-permute-done.refs_1_
  4.4 3.9 %collective-permute-start.3 = (f32[8,768]{1,0:T(8,128)S(1)}, f32[8,768]{1,0:T(8,128)S(1)}, u32[]{:S(2)}, u32[]{:S(2)}) collective-permute-start(f32[8,768]{1,0:T(8,128)S(1)} %join_stats.1.refs_0_), channel_id=1, source_target_pairs={{0,24},{4,28},{8,16},{12,20},{16,8},{20,12},{24,0},{28,4},{1,25},{... | collective-permute-start | bytes 73736 | tf_op jit(solution)/shard_map/ppermute | solution.py:730
  8.3 0.5 collective-permute-start.2
  8.9 0.3 prep.1
  9.2 0.8 collective-permute-done.3.refs_3_
  10.1 2.0 %collective-permute-done.2.refs_2_ = f32[8,768]{1,0:T(8,128)S(1)} collective-permute-done((f32[8,768]{1,0:T(8,128)S(1)}, f32[8,768]{1,0:T(8,128)S(1)}, u32[]{:S(2)}, u32[]{:S(2)}) %collective-permute-start.2) | collective-permute-done | bytes 24608 | tf_op jit(solution)/shard_map/ppermute | solution.py:730
  12.1 0.5 collective-permute-done.1.refs_1_
  12.6 4.0 %attend_first.1 = (f32[8,768]{1,0:T(8,128)S(1)}, bf16[512,768]{1,0:T(8,128)(2,1)S(1)}, bf16[512,384]{1,0:T(8,128)(2,1)S(1)}, bf16[512,384]{1,0:T(8,128)(2,1)S(1)...) custom-call(s32[1]{0:T(128)S(6)} %copy.37.count_ref, ...), custom_call_target="tpu_custom_call" | custom-call | flops 6000000000 | bytes 18000000 | tf_op jit(solution)/shard_map/attend_first/pallas_call | solution.py:60
  16.6 4.0 %collective-permute-start.6 = (bf16[384,256]{1,0:T(8,128)(2,1)S(1)}, bf16[384,256]{1,0:T(8,128)(2,1)S(1)}, u32[]{:S(2)}, u32[]{:S(2)}) collective-permute-start(bf16[384,256]{1,0:T(8,128)(2,1)S(1)} %get-tuple-element.116.refs_7_.refs_8_.refs_6_), channel_id=1, source_target_pairs={{0,3},{1,2},{2,1},{3,0},{4,7},{5,6},{6,5},{7,4},{8,11},{9,10},{10,... | collective-permute-start | bytes 589832 | tf_op jit(solution)/shard_map/ppermute | solution.py:730
  20.6 0.6 collective-permute-start.4
  21.3 2.6 %attend_second.1 = (bf16[384,256]{1,0:T(8,128)(2,1)S(1)}, bf16[6,512,256]{2,1,0:T(8,128)(2,1)S(1)}) custom-call(s32[1]{0:T(128)S(6)} %copy.37.count_ref, bf16[512,384]{1,0:T(8,128)(2,1)S(1)} %get-tuple-element.150.q_ref.refs_0_, bf16[512,384]{1,0:T(8,128)(2,1)S(1)} %get-tuple-element.122.k_ref.refs_1_, bf16[384,512]{1,0:T(8,128)(2,1)S(1)} %get-tuple-element.123.vt_ref, ...), custom_call_target="tpu_custom_call" | custom-call | flops 3000000000 | bytes 9000000 | tf_op jit(solution)/shard_map/attend_second/pallas_call | solution.py:60
  23.9 11.9 %collective-permute-done.5.refs_9_ = bf16[384,256]{1,0:T(8,128)(2,1)S(1)} collective-permute-done((bf16[384,256]{1,0:T(8,128)(2,1)S(1)}, bf16[384,256]{1,0:T(8,128)(2,1)S(1)}, u32[]{:S(2)}, u32[]{:S(2)}) %collective-permute-start.5) | collective-permute-done | bytes 196640 | tf_op jit(solution)/shard_map/ppermute | solution.py:730
  35.8 3.2 %collective-permute-start.9 = (bf16[384,256]{1,0:T(8,128)(2,1)S(1)}, bf16[384,256]{1,0:T(8,128)(2,1)S(1)}, u32[]{:S(2)}, u32[]{:S(2)}) collective-permute-start(bf16[384,256]{1,0:T(8,128)(2,1)S(1)} %get-tuple-element.125.refs_7_.refs_9_), channel_id=1, source_target_pairs={{0,3},{1,2},{2,1},{3,0},{4,7},{5,6},{6,5},{7,4},{8,11},{9,10},{10,... | collective-permute-start | bytes 589832 | tf_op jit(solution)/shard_map/ppermute | solution.py:730
  39.0 1.2 %collective-permute-start.7 = (bf16[384,256]{1,0:T(8,128)(2,1)S(1)}, bf16[384,256]{1,0:T(8,128)(2,1)S(1)}, u32[]{:S(2)}, u32[]{:S(2)}) collective-permute-start(bf16[384,256]{1,0:T(8,128)(2,1)S(1)} %get-tuple-element.125.refs_7_.refs_9_), channel_id=1, source_target_pairs={{0,1},{1,0},{2,3},{3,2},{4,5},{5,4},{6,7},{7,6},{8,9},{9,8},{10,11... | collective-permute-start | bytes 589832 | tf_op jit(solution)/shard_map/ppermute | solution.py:730
  40.3 10.3 %ffn_0.1 = (bf16[256,768]{1,0:T(8,128)(2,1)S(1)}, f32[128,768]{1,0:T(8,128)S(1)}, bf16[256,3072]{1,0:T(8,128)(2,1)S(1)}, bf16[256,3072]{1,0:T(8,128)(2,1)S(1)}, ...) custom-call(bf16[512,768]{1,0:T(8,128)(2,1)S(1)} %copy-done.2, ...), custom_call_target="tpu_custom_call" | custom-call | flops 8999999488 | bytes 27000000 | tf_op jit(solution)/shard_map/ffn_0/pallas_call | solution.py:60
  50.6 3.3 %collective-permute-done.8.refs_9_ = bf16[384,256]{1,0:T(8,128)(2,1)S(1)} collective-permute-done((bf16[384,256]{1,0:T(8,128)(2,1)S(1)}, bf16[384,256]{1,0:T(8,128)(2,1)S(1)}, u32[]{:S(2)}, u32[]{:S(2)}) %collective-permute-start.8) | collective-permute-done | bytes 196640 | tf_op jit(solution)/shard_map/ppermute | solution.py:730
  53.9 10.3 %ffn_1.1 = (bf16[256,768]{1,0:T(8,128)(2,1)S(1)}, f32[128,768]{1,0:T(8,128)S(1)}, bf16[256,3072]{1,0:T(8,128)(2,1)S(1)}, bf16[256,3072]{1,0:T(8,128)(2,1)S(1)}, ...) custom-call(bf16[512,768]{1,0:T(8,128)(2,1)S(1)} %copy-done.2, ...), custom_call_target="tpu_custom_call" | custom-call | flops 8999999488 | bytes 27000000 | tf_op jit(solution)/shard_map/ffn_1/pallas_call | solution.py:60
  64.2 1.1 weight_grad_in.1
  65.4 3.0 %weight_grad_out.1 = (bf16[512,768]{1,0:T(8,128)(2,1)}, f32[4,144,768]{2,1,0:T(8,128)S(1)}, bf16[4,144,768]{2,1,0:T(8,128)(2,1)S(1)}) custom-call(bf16[256,768]{1,0:T(8,128)(2,1)S(1)} %get-tuple-element.131.refs_0_, bf16[256,768]{1,0:T(8,128)(2,1)S(1)} %get-tuple-element.132.refs_1_, bf16[256,3072]{1,0:T(8,128)(2,1)S(1)} %get-tuple-element.133.refs_2_, ...), custom_call_target="tpu_custom_call" | custom-call | flops 3000000000 | bytes 9000000 | tf_op jit(solution)/shard_map/weight_grad_out/pallas_call | solution.py:60
  68.4 0.5 collective-permute-start.11
  69.0 0.9 collective-permute-start.12
  69.9 1.0 collective-permute-done.11.refs_1_
  71.1 1.7 %collective-permute-start.13 = (bf16[2,144,768]{2,1,0:T(8,128)(2,1)S(1)}, bf16[2,144,768]{2,1,0:T(8,128)(2,1)S(1)}, u32[]{:S(2)}, u32[]{:S(2)}) collective-permute-start(bf16[2,144,768]{2,1,0:T(8,128)(2,1)S(1)} %get-tuple-element.165), channel_id=1, source_target_pairs={{0,16},{4,20},{8,24},{12,28},{16,0},{20,4},{24,8},{28,12},{1,17},{... | collective-permute-start | bytes 1327112 | tf_op jit(solution)/shard_map/ppermute | solution.py:730
  72.8 11.5 %back.1 = (f32[8,768]{1,0:T(8,128)S(1)}, f32[2,128,768]{2,1,0:T(8,128)S(1)}, bf16[2,128,768]{2,1,0:T(8,128)(2,1)S(1)}, f32[4,152,768]{2,1,0:T(8,128)S(1)}, bf16[4,152,768]{2,1,0:T(8,128)(2,1)S(1)}) custom-call(s32[1]{0:T(128)S(6)} %copy.37.count_ref, bf16[3,768,384]{2,1,0:T(8,128)(2,1)S(1)} %bitcast.16, bf16[512,768]{1,0:T(8,128)(2,1)S(1)} %copy-done.5, ...), custom_call_target="tpu_custom_call" | custom-call | flops 12000000000 | bytes 36000000 | tf_op jit(solution)/shard_map/back/pallas_call | solution.py:60
  84.5 0.4 collective-permute-start.16
  84.9 2.0 %collective-permute-done.16 = f32[8,768]{1,0:T(8,128)S(1)} collective-permute-done((f32[8,768]{1,0:T(8,128)S(1)}, f32[8,768]{1,0:T(8,128)S(1)}, u32[]{:S(2)}, u32[]{:S(2)}) %collective-permute-start.16) | collective-permute-done | bytes 24608 | tf_op jit(solution)/shard_map/ppermute | solution.py:730
  86.9 0.7 collective-permute-start.17
  87.7 3.0 %collective-permute-done.17 = f32[8,768]{1,0:T(8,128)S(1)} collective-permute-done((f32[8,768]{1,0:T(8,128)S(1)}, f32[8,768]{1,0:T(8,128)S(1)}, u32[]{:S(2)}, u32[]{:S(2)}) %collective-permute-start.17) | collective-permute-done | bytes 24608 | tf_op jit(solution)/shard_map/ppermute | solution.py:730
  90.7 0.9 collective-permute-start.18
  91.6 0.2 join_cores_qkv.1
  91.7 1.2 %collective-permute-start.25 = (bf16[2,80,768]{2,1,0:T(8,128)(2,1)S(1)}, bf16[2,80,768]{2,1,0:T(8,128)(2,1)S(1)}, u32[]{:S(2)}, u32[]{:S(2)}) collective-permute-start(bf16[2,80,768]{2,1,0:T(8,128)(2,1)S(1)} %get-tuple-element.188), channel_id=1, source_target_pairs={{0,16},{4,20},{8,24},{12,28},{16,0},{20,4},{24,8},{28,12},{1,17},{... | collective-permute-start | bytes 737288 | tf_op jit(solution)/shard_map/ppermute | solution.py:730
  93.0 0.7 collective-permute-start.21
  93.7 1.4 %collective-permute-start.24 = (bf16[2,72,768]{2,1,0:T(8,128)(2,1)S(1)}, bf16[2,72,768]{2,1,0:T(8,128)(2,1)S(1)}, u32[]{:S(2)}, u32[]{:S(2)}) collective-permute-start(bf16[2,72,768]{2,1,0:T(8,128)(2,1)S(1)} %get-tuple-element.185), channel_id=1, source_target_pairs={{0,8},{4,12},{8,0},{12,4},{16,24},{20,28},{24,16},{28,20},{1,9},{5... | collective-permute-start | bytes 663560 | tf_op jit(solution)/shard_map/ppermute | solution.py:730
  95.0 0.9 collective-permute-start.20
  96.0 0.7 collective-permute-start.19
  96.7 3.2 %collective-permute-done.19 = f32[8,768]{1,0:T(8,128)S(1)} collective-permute-done((f32[8,768]{1,0:T(8,128)S(1)}, f32[8,768]{1,0:T(8,128)S(1)}, u32[]{:S(2)}, u32[]{:S(2)}) %collective-permute-start.19) | collective-permute-done | bytes 24608 | tf_op jit(solution)/shard_map/ppermute | solution.py:730
  99.9 0.6 collective-permute-start.15
  100.5 2.1 %collective-permute-done.20.refs_1_ = bf16[112,768]{1,0:T(8,128)(2,1)S(1)} collective-permute-done((bf16[112,768]{1,0:T(8,128)(2,1)S(1)}, bf16[112,768]{1,0:T(8,128)(2,1)S(1)}, u32[]{:S(2)}, u32[]{:S(2)}) %collective-permute-start.20) | collective-permute-done | bytes 172064 | tf_op jit(solution)/shard_map/ppermute | solution.py:730
  102.6 0.8 collective-permute-start.22
  103.4 0.4 collective-permute-done.24.refs_1_
  103.9 0.9 collective-permute-start.26
  104.8 0.7 collective-permute-start.27
  105.5 6.1 %collective-permute-done.22.refs_5_ = f32[8,768]{1,0:T(8,128)S(1)} collective-permute-done((f32[8,768]{1,0:T(8,128)S(1)}, f32[8,768]{1,0:T(8,128)S(1)}, u32[]{:S(2)}, u32[]{:S(2)}) %collective-permute-start.22) | collective-permute-done | bytes 24608 | tf_op jit(solution)/shard_map/ppermute | solution.py:730
  111.6 1.1 finish_inputs.1
  112.7 1.4 %finish_grads.1 = (f32[24,3072]{1,0:T(8,128)}, f32[96,768]{1,0:T(8,128)}, f32[96,384]{1,0:T(8,128)}, f32[1,96]{1,0:T(1,128)}, f32[3,96,384]{2,1,0:T(8,128)}, /*i...) custom-call(f32[112,768]{1,0:T(8,128)S(1)} %get-tuple-element.174.re, ...), custom_call_target="tpu_custom_call" | custom-call | flops 2000000000 | bytes 6000000 | tf_op jit(solution)/shard_map/finish_grads/pallas_call | solution.py:60
  (84 shorter events, 1.2 us)
Async XLA Ops:
  1.3 1.1 copy-start.4
  2.4 1.1 copy-start.12
  2.4 1.1 copy-start.13
  2.5 1.1 copy-start.14
  2.5 1.1 %copy-start.15 = (f32[768]{0:T(1024)S(1)}, f32[768]{0:T(1024)}, u32[]{:S(2)}) copy-start(f32[768]{0:T(1024)} %param.36) | copy-start | bytes 9220
  2.5 1.2 %copy-start.16 = (f32[768]{0:T(1024)S(1)}, f32[768]{0:T(1024)}, u32[]{:S(2)}) copy-start(f32[768]{0:T(1024)} %param.37) | copy-start | bytes 9220
  2.5 1.2 %copy-start.17 = (f32[768]{0:T(1024)S(1)}, f32[768]{0:T(1024)}, u32[]{:S(2)}) copy-start(f32[768]{0:T(1024)} %param.38) | copy-start | bytes 9220
  3.0 1.4 %collective-permute-start = (f32[8,768]{1,0:T(8,128)S(1)}, f32[8,768]{1,0:T(8,128)S(1)}, u32[]{:S(2)}, u32[]{:S(2)}) collective-permute-start(f32[8,768]{1,0:T(8,128)S(1)} %stats.1.refs_0_), channel_id=1, source_target_pairs={{0,4},{4,0},{8,12},{12,8},{16,20},{20,16},{24,28},{28,24},{1,5},{5... | collective-permute-start | bytes 73736 | tf_op jit(solution)/shard_map/ppermute | solution.py:730
  3.7 5.2 %copy-start.6 = (f32[3072]{0:T(1024)S(1)}, f32[3072]{0:T(1024)}, u32[]{:S(2)}) copy-start(f32[3072]{0:T(1024)} %param.32) | copy-start | bytes 36868
  3.7 5.2 %copy-start.7 = (s32[2,2,512]{2,1,0:T(2,128)S(1)}, s32[2,2,512]{2,1,0:T(2,128)}, u32[]{:S(2)}) copy-start(s32[2,2,512]{2,1,0:T(2,128)} %box_ref.1) | copy-start | bytes 24580
  3.7 5.2 %copy-start.8 = (s32[2,512]{1,0:T(2,128)S(1)}, s32[2,512]{1,0:T(2,128)}, u32[]{:S(2)}) copy-start(s32[2,512]{1,0:T(2,128)} %line_ref.1) | copy-start | bytes 12292
  3.7 5.2 %copy-start.9 = (f32[6,64]{1,0:T(8,128)S(1)}, f32[6,64]{1,0:T(8,128)}, u32[]{:S(2)}) copy-start(f32[6,64]{1,0:T(8,128)} %table_ref.1) | copy-start | bytes 4612
  4.4 8.2 %copy-start.1 = (bf16[768,3,384]{2,0,1:T(8,128)(2,1)S(1)}, bf16[768,3,384]{2,0,1:T(8,128)(2,1)}, u32[]{:S(2)}) copy-start(bf16[768,3,384]{2,0,1:T(8,128)(2,1)} %param.25) | copy-start | bytes 5308420
  4.4 8.2 %copy-start.2 = (bf16[512,768]{1,0:T(8,128)(2,1)S(1)}, bf16[512,768]{1,0:T(8,128)(2,1)}, u32[]{:S(2)}) copy-start(bf16[512,768]{1,0:T(8,128)(2,1)} %refs_0_.2) | copy-start | bytes 2359300
  4.4 8.2 %copy-start.5 = (bf16[512,768]{1,0:T(8,128)(2,1)S(1)}, bf16[512,768]{1,0:T(8,128)(2,1)}, u32[]{:S(2)}) copy-start(bf16[512,768]{1,0:T(8,128)(2,1)} %visual_ref.7) | copy-start | bytes 2359300
  4.4 5.7 %collective-permute-start.3 = (f32[8,768]{1,0:T(8,128)S(1)}, f32[8,768]{1,0:T(8,128)S(1)}, u32[]{:S(2)}, u32[]{:S(2)}) collective-permute-start(f32[8,768]{1,0:T(8,128)S(1)} %join_stats.1.refs_0_), channel_id=1, source_target_pairs={{0,24},{4,28},{8,16},{12,20},{16,8},{20,12},{24,0},{28,4},{1,25},{... | collective-permute-start | bytes 73736 | tf_op jit(solution)/shard_map/ppermute | solution.py:730
  8.3 3.8 %collective-permute-start.2 = (f32[8,768]{1,0:T(8,128)S(1)}, f32[8,768]{1,0:T(8,128)S(1)}, u32[]{:S(2)}, u32[]{:S(2)}) collective-permute-start(f32[8,768]{1,0:T(8,128)S(1)} %join_stats.1.refs_0_), channel_id=1, source_target_pairs={{0,16},{4,20},{8,24},{12,28},{16,0},{20,4},{24,8},{28,12},{1,17},{... | collective-permute-start | bytes 73736 | tf_op jit(solution)/shard_map/ppermute | solution.py:730
  8.8 3.8 %collective-permute-start.1 = (f32[8,768]{1,0:T(8,128)S(1)}, f32[8,768]{1,0:T(8,128)S(1)}, u32[]{:S(2)}, u32[]{:S(2)}) collective-permute-start(f32[8,768]{1,0:T(8,128)S(1)} %join_stats.1.refs_0_), channel_id=1, source_target_pairs={{0,8},{4,12},{8,0},{12,4},{16,24},{20,28},{24,16},{28,20},{1,9},{5... | collective-permute-start | bytes 73736 | tf_op jit(solution)/shard_map/ppermute | solution.py:730
  8.9 31.3 %slice-start = ((s8[4718592]{0:T(1024)(128)(4,1)}), s8[4194304]{0:T(1024)(128)(4,1)S(1)}, s32[]{:S(2)}) async-start(s8[4718592]{0:T(1024)(128)(4,1)} %bitcast.11), calls=%async_computation | async-start | bytes 8388608
  8.9 31.3 %slice-start.2 = ((s8[4718592]{0:T(1024)(128)(4,1)}), s8[4194304]{0:T(1024)(128)(4,1)S(1)}, s32[]{:S(2)}) async-start(s8[4718592]{0:T(1024)(128)(4,1)} %bitcast.13), calls=%async_computation.2 | async-start | bytes 8388608
  12.6 27.6 %slice-start.1 = ((s8[4718592]{0:T(1024)(128)(4,1)}), s8[524288]{0:T(1024)(128)(4,1)S(1)}, s32[]{:S(2)}) async-start(s8[4718592]{0:T(1024)(128)(4,1)} %bitcast.11), calls=%async_computation.1 | async-start | bytes 1048576
  12.6 27.6 %slice-start.3 = ((s8[4718592]{0:T(1024)(128)(4,1)}), s8[524288]{0:T(1024)(128)(4,1)S(1)}, s32[]{:S(2)}) async-start(s8[4718592]{0:T(1024)(128)(4,1)} %bitcast.13), calls=%async_computation.3 | async-start | bytes 1048576
  16.6 23.6 %collective-permute-start.6 = (bf16[384,256]{1,0:T(8,128)(2,1)S(1)}, bf16[384,256]{1,0:T(8,128)(2,1)S(1)}, u32[]{:S(2)}, u32[]{:S(2)}) collective-permute-start(bf16[384,256]{1,0:T(8,128)(2,1)S(1)} %get-tuple-element.116.refs_7_.refs_8_.refs_6_), channel_id=1, source_target_pairs={{0,3},{1,2},{2,1},{3,0},{4,7},{5,6},{6,5},{7,4},{8,11},{9,10},{10,... | collective-permute-start | bytes 589832 | tf_op jit(solution)/shard_map/ppermute | solution.py:730
  20.6 15.2 %collective-permute-start.5 = (bf16[384,256]{1,0:T(8,128)(2,1)S(1)}, bf16[384,256]{1,0:T(8,128)(2,1)S(1)}, u32[]{:S(2)}, u32[]{:S(2)}) collective-permute-start(bf16[384,256]{1,0:T(8,128)(2,1)S(1)} %get-tuple-element.116.refs_7_.refs_8_.refs_6_), channel_id=1, source_target_pairs={{0,2},{1,3},{2,0},{3,1},{4,6},{5,7},{6,4},{7,5},{8,10},{9,11},{10,... | collective-permute-start | bytes 589832 | tf_op jit(solution)/shard_map/ppermute | solution.py:730
  20.6 19.6 %collective-permute-start.4 = (bf16[384,256]{1,0:T(8,128)(2,1)S(1)}, bf16[384,256]{1,0:T(8,128)(2,1)S(1)}, u32[]{:S(2)}, u32[]{:S(2)}) collective-permute-start(bf16[384,256]{1,0:T(8,128)(2,1)S(1)} %get-tuple-element.116.refs_7_.refs_8_.refs_6_), channel_id=1, source_target_pairs={{0,1},{1,0},{2,3},{3,2},{4,5},{5,4},{6,7},{7,6},{8,9},{9,8},{10,11... | collective-permute-start | bytes 589832 | tf_op jit(solution)/shard_map/ppermute | solution.py:730
  21.3 19.0 %copy-start = (bf16[1536,768]{1,0:T(8,128)(2,1)S(1)}, bf16[1536,768]{1,0:T(8,128)(2,1)}, u32[]{:S(2)}) copy-start(bf16[1536,768]{1,0:T(8,128)(2,1)} %refs_2_.3) | copy-start | bytes 7077892
  21.3 19.0 %copy-start.3 = (bf16[512,768]{1,0:T(8,128)(2,1)S(1)}, bf16[512,768]{1,0:T(8,128)(2,1)}, u32[]{:S(2)}) copy-start(bf16[512,768]{1,0:T(8,128)(2,1)} %refs_1_.3) | copy-start | bytes 2359300
  35.8 14.8 %collective-permute-start.9 = (bf16[384,256]{1,0:T(8,128)(2,1)S(1)}, bf16[384,256]{1,0:T(8,128)(2,1)S(1)}, u32[]{:S(2)}, u32[]{:S(2)}) collective-permute-start(bf16[384,256]{1,0:T(8,128)(2,1)S(1)} %get-tuple-element.125.refs_7_.refs_9_), channel_id=1, source_target_pairs={{0,3},{1,2},{2,1},{3,0},{4,7},{5,6},{6,5},{7,4},{8,11},{9,10},{10,... | collective-permute-start | bytes 589832 | tf_op jit(solution)/shard_map/ppermute | solution.py:730
  39.0 14.9 %collective-permute-start.8 = (bf16[384,256]{1,0:T(8,128)(2,1)S(1)}, bf16[384,256]{1,0:T(8,128)(2,1)S(1)}, u32[]{:S(2)}, u32[]{:S(2)}) collective-permute-start(bf16[384,256]{1,0:T(8,128)(2,1)S(1)} %get-tuple-element.125.refs_7_.refs_9_), channel_id=1, source_target_pairs={{0,2},{1,3},{2,0},{3,1},{4,6},{5,7},{6,4},{7,5},{8,10},{9,11},{10,... | collective-permute-start | bytes 589832 | tf_op jit(solution)/shard_map/ppermute | solution.py:730
  39.0 14.9 %collective-permute-start.7 = (bf16[384,256]{1,0:T(8,128)(2,1)S(1)}, bf16[384,256]{1,0:T(8,128)(2,1)S(1)}, u32[]{:S(2)}, u32[]{:S(2)}) collective-permute-start(bf16[384,256]{1,0:T(8,128)(2,1)S(1)} %get-tuple-element.125.refs_7_.refs_9_), channel_id=1, source_target_pairs={{0,1},{1,0},{2,3},{3,2},{4,5},{5,4},{6,7},{7,6},{8,9},{9,8},{10,11... | collective-permute-start | bytes 589832 | tf_op jit(solution)/shard_map/ppermute | solution.py:730
  65.3 3.1 %collective-permute-start.10 = (bf16[4,112,768]{2,1,0:T(8,128)(2,1)S(1)}, bf16[4,112,768]{2,1,0:T(8,128)(2,1)S(1)}, u32[]{:S(2)}, u32[]{:S(2)}) collective-permute-start(bf16[4,112,768]{2,1,0:T(8,128)(2,1)S(1)} %get-tuple-element.130), channel_id=1, source_target_pairs={{0,4},{4,0},{8,12},{12,8},{16,20},{20,16},{24,28},{28,24},{1,5},{5... | collective-permute-start | bytes 2064392 | tf_op jit(solution)/shard_map/ppermute | solution.py:730
  68.4 2.5 %collective-permute-start.11 = (bf16[4,144,768]{2,1,0:T(8,128)(2,1)S(1)}, bf16[4,144,768]{2,1,0:T(8,128)(2,1)S(1)}, u32[]{:S(2)}, u32[]{:S(2)}) collective-permute-start(bf16[4,144,768]{2,1,0:T(8,128)(2,1)S(1)} %get-tuple-element.148), channel_id=1, source_target_pairs={{0,4},{4,0},{8,12},{12,8},{16,20},{20,16},{24,28},{28,24},{1,5},{5... | collective-permute-start | bytes 2654216 | tf_op jit(solution)/shard_map/ppermute | solution.py:730
  69.0 15.3 %collective-permute-start.12 = (bf16[2,112,768]{2,1,0:T(8,128)(2,1)S(1)}, bf16[2,112,768]{2,1,0:T(8,128)(2,1)S(1)}, u32[]{:S(2)}, u32[]{:S(2)}) collective-permute-start(bf16[2,112,768]{2,1,0:T(8,128)(2,1)S(1)} %get-tuple-element.164), channel_id=1, source_target_pairs={{0,8},{4,12},{8,0},{12,4},{16,24},{20,28},{24,16},{28,20},{1,9},{5... | collective-permute-start | bytes 1032200 | tf_op jit(solution)/shard_map/ppermute | solution.py:730
  71.1 13.2 %collective-permute-start.13 = (bf16[2,144,768]{2,1,0:T(8,128)(2,1)S(1)}, bf16[2,144,768]{2,1,0:T(8,128)(2,1)S(1)}, u32[]{:S(2)}, u32[]{:S(2)}) collective-permute-start(bf16[2,144,768]{2,1,0:T(8,128)(2,1)S(1)} %get-tuple-element.165), channel_id=1, source_target_pairs={{0,16},{4,20},{8,24},{12,28},{16,0},{20,4},{24,8},{28,12},{1,17},{... | collective-permute-start | bytes 1327112 | tf_op jit(solution)/shard_map/ppermute | solution.py:730
  84.3 7.3 %collective-permute-start.23 = (bf16[4,152,768]{2,1,0:T(8,128)(2,1)S(1)}, bf16[4,152,768]{2,1,0:T(8,128)(2,1)S(1)}, u32[]{:S(2)}, u32[]{:S(2)}) collective-permute-start(bf16[4,152,768]{2,1,0:T(8,128)(2,1)S(1)} %get-tuple-element.182), channel_id=1, source_target_pairs={{0,4},{4,0},{8,12},{12,8},{16,20},{20,16},{24,28},{28,24},{1,5},{5... | collective-permute-start | bytes 2801672 | tf_op jit(solution)/shard_map/ppermute | solution.py:730
  84.4 11.5 %collective-permute-start.14 = (bf16[2,128,768]{2,1,0:T(8,128)(2,1)S(1)}, bf16[2,128,768]{2,1,0:T(8,128)(2,1)S(1)}, u32[]{:S(2)}, u32[]{:S(2)}) collective-permute-start(bf16[2,128,768]{2,1,0:T(8,128)(2,1)S(1)} %get-tuple-element.166), channel_id=1, source_target_pairs={{0,1},{1,0},{2,3},{3,2},{4,5},{5,4},{6,7},{7,6},{8,9},{9,8},{10,11... | collective-permute-start | bytes 1179656 | tf_op jit(solution)/shard_map/ppermute | solution.py:730
  84.5 2.4 %collective-permute-start.16 = (f32[8,768]{1,0:T(8,128)S(1)}, f32[8,768]{1,0:T(8,128)S(1)}, u32[]{:S(2)}, u32[]{:S(2)}) collective-permute-start(f32[8,768]{1,0:T(8,128)S(1)} %get-tuple-element.169), channel_id=1, source_target_pairs={{0,4},{4,0},{8,12},{12,8},{16,20},{20,16},{24,28},{28,24},{1,5},{5... | collective-permute-start | bytes 73736 | tf_op jit(solution)/shard_map/ppermute | solution.py:730
  86.9 3.8 %collective-permute-start.17 = (f32[8,768]{1,0:T(8,128)S(1)}, f32[8,768]{1,0:T(8,128)S(1)}, u32[]{:S(2)}, u32[]{:S(2)}) collective-permute-start(f32[8,768]{1,0:T(8,128)S(1)} %add.12), channel_id=1, source_target_pairs={{0,8},{4,12},{8,0},{12,4},{16,24},{20,28},{24,16},{28,20},{1,9},{5... | collective-permute-start | bytes 73736 | tf_op jit(solution)/shard_map/ppermute | solution.py:730
  90.7 4.3 %collective-permute-start.18 = (f32[8,768]{1,0:T(8,128)S(1)}, f32[8,768]{1,0:T(8,128)S(1)}, u32[]{:S(2)}, u32[]{:S(2)}) collective-permute-start(f32[8,768]{1,0:T(8,128)S(1)} %add.13), channel_id=1, source_target_pairs={{0,16},{4,20},{8,24},{12,28},{16,0},{20,4},{24,8},{28,12},{1,17},{... | collective-permute-start | bytes 73736 | tf_op jit(solution)/shard_map/ppermute | solution.py:730
  91.7 12.1 %collective-permute-start.25 = (bf16[2,80,768]{2,1,0:T(8,128)(2,1)S(1)}, bf16[2,80,768]{2,1,0:T(8,128)(2,1)S(1)}, u32[]{:S(2)}, u32[]{:S(2)}) collective-permute-start(bf16[2,80,768]{2,1,0:T(8,128)(2,1)S(1)} %get-tuple-element.188), channel_id=1, source_target_pairs={{0,16},{4,20},{8,24},{12,28},{16,0},{20,4},{24,8},{28,12},{1,17},{... | collective-permute-start | bytes 737288 | tf_op jit(solution)/shard_map/ppermute | solution.py:730
  93.0 9.6 %collective-permute-start.21 = (bf16[144,768]{1,0:T(8,128)(2,1)S(1)}, bf16[144,768]{1,0:T(8,128)(2,1)S(1)}, u32[]{:S(2)}, u32[]{:S(2)}) collective-permute-start(bf16[144,768]{1,0:T(8,128)(2,1)S(1)} %get-tuple-element.177), channel_id=1, source_target_pairs={{0,8},{4,12},{8,0},{12,4},{16,24},{20,28},{24,16},{28,20},{1,9},{5... | collective-permute-start | bytes 663560 | tf_op jit(solution)/shard_map/ppermute | solution.py:730
  93.7 10.2 %collective-permute-start.24 = (bf16[2,72,768]{2,1,0:T(8,128)(2,1)S(1)}, bf16[2,72,768]{2,1,0:T(8,128)(2,1)S(1)}, u32[]{:S(2)}, u32[]{:S(2)}) collective-permute-start(bf16[2,72,768]{2,1,0:T(8,128)(2,1)S(1)} %get-tuple-element.185), channel_id=1, source_target_pairs={{0,8},{4,12},{8,0},{12,4},{16,24},{20,28},{24,16},{28,20},{1,9},{5... | collective-permute-start | bytes 663560 | tf_op jit(solution)/shard_map/ppermute | solution.py:730
  95.0 7.6 %collective-permute-start.20 = (bf16[112,768]{1,0:T(8,128)(2,1)S(1)}, bf16[112,768]{1,0:T(8,128)(2,1)S(1)}, u32[]{:S(2)}, u32[]{:S(2)}) collective-permute-start(bf16[112,768]{1,0:T(8,128)(2,1)S(1)} %get-tuple-element.175), channel_id=1, source_target_pairs={{0,16},{4,20},{8,24},{12,28},{16,0},{20,4},{24,8},{28,12},{1,17},{... | collective-permute-start | bytes 516104 | tf_op jit(solution)/shard_map/ppermute | solution.py:730
  96.0 3.9 %collective-permute-start.19 = (f32[8,768]{1,0:T(8,128)S(1)}, f32[8,768]{1,0:T(8,128)S(1)}, u32[]{:S(2)}, u32[]{:S(2)}) collective-permute-start(f32[8,768]{1,0:T(8,128)S(1)} %add.14), channel_id=1, source_target_pairs={{0,1},{1,0},{2,3},{3,2},{4,5},{5,4},{6,7},{7,6},{8,9},{9,8},{10,11... | collective-permute-start | bytes 73736 | tf_op jit(solution)/shard_map/ppermute | solution.py:730
  99.9 11.7 %collective-permute-start.15 = (bf16[128,768]{1,0:T(8,128)(2,1)S(1)}, bf16[128,768]{1,0:T(8,128)(2,1)S(1)}, u32[]{:S(2)}, u32[]{:S(2)}) collective-permute-start(bf16[128,768]{1,0:T(8,128)(2,1)S(1)} %get-tuple-element.168), channel_id=1, source_target_pairs={{0,2},{1,3},{2,0},{3,1},{4,6},{5,7},{6,4},{7,5},{8,10},{9,11},{10,... | collective-permute-start | bytes 589832 | tf_op jit(solution)/shard_map/ppermute | solution.py:730
  102.6 8.9 %collective-permute-start.22 = (f32[8,768]{1,0:T(8,128)S(1)}, f32[8,768]{1,0:T(8,128)S(1)}, u32[]{:S(2)}, u32[]{:S(2)}) collective-permute-start(f32[8,768]{1,0:T(8,128)S(1)} %add.15.refs_4_), channel_id=1, source_target_pairs={{0,2},{1,3},{2,0},{3,1},{4,6},{5,7},{6,4},{7,5},{8,10},{9,11},{10,... | collective-permute-start | bytes 73736 | tf_op jit(solution)/shard_map/ppermute | solution.py:730
  103.9 8.7 %collective-permute-start.26 = (bf16[72,768]{1,0:T(8,128)(2,1)S(1)}, bf16[72,768]{1,0:T(8,128)(2,1)S(1)}, u32[]{:S(2)}, u32[]{:S(2)}) collective-permute-start(bf16[72,768]{1,0:T(8,128)(2,1)S(1)} %get-tuple-element.190), channel_id=1, source_target_pairs={{0,16},{4,20},{8,24},{12,28},{16,0},{20,4},{24,8},{28,12},{1,17},{... | collective-permute-start | bytes 331784 | tf_op jit(solution)/shard_map/ppermute | solution.py:730
  104.8 7.9 %collective-permute-start.27 = (bf16[80,768]{1,0:T(8,128)(2,1)S(1)}, bf16[80,768]{1,0:T(8,128)(2,1)S(1)}, u32[]{:S(2)}, u32[]{:S(2)}) collective-permute-start(bf16[80,768]{1,0:T(8,128)(2,1)S(1)} %get-tuple-element.192), channel_id=1, source_target_pairs={{0,8},{4,12},{8,0},{12,4},{16,24},{20,28},{24,16},{28,20},{1,9},{5... | collective-permute-start | bytes 368648 | tf_op jit(solution)/shard_map/ppermute | solution.py:730
  (2 other events, 2.2 us)
